TPU v7x, 256 devices: a whole 4x4x8 slice. The times are simulated.
256 devices in a mesh: server: 32 (over z, x), section: 2 (over core), dp: 4 (over y).
Axes of the slice: x: 4, y: 4, z: 8, core: 2. Of those that a mesh axis runs over, the one named last changes fastest.
Arguments:
- queries: bfloat16 [4, 4096, 2048], P('dp', 'server', 'section'), may hold values from -90 to 90
- key_rows: bfloat16 [4, 4096, 512], P('dp', 'server', 'section'), may hold values from -4 to 4
- saved_value_rows: bfloat16 [4, 4096, 512], P('dp', 'server', 'section'), may hold values from -5 to 5
- out_grad: bfloat16 [4, 4096, 2048], P('dp', 'server', 'section'), may hold values from -5 to 5
- doc_lens: int32 [4, 8], P('dp'), may hold values from 1 to 2048, 4096 in all within a row
- w_query: bfloat16 [4096, 2048], P('dp', 'section'), may hold values from -0.125 to 0.125
- key_weight: bfloat16 [4096, 512], P('dp', 'section'), may hold values from -0.25 to 0.25
- value_weight: bfloat16 [4096, 512], P('dp', 'section'), may hold values from -0.25 to 0.25
Outputs:
- input_grad: bfloat16 [4, 4096, 4096], P('dp', 'server')
Inputs may be any that keep to these rules, and one draw needn't show every extreme that they name: `doc_lens`: each document holds at most 2048 positions.
All inputs are finite; a program needn't handle non-finite values.
Results may differ from a plain program's by a relative error of at most 0.006.
Values may be sent and summed in bfloat16 or wider, within the bound.
No kernel may reach another device: no remote copies, remote signals or barrier semaphores. Data moves between devices by JAX's collectives and lax.ppermute only.
A program may use at most 128 MiB of HBM per device.

v0:
```python
from functools import partial
import math

import jax
import jax.numpy as jnp
from jax import lax
from jax.sharding import PartitionSpec as P

HEAD_SIZE = 128


negative_fill = -1e30


def body(
    queries, key_rows, saved_value_rows, out_grad, doc_lens, w_query, key_weight, value_weight
):
    local_rows = queries.shape[1]
    servers = lax.axis_size("server")
    seq_len = local_rows * servers
    server_index = lax.axis_index("server")
    kv_local = key_rows.shape[2] // HEAD_SIZE
    heads_local = queries.shape[2] // HEAD_SIZE
    group_size = heads_local // kv_local
    stacked_rows = group_size * local_rows
    factor = HEAD_SIZE ** (-0.5)
    doc_ends = jnp.cumsum(doc_lens[0])

    def segment_of(positions):
        return jnp.sum((positions[:, None] >= doc_ends[None, :-1]).astype(jnp.int32), axis=1)

    row_pos = server_index * local_rows + jnp.arange(local_rows, dtype=jnp.int32)
    stacked_pos = jnp.tile(row_pos, group_size)
    stacked_seg = segment_of(stacked_pos)
    query_group = (
        queries[0]
        .reshape(local_rows, kv_local, group_size, HEAD_SIZE)
        .transpose(1, 2, 0, 3)
        .reshape(kv_local, stacked_rows, HEAD_SIZE)
    )
    grad_group = (
        out_grad[0]
        .reshape(local_rows, kv_local, group_size, HEAD_SIZE)
        .transpose(1, 2, 0, 3)
        .reshape(kv_local, stacked_rows, HEAD_SIZE)
    )
    grad_wide = grad_group.astype(jnp.float32)

    def tile_parts(shard_piece, offset):
        key_piece, value_piece = shard_piece
        length = key_piece.shape[1]
        key_block = key_piece[0].reshape(length, kv_local, HEAD_SIZE).transpose(1, 0, 2)
        value_block = value_piece[0].reshape(length, kv_local, HEAD_SIZE).transpose(1, 0, 2)
        key_pos = offset + jnp.arange(length, dtype=jnp.int32)
        visible = (stacked_seg[:, None] == segment_of(key_pos)[None, :]) & (
            key_pos[None, :] <= stacked_pos[:, None]
        )
        return (key_block, value_block, visible)

    def score_of(key_block):
        return (
            jnp.einsum("gqd,gkd->gqk", query_group, key_block, preferred_element_type=jnp.float32)
            * factor
        )

    def stats_step(folded, shard_piece, offset):
        key_block, value_block, visible = tile_parts(shard_piece, offset)
        row_peak, row_total = folded
        scores = score_of(key_block)
        block_peak = jnp.max(jnp.where(visible[None], scores, negative_fill), axis=-1)
        new_peak = jnp.maximum(row_peak, block_peak)
        exp_terms = jnp.where(visible[None], jnp.exp(scores - new_peak[..., None]), 0.0)
        return (new_peak, row_total * jnp.exp(row_peak - new_peak) + jnp.sum(exp_terms, axis=-1))

    def output_step(log_total, folded, shard_piece, offset):
        key_block, value_block, visible = tile_parts(shard_piece, offset)
        weights = jnp.where(
            visible[None], jnp.exp(score_of(key_block) - log_total[..., None]), 0.0
        ).astype(jnp.bfloat16)
        return folded + jnp.einsum(
            "gqk,gkd->gqd", weights, value_block, preferred_element_type=jnp.float32
        )

    def backward_step(log_total, row_delta, folded, shard_piece, offset):
        key_block, value_block, visible = tile_parts(shard_piece, offset)
        length = key_block.shape[1]
        query_acc, key_buffer, value_buffer = folded
        weights = jnp.where(
            visible[None], jnp.exp(score_of(key_block) - log_total[..., None]), 0.0
        ).astype(jnp.bfloat16)
        grad_scores = jnp.einsum(
            "gqd,gkd->gqk", grad_group, value_block, preferred_element_type=jnp.float32
        )
        score_grads = (weights.astype(jnp.float32) * (grad_scores - row_delta[..., None])).astype(
            jnp.bfloat16
        )
        query_acc = query_acc + jnp.einsum(
            "gqk,gkd->gqd", score_grads, key_block, preferred_element_type=jnp.float32
        )
        key_part = jnp.einsum(
            "gqk,gqd->gkd", score_grads, query_group, preferred_element_type=jnp.float32
        )
        value_part = jnp.einsum(
            "gqk,gqd->gkd", weights, grad_group, preferred_element_type=jnp.float32
        )
        key_part = key_part.transpose(1, 0, 2).reshape(length, kv_local * HEAD_SIZE)
        value_part = value_part.transpose(1, 0, 2).reshape(length, kv_local * HEAD_SIZE)
        key_buffer = lax.dynamic_update_slice_in_dim(key_buffer, key_part, offset, 0)
        value_buffer = lax.dynamic_update_slice_in_dim(value_buffer, value_part, offset, 0)
        return (query_acc, key_buffer, value_buffer)

    first_state = (
        jnp.full((kv_local, stacked_rows), negative_fill, jnp.float32),
        jnp.zeros((kv_local, stacked_rows), jnp.float32),
    )
    output_init = jnp.zeros((kv_local, stacked_rows, HEAD_SIZE), jnp.float32)
    backward_init = (
        jnp.zeros((kv_local, stacked_rows, HEAD_SIZE), jnp.float32),
        jnp.zeros((seq_len, kv_local * HEAD_SIZE), jnp.float32),
        jnp.zeros((seq_len, kv_local * HEAD_SIZE), jnp.float32),
    )
    whole_keys, whole_values = (
        lax.all_gather(key_rows, "server", axis=1, tiled=True),
        lax.all_gather(saved_value_rows, "server", axis=1, tiled=True),
    )
    block_width = math.gcd(seq_len, 512)

    def sweep_keys(step_fn, init_state):

        def advance(counter, running):
            offset = counter * block_width
            shard_piece = (
                lax.dynamic_slice_in_dim(whole_keys, offset, block_width, 1),
                lax.dynamic_slice_in_dim(whole_values, offset, block_width, 1),
            )
            return step_fn(running, shard_piece, offset)

        return lax.fori_loop(0, seq_len // block_width, advance, init_state)

    row_peak, row_total = sweep_keys(stats_step, first_state)
    log_total = row_peak + jnp.log(row_total)
    outputs = sweep_keys(partial(output_step, log_total), output_init)
    row_delta = jnp.sum(grad_wide * outputs, axis=-1)
    query_acc, key_buffer, value_buffer = sweep_keys(
        partial(backward_step, log_total, row_delta), backward_init
    )
    key_sum, value_sum = (
        lax.psum_scatter(key_buffer, "server", scatter_dimension=0, tiled=True),
        lax.psum_scatter(value_buffer, "server", scatter_dimension=0, tiled=True),
    )
    key_gradient = (key_sum * factor).astype(jnp.bfloat16)
    value_gradient = value_sum.astype(jnp.bfloat16)
    query_grad = (query_acc * factor).astype(jnp.bfloat16)
    query_grad = (
        query_grad.reshape(kv_local, group_size, local_rows, HEAD_SIZE)
        .transpose(2, 0, 1, 3)
        .reshape(local_rows, heads_local * HEAD_SIZE)
    )

    def contract(left, right):
        return lax.dot_general(
            left, right, (((1,), (1,)), ((), ())), preferred_element_type=jnp.float32
        )

    block = (
        contract(query_grad, lax.all_gather(w_query, "dp", axis=0, tiled=True))
        + contract(key_gradient, lax.all_gather(key_weight, "dp", axis=0, tiled=True))
        + contract(value_gradient, lax.all_gather(value_weight, "dp", axis=0, tiled=True))
    )
    summed = lax.psum(block, "section")
    return summed.astype(jnp.bfloat16)[None]


def solution(mesh):
    return jax.shard_map(
        body,
        mesh=mesh,
        in_specs=(
            P("dp", "server", "section"),
            P("dp", "server", "section"),
            P("dp", "server", "section"),
            P("dp", "server", "section"),
            P("dp", None),
            P("dp", "section"),
            P("dp", "section"),
            P("dp", "section"),
        ),
        out_specs=P("dp", "server", None),
        check_vma=False,
    )
```

profile of v0, /device:TPU:1, one launch (start us, length us, event | category | flops | bytes accessed | tf_op | source)
XLA Modules:
  0.0 795.3 jit_solution(18075537159458093167)
XLA Ops:
  6.5 1.6 copy.85
  8.2 1.6 copy.88
  12.7 1.8 copy.87
  15.2 70.2 %all-gather.6.cloned.1.call-done = bf16[1,4096,256]{1,2,0:T(8,128)(2,1)} async-done(((bf16[1,128,256]{1,2,0:T(8,128)(2,1)}), bf16[1,4096,256]{1,2,0:T(8,128)(2,1)}) %all-gather.6.cloned.1.call-update) | async-done | bytes 2097168 | tf_op jit(solution)/shard_map/all_gather | solution.py:123
  85.4 29.0 %while.48 = (s32[]{:T(128)}, f32[2,512]{1,0:T(2,128)S(1)}, f32[2,512]{1,0:T(2,128)S(1)}, s32[512]{0:T(512)S(1)}, s32[8]{0:T(128)S(1)}, /*index=5*/bf16[1,4096,25...) while((s32[]{:T(128)}, f32[2,512]{1,0:T(2,128)S(1)}, ...), condition=%wide.region_6.7_spmd.clone, body=%wide.region_2.6_spmd.clone.sunk | while | flops 138690048 | bytes 6623962 | solution.py:138
  90.5 1.5 fusion.74
  94.1 1.5 fusion.74
  97.8 1.5 fusion.74
  101.4 1.5 fusion.74
  108.7 1.5 fusion.74
  112.3 1.5 fusion.74
  114.4 47.5 %all-gather.8.cloned.1.call-done = bf16[1,4096,256]{1,2,0:T(8,128)(2,1)} async-done(((bf16[1,128,256]{1,2,0:T(8,128)(2,1)}), bf16[1,4096,256]{1,2,0:T(8,128)(2,1)}) %all-gather.8.cloned.1.call-update) | async-done | bytes 2097168 | tf_op jit(solution)/shard_map/all_gather | solution.py:124
  161.9 30.1 %while.49 = (s32[]{:T(128)}, f32[2,512,128]{2,1,0:T(8,128)}, s32[512]{0:T(512)S(1)}, s32[8]{0:T(128)S(1)}, bf16[1,4096,256]{1,2,0:T(8,128)(2,1)}, /*index=5*/bf1...) while((s32[]{:T(128)}, f32[2,512,128]{2,1,0:T(8,128)}, ...), condition=%wide.region_9.10_spmd.clone, body=%wide.region_7.9_spmd.clone.sunk | while | flops 271591936 | bytes 9720629 | solution.py:138
  193.3 2.5 broadcast.216
  195.8 2.4 broadcast.216.clone
  198.2 67.3 %while.50 = (s32[]{:T(128)}, f32[2,512,128]{2,1,0:T(8,128)S(1)}, f32[4096,256]{0,1:T(8,128)}, f32[4096,256]{0,1:T(8,128)}, s32[512]{0:T(512)S(1)}, /*index=5*/s3...) while((s32[]{:T(128)}, f32[2,512,128]{2,1,0:T(8,128)S(1)}, ...), condition=%wide.region_13.14_spmd.clone, body=%wide.region_11.13_spmd.clone.sunk | while | flops 676342272 | bytes 14967561 | solution.py:138
  199.8 1.6 fusion.92
  208.2 1.7 fusion.92
  216.6 1.6 fusion.92
  225.0 1.6 fusion.92
  233.4 1.6 fusion.92
  241.8 1.6 fusion.92
  250.2 1.6 fusion.92
  258.6 1.6 fusion.92
  267.1 7.8 fusion.36
  274.9 13.0 %all-gather.12.cloned.1.call-done = bf16[4096,256]{1,0:T(8,128)(2,1)} async-done(((bf16[1024,256]{1,0:T(8,128)(2,1)}), bf16[4096,256]{1,0:T(8,128)(2,1)}) %all-gather.12.cloned.1.call-update) | async-done | bytes 2097168 | tf_op jit(solution)/shard_map/all_gather | solution.py:167
  287.9 221.0 %reduce-scatter.3.cloned.1.call-done = f32[128,256]{0,1:T(8,128)} async-done(((f32[4096,256]{0,1:T(8,128)}), f32[128,256]{0,1:T(8,128)}) %reduce-scatter.3.cloned.1.call-update) | async-done | bytes 131088 | tf_op jit(solution)/shard_map/reduce_scatter | solution.py:148
  508.9 3.1 convolution_add_fusion.2
  512.0 35.5 %all-gather.14.cloned.1.call-done = bf16[4096,256]{1,0:T(8,128)(2,1)} async-done(((bf16[1024,256]{1,0:T(8,128)(2,1)}), bf16[4096,256]{1,0:T(8,128)(2,1)}) %all-gather.14.cloned.1.call-update) | async-done | bytes 2097168 | tf_op jit(solution)/shard_map/all_gather | solution.py:168
  547.5 221.8 %reduce-scatter.5.cloned.1.call-done = f32[128,256]{0,1:T(8,128)} async-done(((f32[4096,256]{0,1:T(8,128)}), f32[128,256]{0,1:T(8,128)}) %reduce-scatter.5.cloned.1.call-update) | async-done | bytes 131088 | tf_op jit(solution)/shard_map/reduce_scatter | solution.py:149
  769.4 3.8 convolution_add_fusion.1
  773.2 15.2 %all-reduce.1 = bf16[128,4096]{1,0:T(8,128)(2,1)} all-reduce(f32[128,4096]{1,0:T(8,128)} %convolution_add_fusion.1), channel_id=1, replica_groups=mesh['server'=32,'section'=2,'dp'=4] {'section'}, use_global_device_ids=true, to_apply=%region_16.17 | all-reduce | flops 524288 | bytes 3145728 | tf_op jit(solution)/shard_map/psum | solution.py:170
  (339 shorter events, 108.7 us)
Async XLA Ops:
  6.5 4.7 copy-start.5
  6.5 4.9 copy-start.3
  6.5 78.8 %all-gather.6.cloned.1.call-start = ((), (), s32[]{:S(2)}) async-start(), calls=%async_computation.2 | async-start | bytes 2162688 | tf_op jit(solution)/shard_map/all_gather | solution.py:123
  8.2 153.7 %all-gather.8.cloned.1.call-start = ((), (), s32[]{:S(2)}) async-start(), calls=%async_computation.3 | async-start | bytes 2162688 | tf_op jit(solution)/shard_map/all_gather | solution.py:124
  9.8 4.7 copy-start.4
  9.8 257.3 %all-gather.10.cloned.1.call-start = ((), (), s32[]{:S(2)}) async-start(), calls=%async_computation.4 | async-start | bytes 10485760 | tf_op jit(solution)/shard_map/all_gather | solution.py:166
  10.6 277.3 %all-gather.12.cloned.1.call-start = ((), (), s32[]{:S(2)}) async-start(), calls=%async_computation.6 | async-start | bytes 2621440 | tf_op jit(solution)/shard_map/all_gather | solution.py:167
  11.1 497.8 %reduce-scatter.3.cloned.1.call-start = ((), (), s32[]{:S(2)}) async-start(), calls=%async_computation.5 | async-start | bytes 4325376 | tf_op jit(solution)/shard_map/reduce_scatter | solution.py:148
  161.9 1.8 copy-start
  161.9 1.8 copy-start.1
  165.7 1.8 copy-start
  165.7 1.8 copy-start.1
  168.6 0.8 copy-start.2
  169.4 1.8 copy-start
  169.4 1.8 copy-start.1
  173.1 1.8 copy-start
  173.2 1.8 copy-start.1
  176.1 0.8 copy-start.2
  176.9 1.9 copy-start
  176.9 1.9 copy-start.1
  179.9 0.8 copy-start.2
  180.7 1.9 copy-start
  180.7 1.9 copy-start.1
  183.7 0.8 copy-start.2
  184.5 1.8 copy-start
  184.5 1.8 copy-start.1
  187.5 0.8 copy-start.2
  188.2 1.8 copy-start
  188.2 1.8 copy-start.1
  191.2 0.8 copy-start.2
  265.5 282.0 %all-gather.14.cloned.1.call-start = ((), (), s32[]{:S(2)}) async-start(), calls=%async_computation.8 | async-start | bytes 2621440 | tf_op jit(solution)/shard_map/all_gather | solution.py:168
  266.1 503.3 %reduce-scatter.5.cloned.1.call-start = ((), (), s32[]{:S(2)}) async-start(), calls=%async_computation.7 | async-start | bytes 4325376 | tf_op jit(solution)/shard_map/reduce_scatter | solution.py:149
  (2 other events, 1.6 us)
Sparse Core Ops, SparseCore 0:
  9.8 75.4 all-gather.5
  87.8 74.0 all-gather.7
  163.7 87.9 all-gather.9
  253.4 34.4 all-gather.11
  291.6 217.2 reduce-scatter.2
  510.7 36.7 all-gather.13
  551.9 217.3 reduce-scatter.4
where the time goes:
time: 797 us; the launch traced here: 795 us
  waiting for transfers between devices  611 us (77%)
  matrix products  72.2 us (9%)
  local copies, waits for them, and re-layouts  67.1 us (8%)
  blocking collectives  15.2 us (2%)
  between operations  13.7 us (2%)
  other arithmetic  13.4 us (2%)
    reduce_scatter x1, waiting for transfers between devices, body(): lax.psum_scatter(value_buffer, 'server', scatter_dimension=0, tiled=True)  222 us
    reduce_scatter x1, waiting for transfers between devices, body(): lax.psum_scatter(key_buffer, 'server', scatter_dimension=0, tiled=True)  221 us
    all_gather x1, waiting for transfers between devices, body(): lax.all_gather(key_rows, 'server', axis=1, tiled=True)  70.2 us
    all_gather x1, waiting for transfers between devices, body(): lax.all_gather(saved_value_rows, 'server', axis=1, tiled=True)  47.5 us
    all_gather x1, waiting for transfers between devices, body(): lax.all_gather(value_weight, 'dp', axis=0, tiled=True)  35.5 us
    dot_general x16, matrix products, score_of(): jnp.einsum('gqd,gkd->gqk', query_group, key_block, preferred_element_type...  25.2 us
    dynamic_slice x16, local copies, waits for them, and re-layouts, advance(): lax.dynamic_slice_in_dim(whole_values, offset, block_width, 1)  16.5 us
  transfers between devices with their start and end apart: 7, of which 6 were waited for; matrix products, arithmetic and copies ran while one was open for 18% of the time, Pallas kernels for 0%

commit v1 on v0

v1 whole, which is shorter than its diff:
```python
import functools

import jax
import jax.numpy as jnp
from jax import lax
from jax.experimental import pallas as pl
from jax.experimental.pallas import tpu as pltpu
from jax.sharding import PartitionSpec as P

HEAD = 128
GROUP = 4
ROWS = 128
CHUNK = 2 * ROWS
BACK = 4
CHUNKS = 2 * BACK + 1
FACTOR = HEAD**-0.5
FILL = -1e30
LOG2E = 1.4426950408889634
BF = jnp.bfloat16
F32 = jnp.float32


def nt(a, b):
    return lax.dot_general(a, b, (((1,), (1,)), ((), ())), preferred_element_type=F32)


def nn(a, b):
    return lax.dot_general(a, b, (((1,), (0,)), ((), ())), preferred_element_type=F32)


def tn(a, b):
    return lax.dot_general(a, b, (((0,), (0,)), ((), ())), preferred_element_type=F32)


def attention_kernel(info, qg0, qg1, *refs):
    own_in = refs[: BACK + 1]
    other_in = refs[BACK + 1]
    dq0, dq1, own_out, other_out = refs[BACK + 2 : BACK + 6]
    kv, s_buf, p_buf, part, q_all, g_all = refs[BACK + 6 :]
    block_base, core, odd = info[0], info[1], info[2]
    for n in range(BACK + 1):
        kv[n] = own_in[n][...]
    for n in range(BACK):
        kv[BACK + 1 + n] = other_in[n]
    for h in range(GROUP):
        for slot, ref in enumerate((qg0, qg1)):
            q_all[h, slot * ROWS : (slot + 1) * ROWS, :] = ref[:, h * HEAD : (h + 1) * HEAD]
            g_all[h, slot * ROWS : (slot + 1) * ROWS, :] = ref[
                :, (GROUP + h) * HEAD : (GROUP + h + 1) * HEAD
            ]

    lane = lax.broadcasted_iota(jnp.int32, (1, CHUNK), 1)
    query_pos = block_base + core * CHUNK + jnp.bitwise_xor(lane, odd * ROWS)
    doc_first = jnp.zeros_like(query_pos)
    end = info[8]
    for d in range(7):
        if d:
            end = end + info[8 + d]
        doc_first = jnp.where(query_pos >= end, end, doc_first)
    key_row = jnp.bitwise_xor(
        lax.broadcasted_iota(jnp.int32, (CHUNK, CHUNK), 0), odd * ROWS
    )

    def chunk_base(n):
        own = block_base - n * 2 * CHUNK + core * CHUNK
        i = n - (BACK + 1)
        other = jnp.where(core == 0, block_base - (i + 1) * 2 * CHUNK + CHUNK, block_base - i * 2 * CHUNK)
        return jnp.where(n <= BACK, own, other)

    def score_step(n, peak):
        base = chunk_base(n)
        visible = (key_row >= doc_first - base) & (key_row <= query_pos - base)
        keys = kv[n, :, :HEAD]
        out = []
        for h in range(GROUP):
            s = jnp.where(visible, nt(keys, q_all[h]), FILL)
            s_buf[n, h] = s
            out.append(jnp.maximum(peak[h], jnp.max(s.reshape(CHUNK // 8, 8, CHUNK), axis=0)))
        return tuple(out)

    peak = lax.fori_loop(
        0, CHUNKS, score_step, tuple(jnp.full((8, CHUNK), FILL, F32) for _ in range(GROUP))
    )
    peak = [jnp.max(m, axis=0, keepdims=True) for m in peak]

    def weight_step(n, carry):
        totals, deltas = carry
        values = kv[n, :, HEAD:]
        new_t, new_d = [], []
        for h in range(GROUP):
            e = jnp.exp2((s_buf[n, h] - peak[h]) * (FACTOR * LOG2E))
            dp = nt(values, g_all[h])
            s_buf[n, h] = e
            p_buf[n, h] = dp
            new_t.append(totals[h] + jnp.sum(e.reshape(CHUNK // 8, 8, CHUNK), axis=0))
            new_d.append(deltas[h] + jnp.sum((e * dp).reshape(CHUNK // 8, 8, CHUNK), axis=0))
        return tuple(new_t), tuple(new_d)

    zero = tuple(jnp.zeros((8, CHUNK), F32) for _ in range(GROUP))
    totals, deltas = lax.fori_loop(0, CHUNKS, weight_step, (zero, zero))
    inverse = [1.0 / jnp.sum(t, axis=0, keepdims=True) for t in totals]
    delta = [jnp.sum(d, axis=0, keepdims=True) * inverse[h] for h, d in enumerate(deltas)]

    def grad_step(n, acc):
        keys = kv[n, :, :HEAD]
        dk = jnp.zeros((CHUNK, HEAD), F32)
        dv = jnp.zeros((CHUNK, HEAD), F32)
        out = []
        for h in range(GROUP):
            w = s_buf[n, h] * inverse[h]
            ds = (w * (p_buf[n, h] - delta[h])).astype(BF)
            w = w.astype(BF)
            dv = dv + nn(w, g_all[h])
            dk = dk + nn(ds, q_all[h])
            out.append(acc[h] + tn(keys, ds))
        part[n, :, :HEAD] = dk * FACTOR
        part[n, :, HEAD:] = dv
        return tuple(out)

    acc = lax.fori_loop(
        0, CHUNKS, grad_step, tuple(jnp.zeros((HEAD, CHUNK), F32) for _ in range(GROUP))
    )
    for h in range(GROUP):
        g = (jnp.transpose(acc[h]) * FACTOR).astype(BF)
        dq0[:, h * HEAD : (h + 1) * HEAD] = g[:ROWS]
        dq1[:, h * HEAD : (h + 1) * HEAD] = g[ROWS:]
    for n in range(BACK + 1):
        own_out[n] = part[n]
    for n in range(BACK):
        other_out[n] = part[BACK + 1 + n].astype(BF)


def attention(info, qg0, qg1, own_blocks, other_blocks):
    vmem = pl.BlockSpec(memory_space=pltpu.VMEM)
    return pl.pallas_call(
        attention_kernel,
        out_shape=(
            jax.ShapeDtypeStruct((ROWS, GROUP * HEAD), BF),
            jax.ShapeDtypeStruct((ROWS, GROUP * HEAD), BF),
            jax.ShapeDtypeStruct((BACK + 1, CHUNK, 2 * HEAD), F32),
            jax.ShapeDtypeStruct((BACK, CHUNK, 2 * HEAD), BF),
        ),
        in_specs=[pl.BlockSpec(memory_space=pltpu.SMEM)] + [vmem] * (BACK + 4),
        out_specs=(vmem,) * 4,
        scratch_shapes=[
            pltpu.VMEM((CHUNKS, CHUNK, 2 * HEAD), BF),
            pltpu.VMEM((CHUNKS, GROUP, CHUNK, CHUNK), F32),
            pltpu.VMEM((CHUNKS, GROUP, CHUNK, CHUNK), F32),
            pltpu.VMEM((CHUNKS, CHUNK, 2 * HEAD), F32),
            pltpu.VMEM((GROUP, CHUNK, HEAD), BF),
            pltpu.VMEM((GROUP, CHUNK, HEAD), BF),
        ],
        compiler_params=pltpu.CompilerParams(vmem_limit_bytes=40 * 1024 * 1024),
        cost_estimate=pl.CostEstimate(
            flops=5 * 2 * CHUNKS * GROUP * CHUNK * CHUNK * HEAD,
            bytes_accessed=8 << 20,
            transcendentals=CHUNKS * GROUP * CHUNK * CHUNK,
        ),
        name="attention_grads",
    )(info, qg0, qg1, *own_blocks, other_blocks)


def body(queries, key_rows, saved_value_rows, out_grad, doc_lens, w_query, key_weight, value_weight):
    servers = lax.axis_size("server")
    dps = lax.axis_size("dp")
    server = lax.axis_index("server")
    core = lax.axis_index("section")
    dp = lax.axis_index("dp")
    odd = server % 2
    both = ("server", "section")

    def swap_pairs(j):
        pairs = []
        for s in range(servers):
            z, a, b = s // 4, (s % 4) // 2, s % 2
            for c in range(2):
                target = z * 4 + 2 * c + (b ^ j)
                pairs.append((2 * s + c, 2 * target + a))
        return pairs

    pairs = [swap_pairs(0), swap_pairs(1)]

    def swap(x, j):
        return lax.ppermute(x, both, pairs[j])

    def shift(x, axis, k):
        n = lax.axis_size(axis)
        return lax.ppermute(x, axis, [(i, (i + k) % n) for i in range(n)])

    def flip(x):
        return lax.ppermute(x, "section", [(0, 1), (1, 0)])

    def groups(left, right):
        half = left.shape[-1] // 2
        first = jnp.concatenate([left[:, :half], right[:, :half]], 1)
        second = jnp.concatenate([left[:, half:], right[:, half:]], 1)
        return jnp.where(odd == 0, first, second), jnp.where(odd == 0, second, first)

    kv_first, kv_second = groups(key_rows[0], saved_value_rows[0])
    block = jnp.concatenate([swap(kv_first, 0), swap(kv_second, 1)], 0)
    qg_first, qg_second = groups(queries[0], out_grad[0])
    qg0, qg1 = swap(qg_first, 0), swap(qg_second, 1)

    blocks = [block]
    for _ in range(BACK):
        blocks.append(shift(blocks[-1], "server", 4))
    low = jnp.stack(blocks[:BACK])
    high = jnp.stack(blocks[1:])
    other = flip(jnp.where(core == 0, low, high))

    info = jnp.concatenate(
        [
            jnp.stack([(server // 4) * (4 * ROWS), core, odd]).astype(jnp.int32),
            jnp.zeros((5,), jnp.int32),
            doc_lens[0].astype(jnp.int32),
        ]
    )
    dq0, dq1, own_part, other_part = attention(info, qg0, qg1, blocks, other)

    def my_columns(w):
        half = w.shape[0] // 2
        mine = jnp.where(core == 0, w[:half], w[half:])
        theirs = jnp.where(core == 0, w[half:], w[:half])
        return mine, flip(theirs)

    kw_first, kw_second = groups(key_weight, value_weight)
    kv_weight = jnp.concatenate(my_columns(jnp.concatenate([kw_first, kw_second], 1)), 1)
    kv_weight = lax.all_gather(kv_weight, "dp", axis=0, tiled=True)
    half = w_query.shape[1] // 2
    wq = jnp.where(odd == 0, w_query, jnp.concatenate([w_query[:, half:], w_query[:, :half]], 1))
    wq_mine, wq_theirs = my_columns(wq)

    dq = jnp.concatenate([swap(dq0, 0), swap(dq1, 1)], 1)
    rows = jnp.concatenate([dq] + [shift(dq, "dp", k) for k in range(1, dps)], 0)
    projected = (nt(rows, wq_mine) + nt(flip(rows), wq_theirs)).astype(BF)
    columns = [projected[:ROWS]] + [
        shift(projected[k * ROWS : (k + 1) * ROWS], "dp", -k) for k in range(1, dps)
    ]
    columns = jnp.stack(columns + columns)
    query_term = lax.dynamic_slice_in_dim(columns, (dps - dp) % dps, dps, 0)

    arrived = flip(other_part)
    zero = jnp.zeros_like(arrived[0])
    held = None
    for k in range(BACK, -1, -1):
        total = own_part[k] + jnp.where(
            core == 0, arrived[k] if k < BACK else zero, arrived[k - 1] if k else zero
        ).astype(F32)
        if held is not None:
            total = total + shift(held, "server", -4).astype(F32)
        held = total.astype(BF)
    kv_grad = jnp.concatenate([swap(held[:ROWS], 0), swap(held[ROWS:], 1)], 1)
    kv_grad = jnp.concatenate([kv_grad, flip(kv_grad)], 1)
    kv_term = nt(kv_grad, kv_weight)
    mine = kv_term.reshape(ROWS, dps, -1) + query_term.transpose(1, 0, 2).astype(F32)
    mine = mine.astype(BF)
    theirs = flip(mine)
    out = jnp.stack(
        [jnp.where(core == 0, mine, theirs), jnp.where(core == 0, theirs, mine)], 2
    )
    return out.reshape(1, ROWS, -1)


def solution(mesh):
    return jax.shard_map(
        body,
        mesh=mesh,
        in_specs=(
            P("dp", "server", "section"),
            P("dp", "server", "section"),
            P("dp", "server", "section"),
            P("dp", "server", "section"),
            P("dp", None),
            P("dp", "section"),
            P("dp", "section"),
            P("dp", "section"),
        ),
        out_specs=P("dp", "server", None),
        check_vma=False,
    )
```

time: 797 us -> 151 us (0.19)
  waiting for transfers between devices: 611 us -> 72.3 us
  matrix products: 72.2 us -> 6.56 us
  local copies, waits for them, and re-layouts: 67.1 us -> 4.71 us
  starting transfers between devices: 0.42 us -> 36.9 us
  blocking collectives: 15.2 us -> 0 us
  Pallas kernels: 0 us -> 11.8 us
  other arithmetic: 13.4 us -> 4.3 us
    reduce_scatter x2 -> x0, waiting for transfers between devices: 443 us -> none  [the longest x1 222 us: body(): lax.psum_scatter(value_buffer, 'server', scatter_dimension=0, tiled=True)]
    all_gather x5 -> x1, waiting for transfers between devices: 166 us -> 0.02 us  [body(): kv_weight = lax.all_gather(kv_weight, 'dp', axis=0, tiled=True)]
    ppermute x0 -> x29, waiting for transfers between devices: none -> 72.3 us  [the longest x14 51 us: shift(): return lax.ppermute(x, axis, [(i, (i + k) % n) for i in range(n)])]
    dot_general x59 -> x2, matrix products: 72.2 us -> 3.03 us  [nt(): lax.dot_general(a, b, (((1,), (1,)), ((), ())), preferred_element_type=F32)]
    ppermute x0 -> x29, starting transfers between devices: none -> 36.9 us  [the longest x8 23.6 us: swap(): return lax.ppermute(x, both, pairs[j])]
    dynamic_slice x32 -> x0, local copies, waits for them, and re-layouts: 32.1 us -> none  [the longest x16 16.5 us: advance(): lax.dynamic_slice_in_dim(whole_values, offset, block_width, 1)]
    psum x1 -> x0, blocking collectives: 15.2 us -> none  [body(): summed = lax.psum(block, 'section')]
    pallas_call x0 -> x1, Pallas kernels: none -> 11.8 us  [attention(): pl.pallas_call(attention_kernel, out_shape=(jax.ShapeDtypeStruct((ROWS, G...]
  transfers between devices with their start and end apart: 7 -> 30, of which waited for: 6 -> 20; matrix products, arithmetic and copies ran while one was open for 18% -> 6% of each run, Pallas kernels for 0% -> 8%
where the time goes in v1:
time: 151 us; the launch traced here: 150 us
  waiting for transfers between devices  72.3 us (48%)
  starting transfers between devices  36.9 us (24%)
  between operations  13.9 us (9%)
  Pallas kernels  11.8 us (8%)
  matrix products  6.56 us (4%)
  local copies, waits for them, and re-layouts  4.71 us (3%)
  other arithmetic  4.3 us (3%)
    ppermute x14, waiting for transfers between devices, shift(): return lax.ppermute(x, axis, [(i, (i + k) % n) for i in range(n)])  51 us
    ppermute x8, starting transfers between devices, swap(): return lax.ppermute(x, both, pairs[j])  23.6 us
    ppermute x8, waiting for transfers between devices, swap(): return lax.ppermute(x, both, pairs[j])  19.8 us
    pallas_call x1, Pallas kernels, attention(): pl.pallas_call(attention_kernel, out_shape=(jax.ShapeDtypeStruct((ROWS, G...  11.8 us
    ppermute x14, starting transfers between devices, shift(): return lax.ppermute(x, axis, [(i, (i + k) % n) for i in range(n)])  11.4 us
    reshape x1, matrix products, body(): kv_term.reshape(ROWS, dps, -1) + query_term.transpose(1, 0, 2).astype(F32)  3.53 us
    dot_general x2, matrix products, nt(): lax.dot_general(a, b, (((1,), (1,)), ((), ())), preferred_element_type=F32)  3.03 us
  transfers between devices with their start and end apart: 30, of which 20 were waited for; matrix products, arithmetic and copies ran while one was open for 6% of the time, Pallas kernels for 8%

profile of v1, /device:TPU:1, one launch (start us, length us, event | category | flops | bytes accessed | tf_op | source)
XLA Modules:
  0.0 150.4 jit_solution(8965290080133941367)
XLA Ops:
  7.4 6.0 %collective-permute-start.2 = (bf16[128,256]{1,0:T(8,128)(2,1)S(1)}, bf16[128,256]{1,0:T(8,128)(2,1)S(1)}, u32[]{:S(2)}, u32[]{:S(2)}) collective-permute-start(bf16[128,256]{1,0:T(8,128)(2,1)S(1)} %get-tuple-element.37), channel_id=1, source_target_pairs={{0,0},{4,16},{8,8},{12,24},{16,4},{20,20},{24,12},{28,28},{32,32},... | collective-permute-start | bytes 196616 | tf_op jit(solution)/shard_map/ppermute | solution.py:184
  15.4 3.0 %collective-permute-done.3 = bf16[128,256]{1,0:T(8,128)(2,1)S(1)} collective-permute-done((bf16[128,256]{1,0:T(8,128)(2,1)S(1)}, bf16[128,256]{1,0:T(8,128)(2,1)S(1)}, u32[]{:S(2)}, u32[]{:S(2)}) %collective-permute-start.3) | collective-permute-done | bytes 65568 | tf_op jit(solution)/shard_map/ppermute | solution.py:184
  18.4 1.6 %collective-permute-start.4 = (bf16[256,256]{1,0:T(8,128)(2,1)S(1)}, bf16[256,256]{1,0:T(8,128)(2,1)S(1)}, u32[]{:S(2)}, u32[]{:S(2)}) collective-permute-start(bf16[256,256]{1,0:T(8,128)(2,1)S(1)} %constant_dynamic-update-slice_fusion.refs_0_), channel_id=1, source_target_pairs={{0,32},{8,40},{16,48},{24,56},{32,64},{40,72},{48,80},{56,88},{64,... | collective-permute-start | bytes 393224 | tf_op jit(solution)/shard_map/ppermute | solution.py:188
  20.1 6.3 %collective-permute-done.4.refs_1_ = bf16[256,256]{1,0:T(8,128)(2,1)S(1)} collective-permute-done((bf16[256,256]{1,0:T(8,128)(2,1)S(1)}, bf16[256,256]{1,0:T(8,128)(2,1)S(1)}, u32[]{:S(2)}, u32[]{:S(2)}) %collective-permute-start.4) | collective-permute-done | bytes 131104 | tf_op jit(solution)/shard_map/ppermute | solution.py:188
  27.7 3.7 %collective-permute-done.5.refs_2_ = bf16[256,256]{1,0:T(8,128)(2,1)S(1)} collective-permute-done((bf16[256,256]{1,0:T(8,128)(2,1)S(1)}, bf16[256,256]{1,0:T(8,128)(2,1)S(1)}, u32[]{:S(2)}, u32[]{:S(2)}) %collective-permute-start.5) | collective-permute-done | bytes 131104 | tf_op jit(solution)/shard_map/ppermute | solution.py:188
  31.7 4.8 %collective-permute-done.6.refs_3_ = bf16[256,256]{1,0:T(8,128)(2,1)S(1)} collective-permute-done((bf16[256,256]{1,0:T(8,128)(2,1)S(1)}, bf16[256,256]{1,0:T(8,128)(2,1)S(1)}, u32[]{:S(2)}, u32[]{:S(2)}) %collective-permute-start.6) | collective-permute-done | bytes 131104 | tf_op jit(solution)/shard_map/ppermute | solution.py:188
  36.7 5.2 %collective-permute-done.7.refs_4_ = bf16[256,256]{1,0:T(8,128)(2,1)S(1)} collective-permute-done((bf16[256,256]{1,0:T(8,128)(2,1)S(1)}, bf16[256,256]{1,0:T(8,128)(2,1)S(1)}, u32[]{:S(2)}, u32[]{:S(2)}) %collective-permute-start.7) | collective-permute-done | bytes 131104 | tf_op jit(solution)/shard_map/ppermute | solution.py:188
  42.4 6.2 %collective-permute-start.1 = (bf16[128,1024]{1,0:T(8,128)(2,1)S(1)}, bf16[128,1024]{1,0:T(8,128)(2,1)S(1)}, u32[]{:S(2)}, u32[]{:S(2)}) collective-permute-start(bf16[128,1024]{1,0:T(8,128)(2,1)S(1)} %get-tuple-element.24), channel_id=1, source_target_pairs={{0,8},{4,24},{8,0},{12,16},{16,12},{20,28},{24,4},{28,20},{32,40},... | collective-permute-start | bytes 786440 | tf_op jit(solution)/shard_map/ppermute | solution.py:184
  48.6 1.9 %collective-permute-start = (bf16[128,1024]{1,0:T(8,128)(2,1)S(1)}, bf16[128,1024]{1,0:T(8,128)(2,1)S(1)}, u32[]{:S(2)}, u32[]{:S(2)}) collective-permute-start(bf16[128,1024]{1,0:T(8,128)(2,1)S(1)} %get-tuple-element.25), channel_id=1, source_target_pairs={{0,0},{4,16},{8,8},{12,24},{16,4},{20,20},{24,12},{28,28},{32,32},... | collective-permute-start | bytes 786440 | tf_op jit(solution)/shard_map/ppermute | solution.py:184
  51.7 3.0 %collective-permute-done.1.qg1 = bf16[128,1024]{1,0:T(8,128)(2,1)S(1)} collective-permute-done((bf16[128,1024]{1,0:T(8,128)(2,1)S(1)}, bf16[128,1024]{1,0:T(8,128)(2,1)S(1)}, u32[]{:S(2)}, u32[]{:S(2)}) %collective-permute-start.1) | collective-permute-done | bytes 262176 | tf_op jit(solution)/shard_map/ppermute | solution.py:184
  54.7 3.1 %collective-permute-done.qg0 = bf16[128,1024]{1,0:T(8,128)(2,1)S(1)} collective-permute-done((bf16[128,1024]{1,0:T(8,128)(2,1)S(1)}, bf16[128,1024]{1,0:T(8,128)(2,1)S(1)}, u32[]{:S(2)}, u32[]{:S(2)}) %collective-permute-start) | collective-permute-done | bytes 262176 | tf_op jit(solution)/shard_map/ppermute | solution.py:184
  57.8 11.8 %attention_grads.1 = (bf16[128,512]{1,0:T(8,128)(2,1)S(1)}, bf16[128,512]{1,0:T(8,128)(2,1)S(1)}, f32[5,256,256]{2,1,0:T(8,128)S(1)}, bf16[4,256,256]{2,1,0:T(8,128)(2,1)S(1)}) custom-call(s32[16]{0:T(128)S(1)} %concatenate.46.info, bf16[128,1024]{1,0:T(8,128)(2,1)S(1)} %collective-permute-done.qg0, bf16[128,1024]{1,0:T(8,128)(2,1)S(1)} %collective-permute-done.1.qg1, ...), custom_call_target="tpu_custom_call" | custom-call | flops 3019898880 | bytes 8388608 | tf_op jit(solution)/shard_map/attention_grads/pallas_call | solution.py:135
  70.6 1.9 %collective-permute-start.18 = (bf16[128,512]{1,0:T(8,128)(2,1)S(1)}, bf16[128,512]{1,0:T(8,128)(2,1)S(1)}, u32[]{:S(2)}, u32[]{:S(2)}) collective-permute-start(bf16[128,512]{1,0:T(8,128)(2,1)S(1)} %get-tuple-element.11), channel_id=1, source_target_pairs={{0,0},{4,16},{8,8},{12,24},{16,4},{20,20},{24,12},{28,28},{32,32},... | collective-permute-start | bytes 393224 | tf_op jit(solution)/shard_map/ppermute | solution.py:184
  72.5 2.3 %collective-permute-start.19 = (bf16[128,512]{1,0:T(8,128)(2,1)S(1)}, bf16[128,512]{1,0:T(8,128)(2,1)S(1)}, u32[]{:S(2)}, u32[]{:S(2)}) collective-permute-start(bf16[128,512]{1,0:T(8,128)(2,1)S(1)} %get-tuple-element.12), channel_id=1, source_target_pairs={{0,8},{4,24},{8,0},{12,16},{16,12},{20,28},{24,4},{28,20},{32,40},... | collective-permute-start | bytes 393224 | tf_op jit(solution)/shard_map/ppermute | solution.py:184
  75.0 3.5 %collective-permute-done.18 = bf16[128,512]{1,0:T(8,128)(2,1)S(1)} collective-permute-done((bf16[128,512]{1,0:T(8,128)(2,1)S(1)}, bf16[128,512]{1,0:T(8,128)(2,1)S(1)}, u32[]{:S(2)}, u32[]{:S(2)}) %collective-permute-start.18) | collective-permute-done | bytes 131104 | tf_op jit(solution)/shard_map/ppermute | solution.py:184
  78.5 1.5 %collective-permute-done.19 = bf16[128,512]{1,0:T(8,128)(2,1)S(1)} collective-permute-done((bf16[128,512]{1,0:T(8,128)(2,1)S(1)}, bf16[128,512]{1,0:T(8,128)(2,1)S(1)}, u32[]{:S(2)}, u32[]{:S(2)}) %collective-permute-start.19) | collective-permute-done | bytes 131104 | tf_op jit(solution)/shard_map/ppermute | solution.py:184
  80.0 2.8 %collective-permute-start.22 = (bf16[128,1024]{1,0:T(8,128)(2,1)S(1)}, bf16[128,1024]{1,0:T(8,128)(2,1)S(1)}, u32[]{:S(2)}, u32[]{:S(2)}) collective-permute-start(bf16[128,1024]{1,0:T(8,128)(2,1)S(1)} %constant_dynamic-update-slice_fusion.2), channel_id=1, source_target_pairs={{0,3},{1,0},{2,1},{3,2},{4,7},{5,4},{6,5},{7,6},{8,11},{9,8},{10,9... | collective-permute-start | bytes 786440 | tf_op jit(solution)/shard_map/ppermute | solution.py:188
  84.1 5.0 %collective-permute-done.11 = bf16[256,256]{1,0:T(8,128)(2,1)S(1)} collective-permute-done((bf16[256,256]{1,0:T(8,128)(2,1)S(1)}, bf16[256,256]{1,0:T(8,128)(2,1)S(1)}, u32[]{:S(2)}, u32[]{:S(2)}) %collective-permute-start.11) | collective-permute-done | bytes 131104 | tf_op jit(solution)/shard_map/ppermute | solution.py:188
  90.2 5.2 %collective-permute-done.22 = bf16[128,1024]{1,0:T(8,128)(2,1)S(1)} collective-permute-done((bf16[128,1024]{1,0:T(8,128)(2,1)S(1)}, bf16[128,1024]{1,0:T(8,128)(2,1)S(1)}, u32[]{:S(2)}, u32[]{:S(2)}) %collective-permute-start.22) | collective-permute-done | bytes 262176 | tf_op jit(solution)/shard_map/ppermute | solution.py:188
  95.3 2.7 %collective-permute-done.21 = bf16[128,1024]{1,0:T(8,128)(2,1)S(1)} collective-permute-done((bf16[128,1024]{1,0:T(8,128)(2,1)S(1)}, bf16[128,1024]{1,0:T(8,128)(2,1)S(1)}, u32[]{:S(2)}, u32[]{:S(2)}) %collective-permute-start.21) | collective-permute-done | bytes 262176 | tf_op jit(solution)/shard_map/ppermute | solution.py:188
  98.0 7.6 %collective-permute-done.20 = bf16[128,1024]{1,0:T(8,128)(2,1)S(1)} collective-permute-done((bf16[128,1024]{1,0:T(8,128)(2,1)S(1)}, bf16[128,1024]{1,0:T(8,128)(2,1)S(1)}, u32[]{:S(2)}, u32[]{:S(2)}) %collective-permute-start.20) | collective-permute-done | bytes 262176 | tf_op jit(solution)/shard_map/ppermute | solution.py:188
  106.8 4.6 %collective-permute-done.13 = bf16[256,256]{1,0:T(8,128)(2,1)S(1)} collective-permute-done((bf16[256,256]{1,0:T(8,128)(2,1)S(1)}, bf16[256,256]{1,0:T(8,128)(2,1)S(1)}, u32[]{:S(2)}, u32[]{:S(2)}) %collective-permute-start.13) | collective-permute-done | bytes 131104 | tf_op jit(solution)/shard_map/ppermute | solution.py:188
  112.2 3.7 %collective-permute-start.14 = (bf16[128,256]{1,0:T(8,128)(2,1)}, bf16[128,256]{1,0:T(8,128)(2,1)S(1)}, u32[]{:S(2)}, u32[]{:S(2)}) collective-permute-start(bf16[128,256]{1,0:T(8,128)(2,1)} %get-tuple-element.34), channel_id=1, source_target_pairs={{0,0},{4,16},{8,8},{12,24},{16,4},{20,20},{24,12},{28,28},{32,32},... | collective-permute-start | bytes 196616 | tf_op jit(solution)/shard_map/ppermute | solution.py:184
  116.7 2.7 %collective-permute-done.14 = bf16[128,256]{1,0:T(8,128)(2,1)S(1)} collective-permute-done((bf16[128,256]{1,0:T(8,128)(2,1)}, bf16[128,256]{1,0:T(8,128)(2,1)S(1)}, u32[]{:S(2)}, u32[]{:S(2)}) %collective-permute-start.14) | collective-permute-done | bytes 65568 | tf_op jit(solution)/shard_map/ppermute | solution.py:184
  119.4 1.7 %collective-permute-done.15 = bf16[128,256]{1,0:T(8,128)(2,1)S(1)} collective-permute-done((bf16[128,256]{1,0:T(8,128)(2,1)}, bf16[128,256]{1,0:T(8,128)(2,1)S(1)}, u32[]{:S(2)}, u32[]{:S(2)}) %collective-permute-start.15) | collective-permute-done | bytes 65568 | tf_op jit(solution)/shard_map/ppermute | solution.py:184
  121.2 2.3 %fusion.30 = f32[512,512]{0,1:T(8,128)S(1)} fusion(bf16[512,1024]{1,0:T(8,128)(2,1)} %collective-permute-done.23, bf16[512,1024]{1,0:T(8,128)(2,1)} %collective-permute-done.24), kind=kOutput, calls=%fused_computation.74 | convolution fusion | flops 536870912 | bytes 3145728 | tf_op jit(solution)/shard_map/dot_general | solution.py:24
  124.4 2.3 %collective-permute-start.27 = (bf16[128,512]{0,1:T(8,128)(2,1)S(1)}, bf16[128,512]{0,1:T(8,128)(2,1)S(1)}, u32[]{:S(2)}, u32[]{:S(2)}) collective-permute-start(bf16[128,512]{0,1:T(8,128)(2,1)S(1)} %get-tuple-element.21), channel_id=1, source_target_pairs={{0,1},{1,2},{2,3},{3,0},{4,5},{5,6},{6,7},{7,4},{8,9},{9,10},{10,1... | collective-permute-start | bytes 393224 | tf_op jit(solution)/shard_map/ppermute | solution.py:188
  126.7 2.6 %collective-permute-start.26 = (bf16[128,512]{0,1:T(8,128)(2,1)S(1)}, bf16[128,512]{0,1:T(8,128)(2,1)S(1)}, u32[]{:S(2)}, u32[]{:S(2)}) collective-permute-start(bf16[128,512]{0,1:T(8,128)(2,1)S(1)} %get-tuple-element.22), channel_id=1, source_target_pairs={{0,2},{1,3},{2,0},{3,1},{4,6},{5,7},{6,4},{7,5},{8,10},{9,11},{10,... | collective-permute-start | bytes 393224 | tf_op jit(solution)/shard_map/ppermute | solution.py:188
  129.3 5.5 %collective-permute-done.25 = bf16[128,512]{0,1:T(8,128)(2,1)S(1)} collective-permute-done((bf16[128,512]{0,1:T(8,128)(2,1)S(1)}, bf16[128,512]{0,1:T(8,128)(2,1)S(1)}, u32[]{:S(2)}, u32[]{:S(2)}) %collective-permute-start.25) | collective-permute-done | bytes 131104 | tf_op jit(solution)/shard_map/ppermute | solution.py:188
  135.4 3.5 %fusion.7 = f32[128,2048]{0,1:T(8,128)S(1)} fusion(bf16[2048,1024]{1,0:T(8,128)(2,1)} %all-gather.2.cloned.1.call-done, bf16[128,512]{1,0:T(8,128)(2,1)} %collective-permute-done.16, bf16[128,256]{1,0:T(8,128)(2,1)S(1)} %collective-permute-done.15, bf16[128,256]{1,0:T(8,128)(2,1)S(1)} %collective-permute-done.14), kind=kOutput, calls=%fused_computation.28 | convolution fusion | flops 537657344 | bytes 5505024 | tf_op jit(solution)/shard_map/reshape | solution.py:255
  139.1 1.4 collective-permute-start.28
  140.5 1.5 %collective-permute-done.28 = bf16[128,4,512]{0,2,1:T(8,128)(2,1)S(1)} collective-permute-done((bf16[128,4,512]{0,2,1:T(8,128)(2,1)S(1)}, bf16[128,4,512]{0,2,1:T(8,128)(2,1)S(1)}, u32[]{:S(2)}, u32[]{:S(2)}) %collective-permute-start.28) | collective-permute-done | bytes 524320 | tf_op jit(solution)/shard_map/ppermute | solution.py:191
  (93 shorter events, 15.6 us)
Async XLA Ops:
  6.5 128.8 %all-gather.2.cloned.1.call-start = ((), (), s32[]{:S(2)}) async-start(), calls=%async_computation | async-start | bytes 5242880 | tf_op jit(solution)/shard_map/all_gather | solution.py:228
  7.4 8.0 %collective-permute-start.2 = (bf16[128,256]{1,0:T(8,128)(2,1)S(1)}, bf16[128,256]{1,0:T(8,128)(2,1)S(1)}, u32[]{:S(2)}, u32[]{:S(2)}) collective-permute-start(bf16[128,256]{1,0:T(8,128)(2,1)S(1)} %get-tuple-element.37), channel_id=1, source_target_pairs={{0,0},{4,16},{8,8},{12,24},{16,4},{20,20},{24,12},{28,28},{32,32},... | collective-permute-start | bytes 196616 | tf_op jit(solution)/shard_map/ppermute | solution.py:184
  13.4 5.0 %collective-permute-start.3 = (bf16[128,256]{1,0:T(8,128)(2,1)S(1)}, bf16[128,256]{1,0:T(8,128)(2,1)S(1)}, u32[]{:S(2)}, u32[]{:S(2)}) collective-permute-start(bf16[128,256]{1,0:T(8,128)(2,1)S(1)} %get-tuple-element.36), channel_id=1, source_target_pairs={{0,8},{4,24},{8,0},{12,16},{16,12},{20,28},{24,4},{28,20},{32,40},... | collective-permute-start | bytes 196616 | tf_op jit(solution)/shard_map/ppermute | solution.py:184
  18.4 7.9 %collective-permute-start.4 = (bf16[256,256]{1,0:T(8,128)(2,1)S(1)}, bf16[256,256]{1,0:T(8,128)(2,1)S(1)}, u32[]{:S(2)}, u32[]{:S(2)}) collective-permute-start(bf16[256,256]{1,0:T(8,128)(2,1)S(1)} %constant_dynamic-update-slice_fusion.refs_0_), channel_id=1, source_target_pairs={{0,32},{8,40},{16,48},{24,56},{32,64},{40,72},{48,80},{56,88},{64,... | collective-permute-start | bytes 393224 | tf_op jit(solution)/shard_map/ppermute | solution.py:188
  26.4 5.0 %collective-permute-start.5 = (bf16[256,256]{1,0:T(8,128)(2,1)S(1)}, bf16[256,256]{1,0:T(8,128)(2,1)S(1)}, u32[]{:S(2)}, u32[]{:S(2)}) collective-permute-start(bf16[256,256]{1,0:T(8,128)(2,1)S(1)} %collective-permute-done.4.refs_1_), channel_id=1, source_target_pairs={{0,32},{8,40},{16,48},{24,56},{32,64},{40,72},{48,80},{56,88},{64,... | collective-permute-start | bytes 393224 | tf_op jit(solution)/shard_map/ppermute | solution.py:188
  31.4 5.0 %collective-permute-start.6 = (bf16[256,256]{1,0:T(8,128)(2,1)S(1)}, bf16[256,256]{1,0:T(8,128)(2,1)S(1)}, u32[]{:S(2)}, u32[]{:S(2)}) collective-permute-start(bf16[256,256]{1,0:T(8,128)(2,1)S(1)} %collective-permute-done.5.refs_2_), channel_id=1, source_target_pairs={{0,32},{8,40},{16,48},{24,56},{32,64},{40,72},{48,80},{56,88},{64,... | collective-permute-start | bytes 393224 | tf_op jit(solution)/shard_map/ppermute | solution.py:188
  36.4 5.6 %collective-permute-start.7 = (bf16[256,256]{1,0:T(8,128)(2,1)S(1)}, bf16[256,256]{1,0:T(8,128)(2,1)S(1)}, u32[]{:S(2)}, u32[]{:S(2)}) collective-permute-start(bf16[256,256]{1,0:T(8,128)(2,1)S(1)} %collective-permute-done.6.refs_3_), channel_id=1, source_target_pairs={{0,32},{8,40},{16,48},{24,56},{32,64},{40,72},{48,80},{56,88},{64,... | collective-permute-start | bytes 393224 | tf_op jit(solution)/shard_map/ppermute | solution.py:188
  36.6 13.9 %collective-permute-start.17 = (bf16[512,512]{1,0:T(8,128)(2,1)S(1)}, bf16[512,512]{1,0:T(8,128)(2,1)S(1)}, u32[]{:S(2)}, u32[]{:S(2)}) collective-permute-start(bf16[512,512]{1,0:T(8,128)(2,1)S(1)} %get-tuple-element.18), channel_id=1, source_target_pairs={{0,4},{4,0},{1,5},{5,1},{2,6},{6,2},{3,7},{7,3},{8,12},{12,8},{9,1... | collective-permute-start | bytes 1572872 | tf_op jit(solution)/shard_map/ppermute | solution.py:191
  42.1 15.7 %collective-permute-start.8 = (bf16[4,256,256]{2,1,0:T(8,128)(2,1)S(1)}, bf16[4,256,256]{2,1,0:T(8,128)(2,1)S(1)}, u32[]{:S(2)}, u32[]{:S(2)}) collective-permute-start(bf16[4,256,256]{2,1,0:T(8,128)(2,1)S(1)} %maximum_select_fusion.1), channel_id=1, source_target_pairs={{0,4},{4,0},{1,5},{5,1},{2,6},{6,2},{3,7},{7,3},{8,12},{12,8},{9,1... | collective-permute-start | bytes 1572872 | tf_op jit(solution)/shard_map/ppermute | solution.py:191
  42.4 12.3 %collective-permute-start.1 = (bf16[128,1024]{1,0:T(8,128)(2,1)S(1)}, bf16[128,1024]{1,0:T(8,128)(2,1)S(1)}, u32[]{:S(2)}, u32[]{:S(2)}) collective-permute-start(bf16[128,1024]{1,0:T(8,128)(2,1)S(1)} %get-tuple-element.24), channel_id=1, source_target_pairs={{0,8},{4,24},{8,0},{12,16},{16,12},{20,28},{24,4},{28,20},{32,40},... | collective-permute-start | bytes 786440 | tf_op jit(solution)/shard_map/ppermute | solution.py:184
  48.6 9.2 %collective-permute-start = (bf16[128,1024]{1,0:T(8,128)(2,1)S(1)}, bf16[128,1024]{1,0:T(8,128)(2,1)S(1)}, u32[]{:S(2)}, u32[]{:S(2)}) collective-permute-start(bf16[128,1024]{1,0:T(8,128)(2,1)S(1)} %get-tuple-element.25), channel_id=1, source_target_pairs={{0,0},{4,16},{8,8},{12,24},{16,4},{20,20},{24,12},{28,28},{32,32},... | collective-permute-start | bytes 786440 | tf_op jit(solution)/shard_map/ppermute | solution.py:184
  51.7 17.9 %copy-start = (bf16[1024,1024]{1,0:T(8,128)(2,1)S(1)}, bf16[1024,1024]{1,0:T(8,128)(2,1)}, u32[]{:S(2)}) copy-start(bf16[1024,1024]{1,0:T(8,128)(2,1)} %param.13) | copy-start | bytes 6291460
  69.5 5.3 %collective-permute-start.9 = (bf16[4,256,256]{2,1,0:T(8,128)(2,1)S(1)}, bf16[4,256,256]{2,1,0:T(8,128)(2,1)S(1)}, u32[]{:S(2)}, u32[]{:S(2)}) collective-permute-start(bf16[4,256,256]{2,1,0:T(8,128)(2,1)S(1)} %get-tuple-element.10), channel_id=1, source_target_pairs={{0,4},{4,0},{1,5},{5,1},{2,6},{6,2},{3,7},{7,3},{8,12},{12,8},{9,1... | collective-permute-start | bytes 1572872 | tf_op jit(solution)/shard_map/ppermute | solution.py:191
  70.6 7.9 %collective-permute-start.18 = (bf16[128,512]{1,0:T(8,128)(2,1)S(1)}, bf16[128,512]{1,0:T(8,128)(2,1)S(1)}, u32[]{:S(2)}, u32[]{:S(2)}) collective-permute-start(bf16[128,512]{1,0:T(8,128)(2,1)S(1)} %get-tuple-element.11), channel_id=1, source_target_pairs={{0,0},{4,16},{8,8},{12,24},{16,4},{20,20},{24,12},{28,28},{32,32},... | collective-permute-start | bytes 393224 | tf_op jit(solution)/shard_map/ppermute | solution.py:184
  72.5 7.5 %collective-permute-start.19 = (bf16[128,512]{1,0:T(8,128)(2,1)S(1)}, bf16[128,512]{1,0:T(8,128)(2,1)S(1)}, u32[]{:S(2)}, u32[]{:S(2)}) collective-permute-start(bf16[128,512]{1,0:T(8,128)(2,1)S(1)} %get-tuple-element.12), channel_id=1, source_target_pairs={{0,8},{4,24},{8,0},{12,16},{16,12},{20,28},{24,4},{28,20},{32,40},... | collective-permute-start | bytes 393224 | tf_op jit(solution)/shard_map/ppermute | solution.py:184
  74.9 8.8 %collective-permute-start.10 = (bf16[256,256]{1,0:T(8,128)(2,1)S(1)}, bf16[256,256]{1,0:T(8,128)(2,1)S(1)}, u32[]{:S(2)}, u32[]{:S(2)}) collective-permute-start(bf16[256,256]{1,0:T(8,128)(2,1)S(1)} %fusion.17), channel_id=1, source_target_pairs={{0,224},{8,232},{16,240},{24,248},{32,0},{40,8},{48,16},{56,24},{6... | collective-permute-start | bytes 393224 | tf_op jit(solution)/shard_map/ppermute | solution.py:188
  80.0 15.3 %collective-permute-start.22 = (bf16[128,1024]{1,0:T(8,128)(2,1)S(1)}, bf16[128,1024]{1,0:T(8,128)(2,1)S(1)}, u32[]{:S(2)}, u32[]{:S(2)}) collective-permute-start(bf16[128,1024]{1,0:T(8,128)(2,1)S(1)} %constant_dynamic-update-slice_fusion.2), channel_id=1, source_target_pairs={{0,3},{1,0},{2,1},{3,2},{4,7},{5,4},{6,5},{7,6},{8,11},{9,8},{10,9... | collective-permute-start | bytes 786440 | tf_op jit(solution)/shard_map/ppermute | solution.py:188
  82.8 15.2 %collective-permute-start.21 = (bf16[128,1024]{1,0:T(8,128)(2,1)S(1)}, bf16[128,1024]{1,0:T(8,128)(2,1)S(1)}, u32[]{:S(2)}, u32[]{:S(2)}) collective-permute-start(bf16[128,1024]{1,0:T(8,128)(2,1)S(1)} %constant_dynamic-update-slice_fusion.2), channel_id=1, source_target_pairs={{0,2},{1,3},{2,0},{3,1},{4,6},{5,7},{6,4},{7,5},{8,10},{9,11},{10,... | collective-permute-start | bytes 786440 | tf_op jit(solution)/shard_map/ppermute | solution.py:188
  82.9 22.7 %collective-permute-start.20 = (bf16[128,1024]{1,0:T(8,128)(2,1)S(1)}, bf16[128,1024]{1,0:T(8,128)(2,1)S(1)}, u32[]{:S(2)}, u32[]{:S(2)}) collective-permute-start(bf16[128,1024]{1,0:T(8,128)(2,1)S(1)} %constant_dynamic-update-slice_fusion.2), channel_id=1, source_target_pairs={{0,1},{1,2},{2,3},{3,0},{4,5},{5,6},{6,7},{7,4},{8,9},{9,10},{10,1... | collective-permute-start | bytes 786440 | tf_op jit(solution)/shard_map/ppermute | solution.py:188
  83.8 5.3 %collective-permute-start.11 = (bf16[256,256]{1,0:T(8,128)(2,1)S(1)}, bf16[256,256]{1,0:T(8,128)(2,1)S(1)}, u32[]{:S(2)}, u32[]{:S(2)}) collective-permute-start(bf16[256,256]{1,0:T(8,128)(2,1)S(1)} %fusion.13), channel_id=1, source_target_pairs={{0,224},{8,232},{16,240},{24,248},{32,0},{40,8},{48,16},{56,24},{6... | collective-permute-start | bytes 393224 | tf_op jit(solution)/shard_map/ppermute | solution.py:188
  84.0 37.2 %collective-permute-start.24 = (bf16[512,1024]{1,0:T(8,128)(2,1)S(1)}, bf16[512,1024]{1,0:T(8,128)(2,1)}, u32[]{:S(2)}, u32[]{:S(2)}) collective-permute-start(bf16[512,1024]{1,0:T(8,128)(2,1)S(1)} %broadcast_select_fusion), channel_id=1, source_target_pairs={{0,4},{4,0},{1,5},{5,1},{2,6},{6,2},{3,7},{7,3},{8,12},{12,8},{9,1... | collective-permute-start | bytes 3145736 | tf_op jit(solution)/shard_map/ppermute | solution.py:191
  89.2 17.5 %collective-permute-start.12 = (bf16[256,256]{1,0:T(8,128)(2,1)S(1)}, bf16[256,256]{1,0:T(8,128)(2,1)S(1)}, u32[]{:S(2)}, u32[]{:S(2)}) collective-permute-start(bf16[256,256]{1,0:T(8,128)(2,1)S(1)} %fusion.14), channel_id=1, source_target_pairs={{0,224},{8,232},{16,240},{24,248},{32,0},{40,8},{48,16},{56,24},{6... | collective-permute-start | bytes 393224 | tf_op jit(solution)/shard_map/ppermute | solution.py:188
  98.0 17.9 %copy-start.5 = (bf16[128,1024]{1,0:T(8,128)(2,1)}, bf16[128,1024]{1,0:T(8,128)(2,1)S(1)}, u32[]{:S(2)}) copy-start(bf16[128,1024]{1,0:T(8,128)(2,1)S(1)} %collective-permute-done.21) | copy-start | bytes 786436
  106.6 14.6 %collective-permute-start.23 = (bf16[512,1024]{1,0:T(8,128)(2,1)}, bf16[512,1024]{1,0:T(8,128)(2,1)}, u32[]{:S(2)}, u32[]{:S(2)}) collective-permute-start(bf16[512,1024]{1,0:T(8,128)(2,1)} %pad_maximum_fusion.1), channel_id=1, source_target_pairs={{0,4},{4,0},{1,5},{5,1},{2,6},{6,2},{3,7},{7,3},{8,12},{12,8},{9,1... | collective-permute-start | bytes 3145736 | tf_op jit(solution)/shard_map/ppermute | solution.py:191
  106.7 4.7 %collective-permute-start.13 = (bf16[256,256]{1,0:T(8,128)(2,1)S(1)}, bf16[256,256]{1,0:T(8,128)(2,1)S(1)}, u32[]{:S(2)}, u32[]{:S(2)}) collective-permute-start(bf16[256,256]{1,0:T(8,128)(2,1)S(1)} %fusion.15), channel_id=1, source_target_pairs={{0,224},{8,232},{16,240},{24,248},{32,0},{40,8},{48,16},{56,24},{6... | collective-permute-start | bytes 393224 | tf_op jit(solution)/shard_map/ppermute | solution.py:188
  112.2 7.3 %collective-permute-start.14 = (bf16[128,256]{1,0:T(8,128)(2,1)}, bf16[128,256]{1,0:T(8,128)(2,1)S(1)}, u32[]{:S(2)}, u32[]{:S(2)}) collective-permute-start(bf16[128,256]{1,0:T(8,128)(2,1)} %get-tuple-element.34), channel_id=1, source_target_pairs={{0,0},{4,16},{8,8},{12,24},{16,4},{20,20},{24,12},{28,28},{32,32},... | collective-permute-start | bytes 196616 | tf_op jit(solution)/shard_map/ppermute | solution.py:184
  115.9 5.2 %collective-permute-start.15 = (bf16[128,256]{1,0:T(8,128)(2,1)}, bf16[128,256]{1,0:T(8,128)(2,1)S(1)}, u32[]{:S(2)}, u32[]{:S(2)}) collective-permute-start(bf16[128,256]{1,0:T(8,128)(2,1)} %get-tuple-element.35), channel_id=1, source_target_pairs={{0,8},{4,24},{8,0},{12,16},{16,12},{20,28},{24,4},{28,20},{32,40},... | collective-permute-start | bytes 196616 | tf_op jit(solution)/shard_map/ppermute | solution.py:184
  121.1 14.2 %collective-permute-start.16 = (bf16[128,512]{1,0:T(8,128)(2,1)S(1)}, bf16[128,512]{1,0:T(8,128)(2,1)}, u32[]{:S(2)}, u32[]{:S(2)}) collective-permute-start(bf16[128,512]{1,0:T(8,128)(2,1)S(1)} %pad_maximum_fusion.8), channel_id=1, source_target_pairs={{0,4},{4,0},{1,5},{5,1},{2,6},{6,2},{3,7},{7,3},{8,12},{12,8},{9,1... | collective-permute-start | bytes 393224 | tf_op jit(solution)/shard_map/ppermute | solution.py:191
  124.4 10.8 %collective-permute-start.27 = (bf16[128,512]{0,1:T(8,128)(2,1)S(1)}, bf16[128,512]{0,1:T(8,128)(2,1)S(1)}, u32[]{:S(2)}, u32[]{:S(2)}) collective-permute-start(bf16[128,512]{0,1:T(8,128)(2,1)S(1)} %get-tuple-element.21), channel_id=1, source_target_pairs={{0,1},{1,2},{2,3},{3,0},{4,5},{5,6},{6,7},{7,4},{8,9},{9,10},{10,1... | collective-permute-start | bytes 393224 | tf_op jit(solution)/shard_map/ppermute | solution.py:188
  126.7 8.5 %collective-permute-start.26 = (bf16[128,512]{0,1:T(8,128)(2,1)S(1)}, bf16[128,512]{0,1:T(8,128)(2,1)S(1)}, u32[]{:S(2)}, u32[]{:S(2)}) collective-permute-start(bf16[128,512]{0,1:T(8,128)(2,1)S(1)} %get-tuple-element.22), channel_id=1, source_target_pairs={{0,2},{1,3},{2,0},{3,1},{4,6},{5,7},{6,4},{7,5},{8,10},{9,11},{10,... | collective-permute-start | bytes 393224 | tf_op jit(solution)/shard_map/ppermute | solution.py:188
  129.2 5.5 %collective-permute-start.25 = (bf16[128,512]{0,1:T(8,128)(2,1)S(1)}, bf16[128,512]{0,1:T(8,128)(2,1)S(1)}, u32[]{:S(2)}, u32[]{:S(2)}) collective-permute-start(bf16[128,512]{0,1:T(8,128)(2,1)S(1)} %get-tuple-element.23), channel_id=1, source_target_pairs={{0,3},{1,0},{2,1},{3,2},{4,7},{5,4},{6,5},{7,6},{8,11},{9,8},{10,9... | collective-permute-start | bytes 393224 | tf_op jit(solution)/shard_map/ppermute | solution.py:188
  139.1 3.0 %collective-permute-start.28 = (bf16[128,4,512]{0,2,1:T(8,128)(2,1)S(1)}, bf16[128,4,512]{0,2,1:T(8,128)(2,1)S(1)}, u32[]{:S(2)}, u32[]{:S(2)}) collective-permute-start(bf16[128,4,512]{0,2,1:T(8,128)(2,1)S(1)} %fusion.1), channel_id=1, source_target_pairs={{0,4},{4,0},{1,5},{5,1},{2,6},{6,2},{3,7},{7,3},{8,12},{12,8},{9,1... | collective-permute-start | bytes 1572872 | tf_op jit(solution)/shard_map/ppermute | solution.py:191
  (8 other events, 72.7 us)
Sparse Core Ops, SparseCore 0:
  51.8 62.5 all-gather.1

commit v2 on v1

--- a/solution.py
+++ b/solution.py
@@ -35,8 +35,7 @@
 def attention_kernel(info, qg0, qg1, *refs):
     own_in = refs[: BACK + 1]
     other_in = refs[BACK + 1]
-    dq0, dq1, own_out, other_out = refs[BACK + 2 : BACK + 6]
-    kv, s_buf, p_buf, part, q_all, g_all = refs[BACK + 6 :]
+    dq, own_out, other_out, kv, s_buf, p_buf, part, q_all, g_all = refs[-9:]
     block_base, core, odd = info[0], info[1], info[2]
     for n in range(BACK + 1):
         kv[n] = own_in[n][...]
@@ -121,27 +120,26 @@
         0, CHUNKS, grad_step, tuple(jnp.zeros((HEAD, CHUNK), F32) for _ in range(GROUP))
     )
     for h in range(GROUP):
-        g = (jnp.transpose(acc[h]) * FACTOR).astype(BF)
-        dq0[:, h * HEAD : (h + 1) * HEAD] = g[:ROWS]
-        dq1[:, h * HEAD : (h + 1) * HEAD] = g[ROWS:]
+        dq[:, h * HEAD : (h + 1) * HEAD] = (jnp.transpose(acc[h]) * FACTOR).astype(BF)
     for n in range(BACK + 1):
         own_out[n] = part[n]
     for n in range(BACK):
         other_out[n] = part[BACK + 1 + n].astype(BF)
 
 
-def attention(info, qg0, qg1, own_blocks, other_blocks):
+def attention(info, qg0, qg1, own_blocks, other_blocks, after):
     vmem = pl.BlockSpec(memory_space=pltpu.VMEM)
     return pl.pallas_call(
         attention_kernel,
         out_shape=(
-            jax.ShapeDtypeStruct((ROWS, GROUP * HEAD), BF),
-            jax.ShapeDtypeStruct((ROWS, GROUP * HEAD), BF),
+            jax.ShapeDtypeStruct((CHUNK, GROUP * HEAD), BF),
             jax.ShapeDtypeStruct((BACK + 1, CHUNK, 2 * HEAD), F32),
             jax.ShapeDtypeStruct((BACK, CHUNK, 2 * HEAD), BF),
         ),
-        in_specs=[pl.BlockSpec(memory_space=pltpu.SMEM)] + [vmem] * (BACK + 4),
-        out_specs=(vmem,) * 4,
+        in_specs=[pl.BlockSpec(memory_space=pltpu.SMEM)]
+        + [vmem] * (BACK + 4)
+        + [pl.BlockSpec(memory_space=pl.ANY)] * len(after),
+        out_specs=(vmem,) * 3,
         scratch_shapes=[
             pltpu.VMEM((CHUNKS, CHUNK, 2 * HEAD), BF),
             pltpu.VMEM((CHUNKS, GROUP, CHUNK, CHUNK), F32),
@@ -150,14 +148,100 @@
             pltpu.VMEM((GROUP, CHUNK, HEAD), BF),
             pltpu.VMEM((GROUP, CHUNK, HEAD), BF),
         ],
-        compiler_params=pltpu.CompilerParams(vmem_limit_bytes=40 * 1024 * 1024),
+        compiler_params=pltpu.CompilerParams(vmem_limit_bytes=30 * 1024 * 1024),
         cost_estimate=pl.CostEstimate(
             flops=5 * 2 * CHUNKS * GROUP * CHUNK * CHUNK * HEAD,
             bytes_accessed=8 << 20,
             transcendentals=CHUNKS * GROUP * CHUNK * CHUNK,
         ),
         name="attention_grads",
-    )(info, qg0, qg1, *own_blocks, other_blocks)
+    )(info, qg0, qg1, *own_blocks, other_blocks, *after)
+
+
+def project_query_kernel(info, dq, other, *refs):
+    n = (len(refs) - 1) // 2
+    weights, outs, rows = refs[:n], refs[n : 2 * n], refs[2 * n]
+    core, odd, chip = info[1], info[2], info[3]
+    for source, c in ((dq, core), (other, 1 - core)):
+        for slot in range(2):
+            owner = 2 * c + jnp.bitwise_xor(odd, slot)
+            at = pl.multiple_of(lax.rem(owner - chip + 4, 4) * ROWS, ROWS)
+            rows[pl.ds(at, ROWS), :] = source[slot * ROWS : (slot + 1) * ROWS, :]
+    for k in range(n):
+        width = weights[k].shape[0]
+        product = nt(rows[...], weights[k][...]).astype(BF)
+        for i in range(4):
+            outs[i][:, k * width : (k + 1) * width] = product[i * ROWS : (i + 1) * ROWS]
+
+
+def project_query(info, dq, other, weights):
+    vmem = pl.BlockSpec(memory_space=pltpu.VMEM)
+    n, width, dims = len(weights), weights[0].shape[0], dq.shape[1]
+    return pl.pallas_call(
+        project_query_kernel,
+        grid=(1,),
+        out_shape=(jax.ShapeDtypeStruct((ROWS, n * width), BF),) * 4,
+        in_specs=[pl.BlockSpec(memory_space=pltpu.SMEM), vmem, vmem]
+        + [pl.BlockSpec((width, dims), lambda i, at=w.shape[1] // dims - 1: (0, at)) for w in weights],
+        out_specs=(vmem,) * 4,
+        scratch_shapes=[pltpu.VMEM((4 * ROWS, dims), BF)],
+        compiler_params=pltpu.CompilerParams(vmem_limit_bytes=24 * 1024 * 1024),
+        cost_estimate=pl.CostEstimate(
+            flops=8 * ROWS * n * width * dims, bytes_accessed=4 << 20, transcendentals=0
+        ),
+        name="project_query",
+    )(info, dq, other, *weights)
+
+
+def project_kernel(grad, *refs):
+    n = len(refs) - 5
+    out = refs[-1]
+    for k in range(n):
+        width = refs[k].shape[0]
+        total = nt(grad[...], refs[k][...])
+        for term in refs[n : n + 4]:
+            total = total + term[:, k * width : (k + 1) * width].astype(F32)
+        out[k] = total.astype(BF)
+
+
+def project(grad, weights, terms):
+    vmem = pl.BlockSpec(memory_space=pltpu.VMEM)
+    n, width, dims = len(weights), weights[0].shape[0], grad.shape[1]
+    return pl.pallas_call(
+        project_kernel,
+        grid=(1,),
+        out_shape=jax.ShapeDtypeStruct((n, ROWS, width), BF),
+        in_specs=[vmem] + [pl.BlockSpec((width, dims), lambda i: (0, 0))] * n + [vmem] * 4,
+        out_specs=vmem,
+        compiler_params=pltpu.CompilerParams(vmem_limit_bytes=24 * 1024 * 1024),
+        cost_estimate=pl.CostEstimate(
+            flops=2 * n * ROWS * width * dims, bytes_accessed=8 << 20, transcendentals=0
+        ),
+        name="project_kv",
+    )(grad, *weights, *terms)
+
+
+def assemble_kernel(where, mine, theirs, out):
+    n, _, width = mine.shape
+    for k in range(n):
+        piece = lax.rem(where[0] - k + n, n) * 2
+        near = pl.multiple_of((piece + where[1]) * width, width)
+        far = pl.multiple_of((piece + 1 - where[1]) * width, width)
+        out[:, pl.ds(near, width)] = mine[k]
+        out[:, pl.ds(far, width)] = theirs[k]
+
+
+def assemble(where, mine, theirs):
+    vmem = pl.BlockSpec(memory_space=pltpu.VMEM)
+    n, rows, width = mine.shape
+    return pl.pallas_call(
+        assemble_kernel,
+        out_shape=jax.ShapeDtypeStruct((rows, 2 * n * width), BF),
+        in_specs=[pl.BlockSpec(memory_space=pltpu.SMEM), vmem, vmem],
+        out_specs=vmem,
+        compiler_params=pltpu.CompilerParams(vmem_limit_bytes=16 * 1024 * 1024),
+        name="assemble",
+    )(where, mine, theirs)
 
 
 def body(queries, key_rows, saved_value_rows, out_grad, doc_lens, w_query, key_weight, value_weight):
@@ -198,67 +282,78 @@
 
     kv_first, kv_second = groups(key_rows[0], saved_value_rows[0])
     block = jnp.concatenate([swap(kv_first, 0), swap(kv_second, 1)], 0)
-    qg_first, qg_second = groups(queries[0], out_grad[0])
-    qg0, qg1 = swap(qg_first, 0), swap(qg_second, 1)
-
     blocks = [block]
     for _ in range(BACK):
         blocks.append(shift(blocks[-1], "server", 4))
+
+    queries, out_grad, _ = lax.optimization_barrier((queries, out_grad, block))
+    qg_first, qg_second = groups(queries[0], out_grad[0])
+    qg0, qg1 = swap(qg_first, 0), swap(qg_second, 1)
+
+    kw_first, kw_second = groups(key_weight, value_weight)
+    half = w_query.shape[1] // 2
+    weight = jnp.concatenate(
+        [kw_first, kw_second, jnp.where(odd == 0, w_query[:, :half], w_query[:, half:])], 1
+    )
+    half = weight.shape[0] // 2
+    mine = jnp.where(core == 0, weight[:half], weight[half:])
+    theirs = flip(jnp.where(core == 0, weight[half:], weight[:half]))
+    half = 2 * kw_first.shape[1]
+    wide = jnp.concatenate(
+        [
+            mine[:, :half],
+            theirs[:, :half],
+            jnp.where(core == (server % 4) // 2, mine[:, half:], theirs[:, half:]),
+        ],
+        1,
+    )
+    early = {k: shift(wide if k != 2 else wide[:, 2 * half :], "dp", k) for k in range(1, dps)}
+
     low = jnp.stack(blocks[:BACK])
     high = jnp.stack(blocks[1:])
     other = flip(jnp.where(core == 0, low, high))
 
     info = jnp.concatenate(
         [
-            jnp.stack([(server // 4) * (4 * ROWS), core, odd]).astype(jnp.int32),
-            jnp.zeros((5,), jnp.int32),
+            jnp.stack([(server // 4) * (4 * ROWS), core, odd, server % 4]).astype(jnp.int32),
+            jnp.zeros((4,), jnp.int32),
             doc_lens[0].astype(jnp.int32),
         ]
     )
-    dq0, dq1, own_part, other_part = attention(info, qg0, qg1, blocks, other)
-
-    def my_columns(w):
-        half = w.shape[0] // 2
-        mine = jnp.where(core == 0, w[:half], w[half:])
-        theirs = jnp.where(core == 0, w[half:], w[:half])
-        return mine, flip(theirs)
-
-    kw_first, kw_second = groups(key_weight, value_weight)
-    kv_weight = jnp.concatenate(my_columns(jnp.concatenate([kw_first, kw_second], 1)), 1)
-    kv_weight = lax.all_gather(kv_weight, "dp", axis=0, tiled=True)
-    half = w_query.shape[1] // 2
-    wq = jnp.where(odd == 0, w_query, jnp.concatenate([w_query[:, half:], w_query[:, :half]], 1))
-    wq_mine, wq_theirs = my_columns(wq)
-
-    dq = jnp.concatenate([swap(dq0, 0), swap(dq1, 1)], 1)
-    rows = jnp.concatenate([dq] + [shift(dq, "dp", k) for k in range(1, dps)], 0)
-    projected = (nt(rows, wq_mine) + nt(flip(rows), wq_theirs)).astype(BF)
-    columns = [projected[:ROWS]] + [
-        shift(projected[k * ROWS : (k + 1) * ROWS], "dp", -k) for k in range(1, dps)
-    ]
-    columns = jnp.stack(columns + columns)
-    query_term = lax.dynamic_slice_in_dim(columns, (dps - dp) % dps, dps, 0)
+    dq, own_part, other_part = attention(
+        info, qg0, qg1, blocks, other, [early[k] for k in early if k != 2]
+    )
 
     arrived = flip(other_part)
-    zero = jnp.zeros_like(arrived[0])
-    held = None
-    for k in range(BACK, -1, -1):
-        total = own_part[k] + jnp.where(
-            core == 0, arrived[k] if k < BACK else zero, arrived[k - 1] if k else zero
-        ).astype(F32)
-        if held is not None:
-            total = total + shift(held, "server", -4).astype(F32)
-        held = total.astype(BF)
+    zero = jnp.zeros_like(arrived[:1])
+    arrived = jnp.where(
+        core == 0,
+        jnp.concatenate([arrived, zero], 0),
+        jnp.concatenate([zero, arrived], 0),
+    )
+    totals = own_part + arrived.astype(F32)
+    held = totals[BACK].astype(BF)
+
+    early[0] = wide
+    late = dict(early)
+    late[2] = shift(wide[:, : 2 * half], "dp", 2)
+    early, late = [[w[k] for k in range(dps)] for w in (early, late)]
+
+    sent_products = project_query(info, dq, flip(dq), early)
+    products = [sent_products[0]]
+    for k in range(1, 4):
+        pairs_x = [(s, s // 4 * 4 + (s + k) % 4) for s in range(servers)]
+        products.append(lax.ppermute(sent_products[k], "server", pairs_x))
+
+    for k in range(BACK - 1, -1, -1):
+        held = (totals[k] + shift(held, "server", -4).astype(F32)).astype(BF)
+    held, products = lax.optimization_barrier((held, products))
     kv_grad = jnp.concatenate([swap(held[:ROWS], 0), swap(held[ROWS:], 1)], 1)
     kv_grad = jnp.concatenate([kv_grad, flip(kv_grad)], 1)
-    kv_term = nt(kv_grad, kv_weight)
-    mine = kv_term.reshape(ROWS, dps, -1) + query_term.transpose(1, 0, 2).astype(F32)
-    mine = mine.astype(BF)
+    mine = project(kv_grad, late, products)
     theirs = flip(mine)
-    out = jnp.stack(
-        [jnp.where(core == 0, mine, theirs), jnp.where(core == 0, theirs, mine)], 2
-    )
-    return out.reshape(1, ROWS, -1)
+    where = jnp.stack([dp, core]).astype(jnp.int32)
+    return assemble(where, mine, theirs)[None]
 
 
 def solution(mesh):

time: 151 us -> 136 us (0.901)
  between operations: 13.9 us -> 0.44 us
  Pallas kernels: 11.8 us -> 20.6 us
  waiting for transfers between devices: 72.3 us -> 64.4 us
  matrix products: 6.56 us -> 0 us
  starting transfers between devices: 36.9 us -> 42.3 us
  local copies, waits for them, and re-layouts: 4.71 us -> 2.31 us
    ppermute x14 -> x12, waiting for transfers between devices: 51 us -> 30.4 us  [shift(): return lax.ppermute(x, axis, [(i, (i + k) % n) for i in range(n)])]
    ppermute x0 -> x3, waiting for transfers between devices: none -> 18 us  [body(): products.append(lax.ppermute(sent_products[k], 'server', pairs_x))]
    ppermute x8 -> x6, waiting for transfers between devices: 19.8 us -> 10.9 us  [swap(): return lax.ppermute(x, both, pairs[j])]
    pallas_call x1 -> x4, Pallas kernels: 11.8 us -> 20.6 us  [the longest x1 12.4 us: attention(): pl.pallas_call(attention_kernel, out_shape=(jax.ShapeDtypeStruct((CHUNK,...]
    ppermute x8 -> x6, starting transfers between devices: 23.6 us -> 18.4 us  [swap(): return lax.ppermute(x, both, pairs[j])]
    ppermute x14 -> x12, starting transfers between devices: 11.4 us -> 15.5 us  [shift(): return lax.ppermute(x, axis, [(i, (i + k) % n) for i in range(n)])]
    ppermute x0 -> x3, starting transfers between devices: none -> 3.64 us  [body(): products.append(lax.ppermute(sent_products[k], 'server', pairs_x))]
    ppermute x7 -> x6, waiting for transfers between devices: 1.55 us -> 5.13 us  [flip(): return lax.ppermute(x, 'section', [(0, 1), (1, 0)])]
  transfers between devices with their start and end apart: 30 -> 27, of which waited for: 20 -> 18; matrix products, arithmetic and copies ran while one was open for 6% -> 2% of each run, Pallas kernels for 8% -> 2%
where the time goes in v2:
time: 136 us; the launch traced here: 135 us
  waiting for transfers between devices  64.4 us (47%)
  starting transfers between devices  42.3 us (31%)
  Pallas kernels  20.6 us (15%)
  other arithmetic  4.96 us (4%)
  local copies, waits for them, and re-layouts  2.31 us (2%)
    ppermute x12, waiting for transfers between devices, shift(): return lax.ppermute(x, axis, [(i, (i + k) % n) for i in range(n)])  30.4 us
    ppermute x6, starting transfers between devices, swap(): return lax.ppermute(x, both, pairs[j])  18.4 us
    ppermute x3, waiting for transfers between devices, body(): products.append(lax.ppermute(sent_products[k], 'server', pairs_x))  18 us
    ppermute x12, starting transfers between devices, shift(): return lax.ppermute(x, axis, [(i, (i + k) % n) for i in range(n)])  15.5 us
    pallas_call x1, Pallas kernels, attention(): pl.pallas_call(attention_kernel, out_shape=(jax.ShapeDtypeStruct((CHUNK,...  12.4 us
    ppermute x6, waiting for transfers between devices, swap(): return lax.ppermute(x, both, pairs[j])  10.9 us
    ppermute x6, waiting for transfers between devices, flip(): return lax.ppermute(x, 'section', [(0, 1), (1, 0)])  5.13 us
    ppermute x6, starting transfers between devices, flip(): return lax.ppermute(x, 'section', [(0, 1), (1, 0)])  4.75 us
  transfers between devices with their start and end apart: 27, of which 18 were waited for; matrix products, arithmetic and copies ran while one was open for 2% of the time, Pallas kernels for 2%

profile of v2, /device:TPU:1, one launch (start us, length us, event | category | flops | bytes accessed | tf_op | source)
XLA Modules:
  0.0 135.1 jit_solution(10618673091596755044)
XLA Ops:
  0.0 1.7 %slice_select_fusion = bf16[1024,512]{1,0:T(8,128)(2,1)S(1)} fusion(bf16[1024,1024]{1,0:T(8,128)(2,1)} %param.13, pred[]{:T(512)S(6)} %eq.10), kind=kLoop, calls=%fused_computation.4 | loop fusion | flops 524288 | bytes 3145729 | tf_op jit(solution)/shard_map/jit(_where)/select_n | solution.py:296
  2.7 3.3 %collective-permute-start.9 = (bf16[512,1024]{1,0:T(8,128)(2,1)S(1)}, bf16[512,1024]{1,0:T(8,128)(2,1)S(1)}, u32[]{:S(2)}, u32[]{:S(2)}) collective-permute-start(bf16[512,1024]{1,0:T(8,128)(2,1)S(1)} %get-tuple-element.34), channel_id=1, source_target_pairs={{0,4},{4,0},{1,5},{5,1},{2,6},{6,2},{3,7},{7,3},{8,12},{12,8},{9,1... | collective-permute-start | bytes 3145736 | tf_op jit(solution)/shard_map/ppermute | solution.py:275
  7.5 2.2 %collective-permute-start = (bf16[128,256]{1,0:T(8,128)(2,1)S(1)}, bf16[128,256]{1,0:T(8,128)(2,1)S(1)}, u32[]{:S(2)}, u32[]{:S(2)}) collective-permute-start(bf16[128,256]{1,0:T(8,128)(2,1)S(1)} %get-tuple-element.53), channel_id=1, source_target_pairs={{0,0},{4,16},{8,8},{12,24},{16,4},{20,20},{24,12},{28,28},{32,32},... | collective-permute-start | bytes 196616 | tf_op jit(solution)/shard_map/ppermute | solution.py:268
  10.0 2.8 %collective-permute-start.11 = (bf16[512,1536]{1,0:T(8,128)(2,1)S(1)}, bf16[512,1536]{1,0:T(8,128)(2,1)S(1)}, u32[]{:S(2)}, u32[]{:S(2)}) collective-permute-start(bf16[512,1536]{1,0:T(8,128)(2,1)S(1)} %pad_maximum_fusion.1.refs_0_), channel_id=1, source_target_pairs={{0,3},{1,0},{2,1},{3,2},{4,7},{5,4},{6,5},{7,6},{8,11},{9,8},{10,9... | collective-permute-start | bytes 4718600 | tf_op jit(solution)/shard_map/ppermute | solution.py:272
  12.8 1.7 %collective-permute-done = bf16[128,256]{1,0:T(8,128)(2,1)S(1)} collective-permute-done((bf16[128,256]{1,0:T(8,128)(2,1)S(1)}, bf16[128,256]{1,0:T(8,128)(2,1)S(1)}, u32[]{:S(2)}, u32[]{:S(2)}) %collective-permute-start) | collective-permute-done | bytes 65568 | tf_op jit(solution)/shard_map/ppermute | solution.py:268
  14.6 1.7 %collective-permute-start.4 = (bf16[256,256]{1,0:T(8,128)(2,1)S(1)}, bf16[256,256]{1,0:T(8,128)(2,1)S(1)}, u32[]{:S(2)}, u32[]{:S(2)}) collective-permute-start(bf16[256,256]{1,0:T(8,128)(2,1)S(1)} %constant_dynamic-update-slice_fusion.refs_0_), channel_id=1, source_target_pairs={{0,32},{8,40},{16,48},{24,56},{32,64},{40,72},{48,80},{56,88},{64,... | collective-permute-start | bytes 393224 | tf_op jit(solution)/shard_map/ppermute | solution.py:272
  16.3 6.7 %collective-permute-done.4.refs_1_ = bf16[256,256]{1,0:T(8,128)(2,1)S(1)} collective-permute-done((bf16[256,256]{1,0:T(8,128)(2,1)S(1)}, bf16[256,256]{1,0:T(8,128)(2,1)S(1)}, u32[]{:S(2)}, u32[]{:S(2)}) %collective-permute-start.4) | collective-permute-done | bytes 131104 | tf_op jit(solution)/shard_map/ppermute | solution.py:272
  23.0 5.4 %collective-permute-done.5.refs_2_ = bf16[256,256]{1,0:T(8,128)(2,1)S(1)} collective-permute-done((bf16[256,256]{1,0:T(8,128)(2,1)S(1)}, bf16[256,256]{1,0:T(8,128)(2,1)S(1)}, u32[]{:S(2)}, u32[]{:S(2)}) %collective-permute-start.5) | collective-permute-done | bytes 131104 | tf_op jit(solution)/shard_map/ppermute | solution.py:272
  28.4 5.4 %collective-permute-done.6.refs_3_ = bf16[256,256]{1,0:T(8,128)(2,1)S(1)} collective-permute-done((bf16[256,256]{1,0:T(8,128)(2,1)S(1)}, bf16[256,256]{1,0:T(8,128)(2,1)S(1)}, u32[]{:S(2)}, u32[]{:S(2)}) %collective-permute-start.6) | collective-permute-done | bytes 131104 | tf_op jit(solution)/shard_map/ppermute | solution.py:272
  33.9 5.4 %collective-permute-done.7.refs_4_ = bf16[256,256]{1,0:T(8,128)(2,1)S(1)} collective-permute-done((bf16[256,256]{1,0:T(8,128)(2,1)S(1)}, bf16[256,256]{1,0:T(8,128)(2,1)S(1)}, u32[]{:S(2)}, u32[]{:S(2)}) %collective-permute-start.7) | collective-permute-done | bytes 131104 | tf_op jit(solution)/shard_map/ppermute | solution.py:272
  41.2 4.9 %collective-permute-start.3 = (bf16[128,1024]{1,0:T(8,128)(2,1)}, bf16[128,1024]{1,0:T(8,128)(2,1)}, u32[]{:S(2)}, u32[]{:S(2)}) collective-permute-start(bf16[128,1024]{1,0:T(8,128)(2,1)} %get-tuple-element.44), channel_id=1, source_target_pairs={{0,8},{4,24},{8,0},{12,16},{16,12},{20,28},{24,4},{28,20},{32,40},... | collective-permute-start | bytes 786440 | tf_op jit(solution)/shard_map/ppermute | solution.py:268
  46.1 3.5 %collective-permute-start.2 = (bf16[128,1024]{1,0:T(8,128)(2,1)}, bf16[128,1024]{1,0:T(8,128)(2,1)}, u32[]{:S(2)}, u32[]{:S(2)}) collective-permute-start(bf16[128,1024]{1,0:T(8,128)(2,1)} %get-tuple-element.45), channel_id=1, source_target_pairs={{0,0},{4,16},{8,8},{12,24},{16,4},{20,20},{24,12},{28,28},{32,32},... | collective-permute-start | bytes 786440 | tf_op jit(solution)/shard_map/ppermute | solution.py:268
  50.5 5.1 %collective-permute-done.2.qg0 = bf16[128,1024]{1,0:T(8,128)(2,1)} collective-permute-done((bf16[128,1024]{1,0:T(8,128)(2,1)}, bf16[128,1024]{1,0:T(8,128)(2,1)}, u32[]{:S(2)}, u32[]{:S(2)}) %collective-permute-start.2) | collective-permute-done | bytes 262176 | tf_op jit(solution)/shard_map/ppermute | solution.py:268
  57.4 12.4 %attention_grads.1 = (bf16[256,512]{1,0:T(8,128)(2,1)S(1)}, f32[5,256,256]{2,1,0:T(8,128)S(1)}, bf16[4,256,256]{2,1,0:T(8,128)(2,1)S(1)}) custom-call(s32[16]{0:T(128)S(1)} %concatenate.46.info, bf16[128,1024]{1,0:T(8,128)(2,1)} %collective-permute-done.2.qg0, bf16[128,1024]{1,0:T(8,128)(2,1)} %collective-permute-done.3.qg1, ...), custom_call_target="tpu_custom_call" | custom-call | flops 3019898880 | bytes 8388608 | tf_op jit(solution)/shard_map/attention_grads/pallas_call | solution.py:132
  70.0 1.9 %collective-permute-done.12 = bf16[4,256,256]{2,1,0:T(8,128)(2,1)S(1)} collective-permute-done((bf16[4,256,256]{2,1,0:T(8,128)(2,1)S(1)}, bf16[4,256,256]{2,1,0:T(8,128)(2,1)S(1)}, u32[]{:S(2)}, u32[]{:S(2)}) %collective-permute-start.12) | collective-permute-done | bytes 524320 | tf_op jit(solution)/shard_map/ppermute | solution.py:275
  72.2 3.2 %collective-permute-start.18 = (bf16[512,512]{1,0:T(8,128)(2,1)S(1)}, bf16[512,512]{1,0:T(8,128)(2,1)S(1)}, u32[]{:S(2)}, u32[]{:S(2)}) collective-permute-start(bf16[512,512]{1,0:T(8,128)(2,1)S(1)} %copy-done.9), channel_id=1, source_target_pairs={{0,2},{1,3},{2,0},{3,1},{4,6},{5,7},{6,4},{7,5},{8,10},{9,11},{10,... | collective-permute-start | bytes 1572872 | tf_op jit(solution)/shard_map/ppermute | solution.py:272
  75.4 1.7 %collective-permute-done.13 = bf16[256,256]{1,0:T(8,128)(2,1)S(1)} collective-permute-done((bf16[256,256]{1,0:T(8,128)(2,1)S(1)}, bf16[256,256]{1,0:T(8,128)(2,1)S(1)}, u32[]{:S(2)}, u32[]{:S(2)}) %collective-permute-start.13) | collective-permute-done | bytes 131104 | tf_op jit(solution)/shard_map/ppermute | solution.py:272
  79.7 1.7 %collective-permute-done.14 = bf16[256,256]{1,0:T(8,128)(2,1)S(1)} collective-permute-done((bf16[256,256]{1,0:T(8,128)(2,1)S(1)}, bf16[256,256]{1,0:T(8,128)(2,1)S(1)}, u32[]{:S(2)}, u32[]{:S(2)}) %collective-permute-start.14) | collective-permute-done | bytes 131104 | tf_op jit(solution)/shard_map/ppermute | solution.py:272
  81.4 3.0 %collective-permute-start.15 = (bf16[256,256]{1,0:T(8,128)(2,1)S(1)}, bf16[256,256]{1,0:T(8,128)(2,1)S(1)}, u32[]{:S(2)}, u32[]{:S(2)}) collective-permute-start(bf16[256,256]{1,0:T(8,128)(2,1)S(1)} %fusion.3), channel_id=1, source_target_pairs={{0,224},{8,232},{16,240},{24,248},{32,0},{40,8},{48,16},{56,24},{6... | collective-permute-start | bytes 393224 | tf_op jit(solution)/shard_map/ppermute | solution.py:272
  84.4 3.1 %collective-permute-start.25 = (bf16[512,1024]{1,0:T(8,128)(2,1)S(1)}, bf16[512,1024]{1,0:T(8,128)(2,1)S(1)}, u32[]{:S(2)}, u32[]{:S(2)}) collective-permute-start(bf16[512,1024]{1,0:T(8,128)(2,1)S(1)} %pad_maximum_fusion.2), channel_id=1, source_target_pairs={{0,2},{1,3},{2,0},{3,1},{4,6},{5,7},{6,4},{7,5},{8,10},{9,11},{10,... | collective-permute-start | bytes 3145736 | tf_op jit(solution)/shard_map/ppermute | solution.py:272
  87.5 2.4 %project_query.1 = (bf16[128,2048]{1,0:T(8,128)(2,1)S(1)}, bf16[128,2048]{1,0:T(8,128)(2,1)S(1)}, bf16[128,2048]{1,0:T(8,128)(2,1)S(1)}, bf16[128,2048]{1,0:T(8,128)(2,1)S(1)}) custom-call(s32[16]{0:T(128)S(1)} %concatenate.46.info, bf16[256,512]{1,0:T(8,128)(2,1)S(1)} %get-tuple-element.23.dq, bf16[256,512]{1,0:T(8,128)(2,1)S(1)} %collective-permute-done.17.other, ...), custom_call_target="tpu_custom_call" | custom-call | flops 1073741824 | bytes 4194304 | tf_op jit(solution)/shard_map/project_query/pallas_call | solution.py:180
  91.2 2.4 %collective-permute-start.21 = (bf16[128,2048]{1,0:T(8,128)(2,1)S(1)}, bf16[128,2048]{1,0:T(8,128)(2,1)S(1)}, u32[]{:S(2)}, u32[]{:S(2)}) collective-permute-start(bf16[128,2048]{1,0:T(8,128)(2,1)S(1)} %get-tuple-element.27), channel_id=1, source_target_pairs={{0,24},{8,0},{16,8},{24,16},{32,56},{40,32},{48,40},{56,48},{64,88... | collective-permute-start | bytes 1572872 | tf_op jit(solution)/shard_map/ppermute | solution.py:346
  93.6 4.1 %collective-permute-done.16 = bf16[256,256]{1,0:T(8,128)(2,1)S(1)} collective-permute-done((bf16[256,256]{1,0:T(8,128)(2,1)S(1)}, bf16[256,256]{1,0:T(8,128)(2,1)S(1)}, u32[]{:S(2)}, u32[]{:S(2)}) %collective-permute-start.16) | collective-permute-done | bytes 131104 | tf_op jit(solution)/shard_map/ppermute | solution.py:272
  97.8 6.3 %collective-permute-done.19.refs_5_ = bf16[128,2048]{1,0:T(8,128)(2,1)S(1)} collective-permute-done((bf16[128,2048]{1,0:T(8,128)(2,1)S(1)}, bf16[128,2048]{1,0:T(8,128)(2,1)S(1)}, u32[]{:S(2)}, u32[]{:S(2)}) %collective-permute-start.19) | collective-permute-done | bytes 524320 | tf_op jit(solution)/shard_map/ppermute | solution.py:346
  104.1 8.4 %collective-permute-done.20.refs_6_ = bf16[128,2048]{1,0:T(8,128)(2,1)S(1)} collective-permute-done((bf16[128,2048]{1,0:T(8,128)(2,1)S(1)}, bf16[128,2048]{1,0:T(8,128)(2,1)S(1)}, u32[]{:S(2)}, u32[]{:S(2)}) %collective-permute-start.20) | collective-permute-done | bytes 524320 | tf_op jit(solution)/shard_map/ppermute | solution.py:346
  112.5 3.3 %collective-permute-done.21.refs_7_ = bf16[128,2048]{1,0:T(8,128)(2,1)S(1)} collective-permute-done((bf16[128,2048]{1,0:T(8,128)(2,1)S(1)}, bf16[128,2048]{1,0:T(8,128)(2,1)S(1)}, u32[]{:S(2)}, u32[]{:S(2)}) %collective-permute-start.21) | collective-permute-done | bytes 524320 | tf_op jit(solution)/shard_map/ppermute | solution.py:346
  115.8 4.8 %collective-permute-start.22 = (bf16[128,256]{1,0:T(8,128)(2,1)S(1)}, bf16[128,256]{1,0:T(8,128)(2,1)S(1)}, u32[]{:S(2)}, u32[]{:S(2)}) collective-permute-start(bf16[128,256]{1,0:T(8,128)(2,1)S(1)} %get-tuple-element.50), channel_id=1, source_target_pairs={{0,0},{4,16},{8,8},{12,24},{16,4},{20,20},{24,12},{28,28},{32,32},... | collective-permute-start | bytes 196616 | tf_op jit(solution)/shard_map/ppermute | solution.py:268
  120.7 1.7 %collective-permute-start.23 = (bf16[128,256]{1,0:T(8,128)(2,1)S(1)}, bf16[128,256]{1,0:T(8,128)(2,1)S(1)}, u32[]{:S(2)}, u32[]{:S(2)}) collective-permute-start(bf16[128,256]{1,0:T(8,128)(2,1)S(1)} %get-tuple-element.51), channel_id=1, source_target_pairs={{0,8},{4,24},{8,0},{12,16},{16,12},{20,28},{24,4},{28,20},{32,40},... | collective-permute-start | bytes 196616 | tf_op jit(solution)/shard_map/ppermute | solution.py:268
  123.5 2.1 %collective-permute-done.23 = bf16[128,256]{1,0:T(8,128)(2,1)S(1)} collective-permute-done((bf16[128,256]{1,0:T(8,128)(2,1)S(1)}, bf16[128,256]{1,0:T(8,128)(2,1)S(1)}, u32[]{:S(2)}, u32[]{:S(2)}) %collective-permute-start.23) | collective-permute-done | bytes 65568 | tf_op jit(solution)/shard_map/ppermute | solution.py:268
  127.1 3.7 %project_kv.1.mine = bf16[4,128,512]{2,1,0:T(8,128)(2,1)} custom-call(bf16[128,1024]{1,0:T(8,128)(2,1)S(1)} %pad_maximum_fusion.7.grad, bf16[512,1536]{1,0:T(8,128)(2,1)S(1)} %pad_maximum_fusion.1.refs_0_, bf16[512,1536]{1,0:T(8,128)(2,1)} %collective-permute-done.10.refs_6_.refs_1_, bf16[512,1024]{1,0:T(8,128)(2,1)S(1)} %collective-permute-done.25.refs_2_, ...), custom_call_target="tpu_custom_call" | custom-call | flops 536870912 | bytes 8388608 | tf_op jit(solution)/shard_map/project_kv/pallas_call | solution.py:210
  131.1 1.9 %collective-permute-done.26.theirs = bf16[4,128,512]{2,1,0:T(8,128)(2,1)S(1)} collective-permute-done((bf16[4,128,512]{2,1,0:T(8,128)(2,1)}, bf16[4,128,512]{2,1,0:T(8,128)(2,1)S(1)}, u32[]{:S(2)}, u32[]{:S(2)}) %collective-permute-start.26) | collective-permute-done | bytes 524320 | tf_op jit(solution)/shard_map/ppermute | solution.py:275
  133.0 2.1 %assemble.1 = bf16[128,4096]{1,0:T(8,128)(2,1)} custom-call(s32[2]{0:T(128)S(1)} %pad_add_fusion.where, bf16[4,128,512]{2,1,0:T(8,128)(2,1)} %project_kv.1.mine, bf16[4,128,512]{2,1,0:T(8,128)(2,1)S(1)} %collective-permute-done.26.theirs), custom_call_target="tpu_custom_call" | custom-call | tf_op jit(solution)/shard_map/assemble/pallas_call | solution.py:237
  (88 shorter events, 14.5 us)
Async XLA Ops:
  2.7 7.0 %collective-permute-start.9 = (bf16[512,1024]{1,0:T(8,128)(2,1)S(1)}, bf16[512,1024]{1,0:T(8,128)(2,1)S(1)}, u32[]{:S(2)}, u32[]{:S(2)}) collective-permute-start(bf16[512,1024]{1,0:T(8,128)(2,1)S(1)} %get-tuple-element.34), channel_id=1, source_target_pairs={{0,4},{4,0},{1,5},{5,1},{2,6},{6,2},{3,7},{7,3},{8,12},{12,8},{9,1... | collective-permute-start | bytes 3145736 | tf_op jit(solution)/shard_map/ppermute | solution.py:275
  6.1 8.4 %collective-permute-start.1 = (bf16[128,256]{1,0:T(8,128)(2,1)S(1)}, bf16[128,256]{1,0:T(8,128)(2,1)S(1)}, u32[]{:S(2)}, u32[]{:S(2)}) collective-permute-start(bf16[128,256]{1,0:T(8,128)(2,1)S(1)} %get-tuple-element.52), channel_id=1, source_target_pairs={{0,8},{4,24},{8,0},{12,16},{16,12},{20,28},{24,4},{28,20},{32,40},... | collective-permute-start | bytes 196616 | tf_op jit(solution)/shard_map/ppermute | solution.py:268
  7.5 7.1 %collective-permute-start = (bf16[128,256]{1,0:T(8,128)(2,1)S(1)}, bf16[128,256]{1,0:T(8,128)(2,1)S(1)}, u32[]{:S(2)}, u32[]{:S(2)}) collective-permute-start(bf16[128,256]{1,0:T(8,128)(2,1)S(1)} %get-tuple-element.53), channel_id=1, source_target_pairs={{0,0},{4,16},{8,8},{12,24},{16,4},{20,20},{24,12},{28,28},{32,32},... | collective-permute-start | bytes 196616 | tf_op jit(solution)/shard_map/ppermute | solution.py:268
  9.8 30.3 %copy-start.4 = (bf16[512,512]{1,0:T(8,128)(2,1)}, bf16[512,512]{1,0:T(8,128)(2,1)S(1)}, u32[]{:S(2)}) copy-start(bf16[512,512]{1,0:T(8,128)(2,1)S(1)} %get-tuple-element.35) | copy-start | bytes 1572868
  9.9 30.3 %copy-start.6 = (bf16[512,512]{1,0:T(8,128)(2,1)}, bf16[512,512]{1,0:T(8,128)(2,1)S(1)}, u32[]{:S(2)}) copy-start(bf16[512,512]{1,0:T(8,128)(2,1)S(1)} %get-tuple-element.37) | copy-start | bytes 1572868
  9.9 30.3 %copy-start.8 = (bf16[512,512]{1,0:T(8,128)(2,1)}, bf16[512,512]{1,0:T(8,128)(2,1)S(1)}, u32[]{:S(2)}) copy-start(bf16[512,512]{1,0:T(8,128)(2,1)S(1)} %get-tuple-element.36) | copy-start | bytes 1572868
  9.9 30.4 %copy-start.13 = (bf16[1,128,1024]{2,1,0:T(8,128)(2,1)S(1)}, bf16[1,128,1024]{2,1,0:T(8,128)(2,1)}, u32[]{:S(2)}) copy-start(bf16[1,128,1024]{2,1,0:T(8,128)(2,1)} %param.8) | copy-start | bytes 786436
  10.0 39.6 %copy-start.16 = (s32[1,8]{1,0:T(1,128)S(1)}, s32[1,8]{1,0:T(1,128)}, u32[]{:S(2)}) copy-start(s32[1,8]{1,0:T(1,128)} %param.12) | copy-start | bytes 100
  10.0 45.6 %collective-permute-start.11 = (bf16[512,1536]{1,0:T(8,128)(2,1)S(1)}, bf16[512,1536]{1,0:T(8,128)(2,1)S(1)}, u32[]{:S(2)}, u32[]{:S(2)}) collective-permute-start(bf16[512,1536]{1,0:T(8,128)(2,1)S(1)} %pad_maximum_fusion.1.refs_0_), channel_id=1, source_target_pairs={{0,3},{1,0},{2,1},{3,2},{4,7},{5,4},{6,5},{7,6},{8,11},{9,8},{10,9... | collective-permute-start | bytes 4718600 | tf_op jit(solution)/shard_map/ppermute | solution.py:272
  12.8 42.8 %collective-permute-start.10 = (bf16[512,1536]{1,0:T(8,128)(2,1)S(1)}, bf16[512,1536]{1,0:T(8,128)(2,1)}, u32[]{:S(2)}, u32[]{:S(2)}) collective-permute-start(bf16[512,1536]{1,0:T(8,128)(2,1)S(1)} %pad_maximum_fusion.1.refs_0_), channel_id=1, source_target_pairs={{0,1},{1,2},{2,3},{3,0},{4,5},{5,6},{6,7},{7,4},{8,9},{9,10},{10,1... | collective-permute-start | bytes 4718600 | tf_op jit(solution)/shard_map/ppermute | solution.py:272
  14.6 8.4 %collective-permute-start.4 = (bf16[256,256]{1,0:T(8,128)(2,1)S(1)}, bf16[256,256]{1,0:T(8,128)(2,1)S(1)}, u32[]{:S(2)}, u32[]{:S(2)}) collective-permute-start(bf16[256,256]{1,0:T(8,128)(2,1)S(1)} %constant_dynamic-update-slice_fusion.refs_0_), channel_id=1, source_target_pairs={{0,32},{8,40},{16,48},{24,56},{32,64},{40,72},{48,80},{56,88},{64,... | collective-permute-start | bytes 393224 | tf_op jit(solution)/shard_map/ppermute | solution.py:272
  23.0 5.4 %collective-permute-start.5 = (bf16[256,256]{1,0:T(8,128)(2,1)S(1)}, bf16[256,256]{1,0:T(8,128)(2,1)S(1)}, u32[]{:S(2)}, u32[]{:S(2)}) collective-permute-start(bf16[256,256]{1,0:T(8,128)(2,1)S(1)} %collective-permute-done.4.refs_1_), channel_id=1, source_target_pairs={{0,32},{8,40},{16,48},{24,56},{32,64},{40,72},{48,80},{56,88},{64,... | collective-permute-start | bytes 393224 | tf_op jit(solution)/shard_map/ppermute | solution.py:272
  28.4 5.4 %collective-permute-start.6 = (bf16[256,256]{1,0:T(8,128)(2,1)S(1)}, bf16[256,256]{1,0:T(8,128)(2,1)S(1)}, u32[]{:S(2)}, u32[]{:S(2)}) collective-permute-start(bf16[256,256]{1,0:T(8,128)(2,1)S(1)} %collective-permute-done.5.refs_2_), channel_id=1, source_target_pairs={{0,32},{8,40},{16,48},{24,56},{32,64},{40,72},{48,80},{56,88},{64,... | collective-permute-start | bytes 393224 | tf_op jit(solution)/shard_map/ppermute | solution.py:272
  33.8 5.4 %collective-permute-start.7 = (bf16[256,256]{1,0:T(8,128)(2,1)S(1)}, bf16[256,256]{1,0:T(8,128)(2,1)S(1)}, u32[]{:S(2)}, u32[]{:S(2)}) collective-permute-start(bf16[256,256]{1,0:T(8,128)(2,1)S(1)} %collective-permute-done.6.refs_3_), channel_id=1, source_target_pairs={{0,32},{8,40},{16,48},{24,56},{32,64},{40,72},{48,80},{56,88},{64,... | collective-permute-start | bytes 393224 | tf_op jit(solution)/shard_map/ppermute | solution.py:272
  40.2 15.4 %collective-permute-start.8 = (bf16[4,256,256]{2,1,0:T(8,128)(2,1)}, bf16[4,256,256]{2,1,0:T(8,128)(2,1)}, u32[]{:S(2)}, u32[]{:S(2)}) collective-permute-start(bf16[4,256,256]{2,1,0:T(8,128)(2,1)} %maximum_select_fusion), channel_id=1, source_target_pairs={{0,4},{4,0},{1,5},{5,1},{2,6},{6,2},{3,7},{7,3},{8,12},{12,8},{9,1... | collective-permute-start | bytes 1572872 | tf_op jit(solution)/shard_map/ppermute | solution.py:275
  41.2 9.3 %collective-permute-start.3 = (bf16[128,1024]{1,0:T(8,128)(2,1)}, bf16[128,1024]{1,0:T(8,128)(2,1)}, u32[]{:S(2)}, u32[]{:S(2)}) collective-permute-start(bf16[128,1024]{1,0:T(8,128)(2,1)} %get-tuple-element.44), channel_id=1, source_target_pairs={{0,8},{4,24},{8,0},{12,16},{16,12},{20,28},{24,4},{28,20},{32,40},... | collective-permute-start | bytes 786440 | tf_op jit(solution)/shard_map/ppermute | solution.py:268
  46.1 9.5 %collective-permute-start.2 = (bf16[128,1024]{1,0:T(8,128)(2,1)}, bf16[128,1024]{1,0:T(8,128)(2,1)}, u32[]{:S(2)}, u32[]{:S(2)}) collective-permute-start(bf16[128,1024]{1,0:T(8,128)(2,1)} %get-tuple-element.45), channel_id=1, source_target_pairs={{0,0},{4,16},{8,8},{12,24},{16,4},{20,20},{24,12},{28,28},{32,32},... | collective-permute-start | bytes 786440 | tf_op jit(solution)/shard_map/ppermute | solution.py:268
  69.9 2.0 %collective-permute-start.12 = (bf16[4,256,256]{2,1,0:T(8,128)(2,1)S(1)}, bf16[4,256,256]{2,1,0:T(8,128)(2,1)S(1)}, u32[]{:S(2)}, u32[]{:S(2)}) collective-permute-start(bf16[4,256,256]{2,1,0:T(8,128)(2,1)S(1)} %get-tuple-element.22), channel_id=1, source_target_pairs={{0,4},{4,0},{1,5},{5,1},{2,6},{6,2},{3,7},{7,3},{8,12},{12,8},{9,1... | collective-permute-start | bytes 1572872 | tf_op jit(solution)/shard_map/ppermute | solution.py:275
  72.1 5.0 %collective-permute-start.13 = (bf16[256,256]{1,0:T(8,128)(2,1)S(1)}, bf16[256,256]{1,0:T(8,128)(2,1)S(1)}, u32[]{:S(2)}, u32[]{:S(2)}) collective-permute-start(bf16[256,256]{1,0:T(8,128)(2,1)S(1)} %fusion.8), channel_id=1, source_target_pairs={{0,224},{8,232},{16,240},{24,248},{32,0},{40,8},{48,16},{56,24},{6... | collective-permute-start | bytes 393224 | tf_op jit(solution)/shard_map/ppermute | solution.py:272
  72.2 15.3 %collective-permute-start.18 = (bf16[512,512]{1,0:T(8,128)(2,1)S(1)}, bf16[512,512]{1,0:T(8,128)(2,1)S(1)}, u32[]{:S(2)}, u32[]{:S(2)}) collective-permute-start(bf16[512,512]{1,0:T(8,128)(2,1)S(1)} %copy-done.9), channel_id=1, source_target_pairs={{0,2},{1,3},{2,0},{3,1},{4,6},{5,7},{6,4},{7,5},{8,10},{9,11},{10,... | collective-permute-start | bytes 1572872 | tf_op jit(solution)/shard_map/ppermute | solution.py:272
  77.1 4.2 %collective-permute-start.14 = (bf16[256,256]{1,0:T(8,128)(2,1)S(1)}, bf16[256,256]{1,0:T(8,128)(2,1)S(1)}, u32[]{:S(2)}, u32[]{:S(2)}) collective-permute-start(bf16[256,256]{1,0:T(8,128)(2,1)S(1)} %fusion.1), channel_id=1, source_target_pairs={{0,224},{8,232},{16,240},{24,248},{32,0},{40,8},{48,16},{56,24},{6... | collective-permute-start | bytes 393224 | tf_op jit(solution)/shard_map/ppermute | solution.py:272
  78.7 8.8 %collective-permute-start.17 = (bf16[256,512]{1,0:T(8,128)(2,1)S(1)}, bf16[256,512]{1,0:T(8,128)(2,1)S(1)}, u32[]{:S(2)}, u32[]{:S(2)}) collective-permute-start(bf16[256,512]{1,0:T(8,128)(2,1)S(1)} %get-tuple-element.23.dq), channel_id=1, source_target_pairs={{0,4},{4,0},{1,5},{5,1},{2,6},{6,2},{3,7},{7,3},{8,12},{12,8},{9,1... | collective-permute-start | bytes 786440 | tf_op jit(solution)/shard_map/ppermute | solution.py:275
  81.4 12.2 %collective-permute-start.15 = (bf16[256,256]{1,0:T(8,128)(2,1)S(1)}, bf16[256,256]{1,0:T(8,128)(2,1)S(1)}, u32[]{:S(2)}, u32[]{:S(2)}) collective-permute-start(bf16[256,256]{1,0:T(8,128)(2,1)S(1)} %fusion.3), channel_id=1, source_target_pairs={{0,224},{8,232},{16,240},{24,248},{32,0},{40,8},{48,16},{56,24},{6... | collective-permute-start | bytes 393224 | tf_op jit(solution)/shard_map/ppermute | solution.py:272
  84.4 42.7 %collective-permute-start.25 = (bf16[512,1024]{1,0:T(8,128)(2,1)S(1)}, bf16[512,1024]{1,0:T(8,128)(2,1)S(1)}, u32[]{:S(2)}, u32[]{:S(2)}) collective-permute-start(bf16[512,1024]{1,0:T(8,128)(2,1)S(1)} %pad_maximum_fusion.2), channel_id=1, source_target_pairs={{0,2},{1,3},{2,0},{3,1},{4,6},{5,7},{6,4},{7,5},{8,10},{9,11},{10,... | collective-permute-start | bytes 3145736 | tf_op jit(solution)/shard_map/ppermute | solution.py:272
  89.9 14.2 %collective-permute-start.19 = (bf16[128,2048]{1,0:T(8,128)(2,1)S(1)}, bf16[128,2048]{1,0:T(8,128)(2,1)S(1)}, u32[]{:S(2)}, u32[]{:S(2)}) collective-permute-start(bf16[128,2048]{1,0:T(8,128)(2,1)S(1)} %get-tuple-element.25), channel_id=1, source_target_pairs={{0,8},{8,16},{16,24},{24,0},{32,40},{40,48},{48,56},{56,32},{64,72... | collective-permute-start | bytes 1572872 | tf_op jit(solution)/shard_map/ppermute | solution.py:346
  91.0 21.5 %collective-permute-start.20 = (bf16[128,2048]{1,0:T(8,128)(2,1)S(1)}, bf16[128,2048]{1,0:T(8,128)(2,1)S(1)}, u32[]{:S(2)}, u32[]{:S(2)}) collective-permute-start(bf16[128,2048]{1,0:T(8,128)(2,1)S(1)} %get-tuple-element.26), channel_id=1, source_target_pairs={{0,16},{8,24},{16,0},{24,8},{32,48},{40,56},{48,32},{56,40},{64,80... | collective-permute-start | bytes 1572872 | tf_op jit(solution)/shard_map/ppermute | solution.py:346
  91.2 24.6 %collective-permute-start.21 = (bf16[128,2048]{1,0:T(8,128)(2,1)S(1)}, bf16[128,2048]{1,0:T(8,128)(2,1)S(1)}, u32[]{:S(2)}, u32[]{:S(2)}) collective-permute-start(bf16[128,2048]{1,0:T(8,128)(2,1)S(1)} %get-tuple-element.27), channel_id=1, source_target_pairs={{0,24},{8,0},{16,8},{24,16},{32,56},{40,32},{48,40},{56,48},{64,88... | collective-permute-start | bytes 1572872 | tf_op jit(solution)/shard_map/ppermute | solution.py:346
  93.6 4.2 %collective-permute-start.16 = (bf16[256,256]{1,0:T(8,128)(2,1)S(1)}, bf16[256,256]{1,0:T(8,128)(2,1)S(1)}, u32[]{:S(2)}, u32[]{:S(2)}) collective-permute-start(bf16[256,256]{1,0:T(8,128)(2,1)S(1)} %fusion.5), channel_id=1, source_target_pairs={{0,224},{8,232},{16,240},{24,248},{32,0},{40,8},{48,16},{56,24},{6... | collective-permute-start | bytes 393224 | tf_op jit(solution)/shard_map/ppermute | solution.py:272
  115.8 7.7 %collective-permute-start.22 = (bf16[128,256]{1,0:T(8,128)(2,1)S(1)}, bf16[128,256]{1,0:T(8,128)(2,1)S(1)}, u32[]{:S(2)}, u32[]{:S(2)}) collective-permute-start(bf16[128,256]{1,0:T(8,128)(2,1)S(1)} %get-tuple-element.50), channel_id=1, source_target_pairs={{0,0},{4,16},{8,8},{12,24},{16,4},{20,20},{24,12},{28,28},{32,32},... | collective-permute-start | bytes 196616 | tf_op jit(solution)/shard_map/ppermute | solution.py:268
  120.7 5.0 %collective-permute-start.23 = (bf16[128,256]{1,0:T(8,128)(2,1)S(1)}, bf16[128,256]{1,0:T(8,128)(2,1)S(1)}, u32[]{:S(2)}, u32[]{:S(2)}) collective-permute-start(bf16[128,256]{1,0:T(8,128)(2,1)S(1)} %get-tuple-element.51), channel_id=1, source_target_pairs={{0,8},{4,24},{8,0},{12,16},{16,12},{20,28},{24,4},{28,20},{32,40},... | collective-permute-start | bytes 196616 | tf_op jit(solution)/shard_map/ppermute | solution.py:268
  125.7 1.4 %collective-permute-start.24 = (bf16[128,512]{1,0:T(8,128)(2,1)S(1)}, bf16[128,512]{1,0:T(8,128)(2,1)S(1)}, u32[]{:S(2)}, u32[]{:S(2)}) collective-permute-start(bf16[128,512]{1,0:T(8,128)(2,1)S(1)} %pad_maximum_fusion.8), channel_id=1, source_target_pairs={{0,4},{4,0},{1,5},{5,1},{2,6},{6,2},{3,7},{7,3},{8,12},{12,8},{9,1... | collective-permute-start | bytes 393224 | tf_op jit(solution)/shard_map/ppermute | solution.py:275
  130.9 2.1 %collective-permute-start.26 = (bf16[4,128,512]{2,1,0:T(8,128)(2,1)}, bf16[4,128,512]{2,1,0:T(8,128)(2,1)S(1)}, u32[]{:S(2)}, u32[]{:S(2)}) collective-permute-start(bf16[4,128,512]{2,1,0:T(8,128)(2,1)} %project_kv.1.mine), channel_id=1, source_target_pairs={{0,4},{4,0},{1,5},{5,1},{2,6},{6,2},{3,7},{7,3},{8,12},{12,8},{9,1... | collective-permute-start | bytes 1572872 | tf_op jit(solution)/shard_map/ppermute | solution.py:275
  (12 other events, 69.9 us)

commit v3 on v2

--- a/solution.py
+++ b/solution.py
@@ -158,75 +158,83 @@
     )(info, qg0, qg1, *own_blocks, other_blocks, *after)
 
 
-def project_query_kernel(info, dq, other, *refs):
-    n = (len(refs) - 1) // 2
-    weights, outs, rows = refs[:n], refs[n : 2 * n], refs[2 * n]
+def project_query_kernel(info, own, arrived, dq, other, *refs):
+    weights, *outs, totals, held, rows = refs
     core, odd, chip = info[1], info[2], info[3]
+    for k in range(BACK + 1):
+        near = arrived[k].astype(F32) if k < BACK else 0.0
+        far = arrived[k - 1].astype(F32) if k else 0.0
+        total = own[k] + jnp.where(core == 0, near, far)
+        if k < BACK:
+            totals[k] = total
+        else:
+            held[...] = total.astype(BF)
     for source, c in ((dq, core), (other, 1 - core)):
         for slot in range(2):
             owner = 2 * c + jnp.bitwise_xor(odd, slot)
             at = pl.multiple_of(lax.rem(owner - chip + 4, 4) * ROWS, ROWS)
             rows[pl.ds(at, ROWS), :] = source[slot * ROWS : (slot + 1) * ROWS, :]
-    for k in range(n):
-        width = weights[k].shape[0]
-        product = nt(rows[...], weights[k][...]).astype(BF)
+    width = 4 * ROWS
+    for k in range(weights.shape[0] // width):
+        product = nt(rows[...], weights[k * width : (k + 1) * width]).astype(BF)
         for i in range(4):
             outs[i][:, k * width : (k + 1) * width] = product[i * ROWS : (i + 1) * ROWS]
 
 
-def project_query(info, dq, other, weights):
+def project_query(info, own, arrived, dq, other, weights):
     vmem = pl.BlockSpec(memory_space=pltpu.VMEM)
-    n, width, dims = len(weights), weights[0].shape[0], dq.shape[1]
+    width, dims = weights.shape
     return pl.pallas_call(
         project_query_kernel,
-        grid=(1,),
-        out_shape=(jax.ShapeDtypeStruct((ROWS, n * width), BF),) * 4,
-        in_specs=[pl.BlockSpec(memory_space=pltpu.SMEM), vmem, vmem]
-        + [pl.BlockSpec((width, dims), lambda i, at=w.shape[1] // dims - 1: (0, at)) for w in weights],
-        out_specs=(vmem,) * 4,
+        out_shape=(jax.ShapeDtypeStruct((ROWS, width), BF),) * 4
+        + (
+            jax.ShapeDtypeStruct((BACK,) + own.shape[1:], F32),
+            jax.ShapeDtypeStruct(own.shape[1:], BF),
+        ),
+        in_specs=[pl.BlockSpec(memory_space=pltpu.SMEM)]
+        + [vmem] * 5,
+        out_specs=(vmem,) * 6,
         scratch_shapes=[pltpu.VMEM((4 * ROWS, dims), BF)],
         compiler_params=pltpu.CompilerParams(vmem_limit_bytes=24 * 1024 * 1024),
         cost_estimate=pl.CostEstimate(
-            flops=8 * ROWS * n * width * dims, bytes_accessed=4 << 20, transcendentals=0
+            flops=8 * ROWS * width * dims, bytes_accessed=4 << 20, transcendentals=0
         ),
         name="project_query",
-    )(info, dq, other, *weights)
-
-
-def project_kernel(grad, *refs):
-    n = len(refs) - 5
-    out = refs[-1]
+    )(info, own, arrived, dq, other, weights)
+
+
+def project_kernel(grad, weights, *refs):
+    *terms, out = refs
+    n, _, width = out.shape
     for k in range(n):
-        width = refs[k].shape[0]
-        total = nt(grad[...], refs[k][...])
-        for term in refs[n : n + 4]:
-            total = total + term[:, k * width : (k + 1) * width].astype(F32)
+        at = slice(k * width, (k + 1) * width)
+        total = nt(grad[...], weights[at])
+        for term in terms:
+            total = total + term[:, at].astype(F32)
         out[k] = total.astype(BF)
 
 
-def project(grad, weights, terms):
+def project(grad, weights, terms, n):
     vmem = pl.BlockSpec(memory_space=pltpu.VMEM)
-    n, width, dims = len(weights), weights[0].shape[0], grad.shape[1]
+    width, dims = weights.shape
     return pl.pallas_call(
         project_kernel,
-        grid=(1,),
-        out_shape=jax.ShapeDtypeStruct((n, ROWS, width), BF),
-        in_specs=[vmem] + [pl.BlockSpec((width, dims), lambda i: (0, 0))] * n + [vmem] * 4,
+        out_shape=jax.ShapeDtypeStruct((n, ROWS, width // n), BF),
+        in_specs=[vmem] * (2 + len(terms)),
         out_specs=vmem,
         compiler_params=pltpu.CompilerParams(vmem_limit_bytes=24 * 1024 * 1024),
         cost_estimate=pl.CostEstimate(
-            flops=2 * n * ROWS * width * dims, bytes_accessed=8 << 20, transcendentals=0
+            flops=2 * ROWS * width * dims, bytes_accessed=8 << 20, transcendentals=0
         ),
         name="project_kv",
-    )(grad, *weights, *terms)
+    )(grad, weights, *terms)
 
 
 def assemble_kernel(where, mine, theirs, out):
     n, _, width = mine.shape
     for k in range(n):
-        piece = lax.rem(where[0] - k + n, n) * 2
-        near = pl.multiple_of((piece + where[1]) * width, width)
-        far = pl.multiple_of((piece + 1 - where[1]) * width, width)
+        near = pl.multiple_of((2 * k + where[0]) * width, width)
+        far = pl.multiple_of((2 * k + 1 - where[0]) * width, width)
         out[:, pl.ds(near, width)] = mine[k]
         out[:, pl.ds(far, width)] = theirs[k]
 
@@ -249,7 +257,6 @@
     dps = lax.axis_size("dp")
     server = lax.axis_index("server")
     core = lax.axis_index("section")
-    dp = lax.axis_index("dp")
     odd = server % 2
     both = ("server", "section")
 
@@ -283,8 +290,6 @@
     kv_first, kv_second = groups(key_rows[0], saved_value_rows[0])
     block = jnp.concatenate([swap(kv_first, 0), swap(kv_second, 1)], 0)
     blocks = [block]
-    for _ in range(BACK):
-        blocks.append(shift(blocks[-1], "server", 4))
 
     queries, out_grad, _ = lax.optimization_barrier((queries, out_grad, block))
     qg_first, qg_second = groups(queries[0], out_grad[0])
@@ -307,8 +312,15 @@
         ],
         1,
     )
-    early = {k: shift(wide if k != 2 else wide[:, 2 * half :], "dp", k) for k in range(1, dps)}
-
+    query_weight, kv_weight = [
+        lax.all_gather(w, "dp", axis=0, tiled=True)
+        for w in (wide[:, 2 * half :], wide[:, : 2 * half])
+    ]
+
+    for k in range(1, BACK + 1):
+        if k == BACK:
+            blocks[-1], qg0, qg1 = lax.optimization_barrier((blocks[-1], qg0, qg1))
+        blocks.append(shift(blocks[-1], "server", 4))
     low = jnp.stack(blocks[:BACK])
     high = jnp.stack(blocks[1:])
     other = flip(jnp.where(core == 0, low, high))
@@ -321,38 +333,29 @@
         ]
     )
     dq, own_part, other_part = attention(
-        info, qg0, qg1, blocks, other, [early[k] for k in early if k != 2]
-    )
-
-    arrived = flip(other_part)
-    zero = jnp.zeros_like(arrived[:1])
-    arrived = jnp.where(
-        core == 0,
-        jnp.concatenate([arrived, zero], 0),
-        jnp.concatenate([zero, arrived], 0),
-    )
-    totals = own_part + arrived.astype(F32)
-    held = totals[BACK].astype(BF)
-
-    early[0] = wide
-    late = dict(early)
-    late[2] = shift(wide[:, : 2 * half], "dp", 2)
-    early, late = [[w[k] for k in range(dps)] for w in (early, late)]
-
-    sent_products = project_query(info, dq, flip(dq), early)
+        info, qg0, qg1, blocks, other, []
+    )
+
+    *sent_products, totals, held = project_query(
+        info, own_part, flip(other_part), dq, flip(dq), query_weight
+    )
     products = [sent_products[0]]
     for k in range(1, 4):
         pairs_x = [(s, s // 4 * 4 + (s + k) % 4) for s in range(servers)]
         products.append(lax.ppermute(sent_products[k], "server", pairs_x))
 
     for k in range(BACK - 1, -1, -1):
+        if k == 1:
+            held, products[1], products[3] = lax.optimization_barrier(
+                (held, products[1], products[3])
+            )
         held = (totals[k] + shift(held, "server", -4).astype(F32)).astype(BF)
-    held, products = lax.optimization_barrier((held, products))
+    held, products[2] = lax.optimization_barrier((held, products[2]))
     kv_grad = jnp.concatenate([swap(held[:ROWS], 0), swap(held[ROWS:], 1)], 1)
     kv_grad = jnp.concatenate([kv_grad, flip(kv_grad)], 1)
-    mine = project(kv_grad, late, products)
+    mine = project(kv_grad, kv_weight, products, dps)
     theirs = flip(mine)
-    where = jnp.stack([dp, core]).astype(jnp.int32)
+    where = core.astype(jnp.int32)[None]
     return assemble(where, mine, theirs)[None]
 
 

time: 136 us -> 129 us (0.949)
  between operations: 0.44 us -> 13.7 us
  starting transfers between devices: 42.3 us -> 30.3 us
  waiting for transfers between devices: 64.4 us -> 58.7 us
  Pallas kernels: 20.6 us -> 16.5 us
  local copies, waits for them, and re-layouts: 2.31 us -> 4.4 us
    ppermute x12 -> x8, starting transfers between devices: 15.5 us -> 3.93 us  [shift(): return lax.ppermute(x, axis, [(i, (i + k) % n) for i in range(n)])]
    ppermute x3, waiting for transfers between devices: 18 us -> 12.8 us  [body(): products.append(lax.ppermute(sent_products[k], 'server', pairs_x))]
    ppermute x6, starting transfers between devices: 18.4 us -> 13.9 us  [swap(): return lax.ppermute(x, both, pairs[j])]
    ppermute x3, starting transfers between devices: 3.64 us -> 8.07 us  [body(): products.append(lax.ppermute(sent_products[k], 'server', pairs_x))]
    ppermute x6, waiting for transfers between devices: 5.13 us -> 8.94 us  [flip(): return lax.ppermute(x, 'section', [(0, 1), (1, 0)])]
    ppermute x12 -> x8, waiting for transfers between devices: 30.4 us -> 26.8 us  [shift(): return lax.ppermute(x, axis, [(i, (i + k) % n) for i in range(n)])]
    pallas_call x2, Pallas kernels: 6.1 us -> 3.69 us  [the longest x1 2.04 us: project_query(): pl.pallas_call(project_query_kernel, out_shape=(jax.ShapeDtypeStruct((ROW...]
    unnamed x35 -> x19, local copies, waits for them, and re-layouts: 1.95 us -> 4.05 us
  transfers between devices with their start and end apart: 27 -> 25, of which waited for: 18 -> 18; matrix products, arithmetic and copies ran while one was open for 2% -> 1% of each run, Pallas kernels for 2% -> 11%
where the time goes in v3:
time: 129 us; the launch traced here: 128 us
  waiting for transfers between devices  58.7 us (46%)
  starting transfers between devices  30.3 us (23%)
  Pallas kernels  16.5 us (13%)
  between operations  13.7 us (11%)
  other arithmetic  4.82 us (4%)
  local copies, waits for them, and re-layouts  4.4 us (3%)
    ppermute x8, waiting for transfers between devices, shift(): return lax.ppermute(x, axis, [(i, (i + k) % n) for i in range(n)])  26.8 us
    ppermute x6, starting transfers between devices, swap(): return lax.ppermute(x, both, pairs[j])  13.9 us
    ppermute x3, waiting for transfers between devices, body(): products.append(lax.ppermute(sent_products[k], 'server', pairs_x))  12.8 us
    pallas_call x1, Pallas kernels, attention(): pl.pallas_call(attention_kernel, out_shape=(jax.ShapeDtypeStruct((CHUNK,...  11.8 us
    ppermute x6, waiting for transfers between devices, swap(): return lax.ppermute(x, both, pairs[j])  10 us
    ppermute x6, waiting for transfers between devices, flip(): return lax.ppermute(x, 'section', [(0, 1), (1, 0)])  8.94 us
    ppermute x3, starting transfers between devices, body(): products.append(lax.ppermute(sent_products[k], 'server', pairs_x))  8.07 us
    ppermute x6, starting transfers between devices, flip(): return lax.ppermute(x, 'section', [(0, 1), (1, 0)])  4.34 us
  transfers between devices with their start and end apart: 25, of which 18 were waited for; matrix products, arithmetic and copies ran while one was open for 1% of the time, Pallas kernels for 11%

profile of v3, /device:TPU:1, one launch (start us, length us, event | category | flops | bytes accessed | tf_op | source)
XLA Modules:
  0.0 128.3 jit_solution(3887006077576039954)
XLA Ops:
  6.5 1.7 %slice_select_fusion = bf16[1024,512]{1,0:T(8,128)(2,1)S(1)} fusion(bf16[1024,1024]{1,0:T(8,128)(2,1)} %param.13, pred[]{:T(512)S(6)} %eq.10), kind=kLoop, calls=%fused_computation.2 | loop fusion | flops 524288 | bytes 3145729 | tf_op jit(solution)/shard_map/jit(_where)/select_n | solution.py:301
  9.3 3.3 %collective-permute-start.11 = (bf16[512,1024]{1,0:T(8,128)(2,1)S(1)}, bf16[512,1024]{1,0:T(8,128)(2,1)S(1)}, u32[]{:S(2)}, u32[]{:S(2)}) collective-permute-start(bf16[512,1024]{1,0:T(8,128)(2,1)S(1)} %get-tuple-element.44), channel_id=1, source_target_pairs={{0,4},{4,0},{1,5},{5,1},{2,6},{6,2},{3,7},{7,3},{8,12},{12,8},{9,1... | collective-permute-start | bytes 3145736 | tf_op jit(solution)/shard_map/ppermute | solution.py:282
  12.6 2.3 %collective-permute-done.11 = bf16[512,1024]{1,0:T(8,128)(2,1)S(1)} collective-permute-done((bf16[512,1024]{1,0:T(8,128)(2,1)S(1)}, bf16[512,1024]{1,0:T(8,128)(2,1)S(1)}, u32[]{:S(2)}, u32[]{:S(2)}) %collective-permute-start.11) | collective-permute-done | bytes 1048608 | tf_op jit(solution)/shard_map/ppermute | solution.py:282
  17.1 3.2 %collective-permute-start = (bf16[128,256]{1,0:T(8,128)(2,1)S(1)}, bf16[128,256]{1,0:T(8,128)(2,1)S(1)}, u32[]{:S(2)}, u32[]{:S(2)}) collective-permute-start(bf16[128,256]{1,0:T(8,128)(2,1)S(1)} %get-tuple-element.63), channel_id=1, source_target_pairs={{0,0},{4,16},{8,8},{12,24},{16,4},{20,20},{24,12},{28,28},{32,32},... | collective-permute-start | bytes 196616 | tf_op jit(solution)/shard_map/ppermute | solution.py:275
  21.3 2.9 %collective-permute-done = bf16[128,256]{1,0:T(8,128)(2,1)S(1)} collective-permute-done((bf16[128,256]{1,0:T(8,128)(2,1)S(1)}, bf16[128,256]{1,0:T(8,128)(2,1)S(1)}, u32[]{:S(2)}, u32[]{:S(2)}) %collective-permute-start) | collective-permute-done | bytes 65568 | tf_op jit(solution)/shard_map/ppermute | solution.py:275
  25.3 1.6 %collective-permute-start.2 = (bf16[256,256]{1,0:T(8,128)(2,1)S(1)}, bf16[256,256]{1,0:T(8,128)(2,1)S(1)}, u32[]{:S(2)}, u32[]{:S(2)}) collective-permute-start(bf16[256,256]{1,0:T(8,128)(2,1)S(1)} %constant_dynamic-update-slice_fusion.refs_0_), channel_id=1, source_target_pairs={{0,32},{8,40},{16,48},{24,56},{32,64},{40,72},{48,80},{56,88},{64,... | collective-permute-start | bytes 393224 | tf_op jit(solution)/shard_map/ppermute | solution.py:279
  27.1 2.5 %collective-permute-start.5 = (bf16[128,1024]{1,0:T(8,128)(2,1)S(1)}, bf16[128,1024]{1,0:T(8,128)(2,1)S(1)}, u32[]{:S(2)}, u32[]{:S(2)}) collective-permute-start(bf16[128,1024]{1,0:T(8,128)(2,1)S(1)} %get-tuple-element.55), channel_id=1, source_target_pairs={{0,0},{4,16},{8,8},{12,24},{16,4},{20,20},{24,12},{28,28},{32,32},... | collective-permute-start | bytes 786440 | tf_op jit(solution)/shard_map/ppermute | solution.py:275
  29.6 1.3 %collective-permute-start.6 = (bf16[128,1024]{1,0:T(8,128)(2,1)S(1)}, bf16[128,1024]{1,0:T(8,128)(2,1)S(1)}, u32[]{:S(2)}, u32[]{:S(2)}) collective-permute-start(bf16[128,1024]{1,0:T(8,128)(2,1)S(1)} %get-tuple-element.54), channel_id=1, source_target_pairs={{0,8},{4,24},{8,0},{12,16},{16,12},{20,28},{24,4},{28,20},{32,40},... | collective-permute-start | bytes 786440 | tf_op jit(solution)/shard_map/ppermute | solution.py:275
  30.9 2.4 %collective-permute-done.2.refs_1_ = bf16[256,256]{1,0:T(8,128)(2,1)S(1)} collective-permute-done((bf16[256,256]{1,0:T(8,128)(2,1)S(1)}, bf16[256,256]{1,0:T(8,128)(2,1)S(1)}, u32[]{:S(2)}, u32[]{:S(2)}) %collective-permute-start.2) | collective-permute-done | bytes 131104 | tf_op jit(solution)/shard_map/ppermute | solution.py:279
  33.2 5.4 %collective-permute-done.3.refs_2_ = bf16[256,256]{1,0:T(8,128)(2,1)S(1)} collective-permute-done((bf16[256,256]{1,0:T(8,128)(2,1)S(1)}, bf16[256,256]{1,0:T(8,128)(2,1)S(1)}, u32[]{:S(2)}, u32[]{:S(2)}) %collective-permute-start.3) | collective-permute-done | bytes 131104 | tf_op jit(solution)/shard_map/ppermute | solution.py:279
  39.5 4.6 %collective-permute-done.4.refs_3_ = bf16[256,256]{1,0:T(8,128)(2,1)S(1)} collective-permute-done((bf16[256,256]{1,0:T(8,128)(2,1)S(1)}, bf16[256,256]{1,0:T(8,128)(2,1)S(1)}, u32[]{:S(2)}, u32[]{:S(2)}) %collective-permute-start.4) | collective-permute-done | bytes 131104 | tf_op jit(solution)/shard_map/ppermute | solution.py:279
  44.1 5.4 %collective-permute-done.7.refs_4_ = bf16[256,256]{1,0:T(8,128)(2,1)S(1)} collective-permute-done((bf16[256,256]{1,0:T(8,128)(2,1)S(1)}, bf16[256,256]{1,0:T(8,128)(2,1)S(1)}, u32[]{:S(2)}, u32[]{:S(2)}) %collective-permute-start.7) | collective-permute-done | bytes 131104 | tf_op jit(solution)/shard_map/ppermute | solution.py:279
  49.9 1.8 %collective-permute-done.8.refs_5_ = bf16[4,256,256]{2,1,0:T(8,128)(2,1)S(1)} collective-permute-done((bf16[4,256,256]{2,1,0:T(8,128)(2,1)S(1)}, bf16[4,256,256]{2,1,0:T(8,128)(2,1)S(1)}, u32[]{:S(2)}, u32[]{:S(2)}) %collective-permute-start.8) | collective-permute-done | bytes 524320 | tf_op jit(solution)/shard_map/ppermute | solution.py:282
  51.6 11.8 %attention_grads.1 = (bf16[256,512]{1,0:T(8,128)(2,1)S(1)}, f32[5,256,256]{2,1,0:T(8,128)S(1)}, bf16[4,256,256]{2,1,0:T(8,128)(2,1)S(1)}) custom-call(s32[16]{0:T(128)S(1)} %concatenate.37.info, bf16[128,1024]{1,0:T(8,128)(2,1)S(1)} %collective-permute-done.5.qg0, bf16[128,1024]{1,0:T(8,128)(2,1)S(1)} %collective-permute-done.6.qg1, ...), custom_call_target="tpu_custom_call" | custom-call | flops 3019898880 | bytes 8388608 | tf_op jit(solution)/shard_map/attention_grads/pallas_call | solution.py:132
  64.0 1.8 %collective-permute-done.10.other = bf16[256,512]{1,0:T(8,128)(2,1)S(1)} collective-permute-done((bf16[256,512]{1,0:T(8,128)(2,1)S(1)}, bf16[256,512]{1,0:T(8,128)(2,1)S(1)}, u32[]{:S(2)}, u32[]{:S(2)}) %collective-permute-start.10) | collective-permute-done | bytes 262176 | tf_op jit(solution)/shard_map/ppermute | solution.py:282
  65.8 1.8 %copy-done.1 = bf16[2048,512]{1,0:T(8,128)(2,1)S(1)} copy-done((bf16[2048,512]{1,0:T(8,128)(2,1)S(1)}, bf16[2048,512]{1,0:T(8,128)(2,1)}, u32[]{:S(2)}) %copy-start.1) | copy-done | bytes 2097176
  67.5 2.0 %project_query.1 = (bf16[128,2048]{1,0:T(8,128)(2,1)S(1)}, bf16[128,2048]{1,0:T(8,128)(2,1)S(1)}, bf16[128,2048]{1,0:T(8,128)(2,1)S(1)}, bf16[128,2048]{1,0:T(8,...) custom-call(s32[16]{0:T(128)S(1)} %concatenate.37.info, ...), custom_call_target="tpu_custom_call" | custom-call | flops 1073741824 | bytes 4194304 | tf_op jit(solution)/shard_map/project_query/pallas_call | solution.py:187
  70.9 4.9 %collective-permute-start.15 = (bf16[128,2048]{1,0:T(8,128)(2,1)S(1)}, bf16[128,2048]{1,0:T(8,128)(2,1)S(1)}, u32[]{:S(2)}, u32[]{:S(2)}) collective-permute-start(bf16[128,2048]{1,0:T(8,128)(2,1)S(1)} %get-tuple-element.35), channel_id=1, source_target_pairs={{0,24},{8,0},{16,8},{24,16},{32,56},{40,32},{48,40},{56,48},{64,88... | collective-permute-start | bytes 1572872 | tf_op jit(solution)/shard_map/ppermute | solution.py:345
  76.4 4.0 %collective-permute-done.13 = bf16[256,256]{1,0:T(8,128)(2,1)S(1)} collective-permute-done((bf16[256,256]{1,0:T(8,128)(2,1)S(1)}, bf16[256,256]{1,0:T(8,128)(2,1)S(1)}, u32[]{:S(2)}, u32[]{:S(2)}) %collective-permute-start.13) | collective-permute-done | bytes 131104 | tf_op jit(solution)/shard_map/ppermute | solution.py:279
  80.4 7.4 %collective-permute-done.14.refs_1_ = bf16[128,2048]{1,0:T(8,128)(2,1)S(1)} collective-permute-done((bf16[128,2048]{1,0:T(8,128)(2,1)S(1)}, bf16[128,2048]{1,0:T(8,128)(2,1)S(1)}, u32[]{:S(2)}, u32[]{:S(2)}) %collective-permute-start.14) | collective-permute-done | bytes 524320 | tf_op jit(solution)/shard_map/ppermute | solution.py:345
  87.8 2.0 %collective-permute-start.18 = (bf16[128,2048]{1,0:T(8,128)(2,1)S(1)}, bf16[128,2048]{1,0:T(8,128)(2,1)S(1)}, u32[]{:S(2)}, u32[]{:S(2)}) collective-permute-start(bf16[128,2048]{1,0:T(8,128)(2,1)S(1)} %get-tuple-element.37), channel_id=1, source_target_pairs={{0,16},{8,24},{16,0},{24,8},{32,48},{40,56},{48,32},{56,40},{64,80... | collective-permute-start | bytes 1572872 | tf_op jit(solution)/shard_map/ppermute | solution.py:345
  89.8 2.3 %collective-permute-done.16 = bf16[256,256]{1,0:T(8,128)(2,1)S(1)} collective-permute-done((bf16[256,256]{1,0:T(8,128)(2,1)S(1)}, bf16[256,256]{1,0:T(8,128)(2,1)S(1)}, u32[]{:S(2)}, u32[]{:S(2)}) %collective-permute-start.16) | collective-permute-done | bytes 131104 | tf_op jit(solution)/shard_map/ppermute | solution.py:279
  92.1 1.6 %collective-permute-start.17 = (bf16[256,256]{1,0:T(8,128)(2,1)S(1)}, bf16[256,256]{1,0:T(8,128)(2,1)S(1)}, u32[]{:S(2)}, u32[]{:S(2)}) collective-permute-start(bf16[256,256]{1,0:T(8,128)(2,1)S(1)} %fusion.2), channel_id=1, source_target_pairs={{0,224},{8,232},{16,240},{24,248},{32,0},{40,8},{48,16},{56,24},{6... | collective-permute-start | bytes 393224 | tf_op jit(solution)/shard_map/ppermute | solution.py:279
  93.8 2.7 %collective-permute-done.17 = bf16[256,256]{1,0:T(8,128)(2,1)S(1)} collective-permute-done((bf16[256,256]{1,0:T(8,128)(2,1)S(1)}, bf16[256,256]{1,0:T(8,128)(2,1)S(1)}, u32[]{:S(2)}, u32[]{:S(2)}) %collective-permute-start.17) | collective-permute-done | bytes 131104 | tf_op jit(solution)/shard_map/ppermute | solution.py:279
  96.5 5.5 %collective-permute-done.18.refs_2_ = bf16[128,2048]{1,0:T(8,128)(2,1)S(1)} collective-permute-done((bf16[128,2048]{1,0:T(8,128)(2,1)S(1)}, bf16[128,2048]{1,0:T(8,128)(2,1)S(1)}, u32[]{:S(2)}, u32[]{:S(2)}) %collective-permute-start.18) | collective-permute-done | bytes 524320 | tf_op jit(solution)/shard_map/ppermute | solution.py:345
  102.0 4.1 %collective-permute-start.20 = (bf16[128,256]{1,0:T(8,128)(2,1)S(1)}, bf16[128,256]{1,0:T(8,128)(2,1)S(1)}, u32[]{:S(2)}, u32[]{:S(2)}) collective-permute-start(bf16[128,256]{1,0:T(8,128)(2,1)S(1)} %get-tuple-element.61), channel_id=1, source_target_pairs={{0,8},{4,24},{8,0},{12,16},{16,12},{20,28},{24,4},{28,20},{32,40},... | collective-permute-start | bytes 196616 | tf_op jit(solution)/shard_map/ppermute | solution.py:275
  106.0 1.9 %collective-permute-start.19 = (bf16[128,256]{1,0:T(8,128)(2,1)S(1)}, bf16[128,256]{1,0:T(8,128)(2,1)S(1)}, u32[]{:S(2)}, u32[]{:S(2)}) collective-permute-start(bf16[128,256]{1,0:T(8,128)(2,1)S(1)} %get-tuple-element.60), channel_id=1, source_target_pairs={{0,0},{4,16},{8,8},{12,24},{16,4},{20,20},{24,12},{28,28},{32,32},... | collective-permute-start | bytes 196616 | tf_op jit(solution)/shard_map/ppermute | solution.py:275
  108.0 5.1 %collective-permute-done.19 = bf16[128,256]{1,0:T(8,128)(2,1)S(1)} collective-permute-done((bf16[128,256]{1,0:T(8,128)(2,1)S(1)}, bf16[128,256]{1,0:T(8,128)(2,1)S(1)}, u32[]{:S(2)}, u32[]{:S(2)}) %collective-permute-start.19) | collective-permute-done | bytes 65568 | tf_op jit(solution)/shard_map/ppermute | solution.py:275
  113.2 1.3 %collective-permute-done.21 = bf16[128,512]{1,0:T(8,128)(2,1)S(1)} collective-permute-done((bf16[128,512]{1,0:T(8,128)(2,1)S(1)}, bf16[128,512]{1,0:T(8,128)(2,1)S(1)}, u32[]{:S(2)}, u32[]{:S(2)}) %collective-permute-start.21) | collective-permute-done | bytes 131104 | tf_op jit(solution)/shard_map/ppermute | solution.py:282
  114.6 2.2 %copy-done = bf16[2048,1024]{1,0:T(8,128)(2,1)S(1)} copy-done((bf16[2048,1024]{1,0:T(8,128)(2,1)S(1)}, bf16[2048,1024]{1,0:T(8,128)(2,1)}, u32[]{:S(2)}) %copy-start) | copy-done | bytes 4194328
  116.8 1.6 %project_kv.1.mine = bf16[4,128,512]{2,1,0:T(8,128)(2,1)S(1)} custom-call(bf16[128,1024]{1,0:T(8,128)(2,1)S(1)} %pad_maximum_fusion.6.grad, bf16[2048,1024]{1,0:T(8,128)(2,1)S(1)} %copy-done, bf16[128,2048]{1,0:T(8,128)(2,1)S(1)} %get-tuple-element.39.refs_0_, bf16[128,2048]{1,0:T(8,128)(2,1)S(1)} %collective-permute-done.14.refs_1_, ...), custom_call_target="tpu_custom_call" | custom-call | flops 536870912 | bytes 8388608 | tf_op jit(solution)/shard_map/project_kv/pallas_call | solution.py:220
  118.7 1.8 %collective-permute-done.22.theirs = bf16[4,128,512]{2,1,0:T(8,128)(2,1)S(1)} collective-permute-done((bf16[4,128,512]{2,1,0:T(8,128)(2,1)S(1)}, bf16[4,128,512]{2,1,0:T(8,128)(2,1)S(1)}, u32[]{:S(2)}, u32[]{:S(2)}) %collective-permute-start.22) | collective-permute-done | bytes 524320 | tf_op jit(solution)/shard_map/ppermute | solution.py:282
  (66 shorter events, 10.5 us)
Async XLA Ops:
  6.5 1.8 %copy-start.2 = (bf16[1024,256]{1,0:T(8,128)(2,1)S(1)}, bf16[1024,256]{1,0:T(8,128)(2,1)}, u32[]{:S(2)}) copy-start(bf16[1024,256]{1,0:T(8,128)(2,1)} %param.14) | copy-start | bytes 1572868
  6.5 1.8 %copy-start.3 = (bf16[1024,256]{1,0:T(8,128)(2,1)S(1)}, bf16[1024,256]{1,0:T(8,128)(2,1)}, u32[]{:S(2)}) copy-start(bf16[1024,256]{1,0:T(8,128)(2,1)} %param.15) | copy-start | bytes 1572868
  6.5 59.2 %all-gather.3.cloned.1.call-start = ((), (), s32[]{:S(2)}) async-start(), calls=%async_computation | async-start | bytes 2621440 | tf_op jit(solution)/shard_map/all_gather | solution.py:316
  9.3 5.6 %collective-permute-start.11 = (bf16[512,1024]{1,0:T(8,128)(2,1)S(1)}, bf16[512,1024]{1,0:T(8,128)(2,1)S(1)}, u32[]{:S(2)}, u32[]{:S(2)}) collective-permute-start(bf16[512,1024]{1,0:T(8,128)(2,1)S(1)} %get-tuple-element.44), channel_id=1, source_target_pairs={{0,4},{4,0},{1,5},{5,1},{2,6},{6,2},{3,7},{7,3},{8,12},{12,8},{9,1... | collective-permute-start | bytes 3145736 | tf_op jit(solution)/shard_map/ppermute | solution.py:282
  15.8 11.1 %copy-start.4 = (bf16[1,128,1024]{2,1,0:T(8,128)(2,1)S(1)}, bf16[1,128,1024]{2,1,0:T(8,128)(2,1)}, u32[]{:S(2)}) copy-start(bf16[1,128,1024]{2,1,0:T(8,128)(2,1)} %param.11) | copy-start | bytes 786436
  15.8 98.8 %all-gather.5.cloned.1.call-start = ((), (), s32[]{:S(2)}) async-start(), calls=%async_computation.1 | async-start | bytes 5242880 | tf_op jit(solution)/shard_map/all_gather | solution.py:316
  15.9 11.1 %copy-start.5 = (bf16[1,128,1024]{2,1,0:T(8,128)(2,1)S(1)}, bf16[1,128,1024]{2,1,0:T(8,128)(2,1)}, u32[]{:S(2)}) copy-start(bf16[1,128,1024]{2,1,0:T(8,128)(2,1)} %param.8) | copy-start | bytes 786436
  17.0 32.7 %copy-start.8 = (s32[1,8]{1,0:T(1,128)S(1)}, s32[1,8]{1,0:T(1,128)}, u32[]{:S(2)}) copy-start(s32[1,8]{1,0:T(1,128)} %param.12) | copy-start | bytes 100
  17.1 7.1 %collective-permute-start = (bf16[128,256]{1,0:T(8,128)(2,1)S(1)}, bf16[128,256]{1,0:T(8,128)(2,1)S(1)}, u32[]{:S(2)}, u32[]{:S(2)}) collective-permute-start(bf16[128,256]{1,0:T(8,128)(2,1)S(1)} %get-tuple-element.63), channel_id=1, source_target_pairs={{0,0},{4,16},{8,8},{12,24},{16,4},{20,20},{24,12},{28,28},{32,32},... | collective-permute-start | bytes 196616 | tf_op jit(solution)/shard_map/ppermute | solution.py:275
  20.3 5.0 %collective-permute-start.1 = (bf16[128,256]{1,0:T(8,128)(2,1)S(1)}, bf16[128,256]{1,0:T(8,128)(2,1)S(1)}, u32[]{:S(2)}, u32[]{:S(2)}) collective-permute-start(bf16[128,256]{1,0:T(8,128)(2,1)S(1)} %get-tuple-element.62), channel_id=1, source_target_pairs={{0,8},{4,24},{8,0},{12,16},{16,12},{20,28},{24,4},{28,20},{32,40},... | collective-permute-start | bytes 196616 | tf_op jit(solution)/shard_map/ppermute | solution.py:275
  25.3 7.9 %collective-permute-start.2 = (bf16[256,256]{1,0:T(8,128)(2,1)S(1)}, bf16[256,256]{1,0:T(8,128)(2,1)S(1)}, u32[]{:S(2)}, u32[]{:S(2)}) collective-permute-start(bf16[256,256]{1,0:T(8,128)(2,1)S(1)} %constant_dynamic-update-slice_fusion.refs_0_), channel_id=1, source_target_pairs={{0,32},{8,40},{16,48},{24,56},{32,64},{40,72},{48,80},{56,88},{64,... | collective-permute-start | bytes 393224 | tf_op jit(solution)/shard_map/ppermute | solution.py:279
  27.1 11.6 %collective-permute-start.5 = (bf16[128,1024]{1,0:T(8,128)(2,1)S(1)}, bf16[128,1024]{1,0:T(8,128)(2,1)S(1)}, u32[]{:S(2)}, u32[]{:S(2)}) collective-permute-start(bf16[128,1024]{1,0:T(8,128)(2,1)S(1)} %get-tuple-element.55), channel_id=1, source_target_pairs={{0,0},{4,16},{8,8},{12,24},{16,4},{20,20},{24,12},{28,28},{32,32},... | collective-permute-start | bytes 786440 | tf_op jit(solution)/shard_map/ppermute | solution.py:275
  29.6 9.9 %collective-permute-start.6 = (bf16[128,1024]{1,0:T(8,128)(2,1)S(1)}, bf16[128,1024]{1,0:T(8,128)(2,1)S(1)}, u32[]{:S(2)}, u32[]{:S(2)}) collective-permute-start(bf16[128,1024]{1,0:T(8,128)(2,1)S(1)} %get-tuple-element.54), channel_id=1, source_target_pairs={{0,8},{4,24},{8,0},{12,16},{16,12},{20,28},{24,4},{28,20},{32,40},... | collective-permute-start | bytes 786440 | tf_op jit(solution)/shard_map/ppermute | solution.py:275
  33.2 5.4 %collective-permute-start.3 = (bf16[256,256]{1,0:T(8,128)(2,1)S(1)}, bf16[256,256]{1,0:T(8,128)(2,1)S(1)}, u32[]{:S(2)}, u32[]{:S(2)}) collective-permute-start(bf16[256,256]{1,0:T(8,128)(2,1)S(1)} %collective-permute-done.2.refs_1_), channel_id=1, source_target_pairs={{0,32},{8,40},{16,48},{24,56},{32,64},{40,72},{48,80},{56,88},{64,... | collective-permute-start | bytes 393224 | tf_op jit(solution)/shard_map/ppermute | solution.py:279
  38.7 5.4 %collective-permute-start.4 = (bf16[256,256]{1,0:T(8,128)(2,1)S(1)}, bf16[256,256]{1,0:T(8,128)(2,1)S(1)}, u32[]{:S(2)}, u32[]{:S(2)}) collective-permute-start(bf16[256,256]{1,0:T(8,128)(2,1)S(1)} %collective-permute-done.3.refs_2_), channel_id=1, source_target_pairs={{0,32},{8,40},{16,48},{24,56},{32,64},{40,72},{48,80},{56,88},{64,... | collective-permute-start | bytes 393224 | tf_op jit(solution)/shard_map/ppermute | solution.py:279
  44.1 5.4 %collective-permute-start.7 = (bf16[256,256]{1,0:T(8,128)(2,1)S(1)}, bf16[256,256]{1,0:T(8,128)(2,1)S(1)}, u32[]{:S(2)}, u32[]{:S(2)}) collective-permute-start(bf16[256,256]{1,0:T(8,128)(2,1)S(1)} %collective-permute-done.4.refs_3_), channel_id=1, source_target_pairs={{0,32},{8,40},{16,48},{24,56},{32,64},{40,72},{48,80},{56,88},{64,... | collective-permute-start | bytes 393224 | tf_op jit(solution)/shard_map/ppermute | solution.py:279
  49.6 2.0 %collective-permute-start.8 = (bf16[4,256,256]{2,1,0:T(8,128)(2,1)S(1)}, bf16[4,256,256]{2,1,0:T(8,128)(2,1)S(1)}, u32[]{:S(2)}, u32[]{:S(2)}) collective-permute-start(bf16[4,256,256]{2,1,0:T(8,128)(2,1)S(1)} %maximum_select_fusion), channel_id=1, source_target_pairs={{0,4},{4,0},{1,5},{5,1},{2,6},{6,2},{3,7},{7,3},{8,12},{12,8},{9,1... | collective-permute-start | bytes 1572872 | tf_op jit(solution)/shard_map/ppermute | solution.py:282
  63.4 2.4 %collective-permute-start.9 = (bf16[4,256,256]{2,1,0:T(8,128)(2,1)S(1)}, bf16[4,256,256]{2,1,0:T(8,128)(2,1)S(1)}, u32[]{:S(2)}, u32[]{:S(2)}) collective-permute-start(bf16[4,256,256]{2,1,0:T(8,128)(2,1)S(1)} %get-tuple-element.30), channel_id=1, source_target_pairs={{0,4},{4,0},{1,5},{5,1},{2,6},{6,2},{3,7},{7,3},{8,12},{12,8},{9,1... | collective-permute-start | bytes 1572872 | tf_op jit(solution)/shard_map/ppermute | solution.py:282
  63.6 2.2 %collective-permute-start.10 = (bf16[256,512]{1,0:T(8,128)(2,1)S(1)}, bf16[256,512]{1,0:T(8,128)(2,1)S(1)}, u32[]{:S(2)}, u32[]{:S(2)}) collective-permute-start(bf16[256,512]{1,0:T(8,128)(2,1)S(1)} %get-tuple-element.31.dq), channel_id=1, source_target_pairs={{0,4},{4,0},{1,5},{5,1},{2,6},{6,2},{3,7},{7,3},{8,12},{12,8},{9,1... | collective-permute-start | bytes 786440 | tf_op jit(solution)/shard_map/ppermute | solution.py:282
  65.8 1.8 %copy-start.1 = (bf16[2048,512]{1,0:T(8,128)(2,1)S(1)}, bf16[2048,512]{1,0:T(8,128)(2,1)}, u32[]{:S(2)}) copy-start(bf16[2048,512]{1,0:T(8,128)(2,1)} %all-gather.3.cloned.1.call-done.refs_0_) | copy-start | bytes 6291460
  69.6 6.2 %collective-permute-start.12 = (bf16[256,256]{1,0:T(8,128)(2,1)S(1)}, bf16[256,256]{1,0:T(8,128)(2,1)S(1)}, u32[]{:S(2)}, u32[]{:S(2)}) collective-permute-start(bf16[256,256]{1,0:T(8,128)(2,1)S(1)} %get-tuple-element.33), channel_id=1, source_target_pairs={{0,224},{8,232},{16,240},{24,248},{32,0},{40,8},{48,16},{56,24},{6... | collective-permute-start | bytes 393224 | tf_op jit(solution)/shard_map/ppermute | solution.py:279
  69.7 18.1 %collective-permute-start.14 = (bf16[128,2048]{1,0:T(8,128)(2,1)S(1)}, bf16[128,2048]{1,0:T(8,128)(2,1)S(1)}, u32[]{:S(2)}, u32[]{:S(2)}) collective-permute-start(bf16[128,2048]{1,0:T(8,128)(2,1)S(1)} %get-tuple-element.34), channel_id=1, source_target_pairs={{0,8},{8,16},{16,24},{24,0},{32,40},{40,48},{48,56},{56,32},{64,72... | collective-permute-start | bytes 1572872 | tf_op jit(solution)/shard_map/ppermute | solution.py:345
  70.9 16.9 %collective-permute-start.15 = (bf16[128,2048]{1,0:T(8,128)(2,1)S(1)}, bf16[128,2048]{1,0:T(8,128)(2,1)S(1)}, u32[]{:S(2)}, u32[]{:S(2)}) collective-permute-start(bf16[128,2048]{1,0:T(8,128)(2,1)S(1)} %get-tuple-element.35), channel_id=1, source_target_pairs={{0,24},{8,0},{16,8},{24,16},{32,56},{40,32},{48,40},{56,48},{64,88... | collective-permute-start | bytes 1572872 | tf_op jit(solution)/shard_map/ppermute | solution.py:345
  75.8 4.6 %collective-permute-start.13 = (bf16[256,256]{1,0:T(8,128)(2,1)S(1)}, bf16[256,256]{1,0:T(8,128)(2,1)S(1)}, u32[]{:S(2)}, u32[]{:S(2)}) collective-permute-start(bf16[256,256]{1,0:T(8,128)(2,1)S(1)} %fusion), channel_id=1, source_target_pairs={{0,224},{8,232},{16,240},{24,248},{32,0},{40,8},{48,16},{56,24},{6... | collective-permute-start | bytes 393224 | tf_op jit(solution)/shard_map/ppermute | solution.py:279
  87.8 4.3 %collective-permute-start.16 = (bf16[256,256]{1,0:T(8,128)(2,1)S(1)}, bf16[256,256]{1,0:T(8,128)(2,1)S(1)}, u32[]{:S(2)}, u32[]{:S(2)}) collective-permute-start(bf16[256,256]{1,0:T(8,128)(2,1)S(1)} %fusion.1), channel_id=1, source_target_pairs={{0,224},{8,232},{16,240},{24,248},{32,0},{40,8},{48,16},{56,24},{6... | collective-permute-start | bytes 393224 | tf_op jit(solution)/shard_map/ppermute | solution.py:279
  87.8 14.2 %collective-permute-start.18 = (bf16[128,2048]{1,0:T(8,128)(2,1)S(1)}, bf16[128,2048]{1,0:T(8,128)(2,1)S(1)}, u32[]{:S(2)}, u32[]{:S(2)}) collective-permute-start(bf16[128,2048]{1,0:T(8,128)(2,1)S(1)} %get-tuple-element.37), channel_id=1, source_target_pairs={{0,16},{8,24},{16,0},{24,8},{32,48},{40,56},{48,32},{56,40},{64,80... | collective-permute-start | bytes 1572872 | tf_op jit(solution)/shard_map/ppermute | solution.py:345
  92.1 4.3 %collective-permute-start.17 = (bf16[256,256]{1,0:T(8,128)(2,1)S(1)}, bf16[256,256]{1,0:T(8,128)(2,1)S(1)}, u32[]{:S(2)}, u32[]{:S(2)}) collective-permute-start(bf16[256,256]{1,0:T(8,128)(2,1)S(1)} %fusion.2), channel_id=1, source_target_pairs={{0,224},{8,232},{16,240},{24,248},{32,0},{40,8},{48,16},{56,24},{6... | collective-permute-start | bytes 393224 | tf_op jit(solution)/shard_map/ppermute | solution.py:279
  102.0 6.0 %collective-permute-start.20 = (bf16[128,256]{1,0:T(8,128)(2,1)S(1)}, bf16[128,256]{1,0:T(8,128)(2,1)S(1)}, u32[]{:S(2)}, u32[]{:S(2)}) collective-permute-start(bf16[128,256]{1,0:T(8,128)(2,1)S(1)} %get-tuple-element.61), channel_id=1, source_target_pairs={{0,8},{4,24},{8,0},{12,16},{16,12},{20,28},{24,4},{28,20},{32,40},... | collective-permute-start | bytes 196616 | tf_op jit(solution)/shard_map/ppermute | solution.py:275
  106.0 7.1 %collective-permute-start.19 = (bf16[128,256]{1,0:T(8,128)(2,1)S(1)}, bf16[128,256]{1,0:T(8,128)(2,1)S(1)}, u32[]{:S(2)}, u32[]{:S(2)}) collective-permute-start(bf16[128,256]{1,0:T(8,128)(2,1)S(1)} %get-tuple-element.60), channel_id=1, source_target_pairs={{0,0},{4,16},{8,8},{12,24},{16,4},{20,20},{24,12},{28,28},{32,32},... | collective-permute-start | bytes 196616 | tf_op jit(solution)/shard_map/ppermute | solution.py:275
  113.1 1.4 %collective-permute-start.21 = (bf16[128,512]{1,0:T(8,128)(2,1)S(1)}, bf16[128,512]{1,0:T(8,128)(2,1)S(1)}, u32[]{:S(2)}, u32[]{:S(2)}) collective-permute-start(bf16[128,512]{1,0:T(8,128)(2,1)S(1)} %pad_maximum_fusion.7), channel_id=1, source_target_pairs={{0,4},{4,0},{1,5},{5,1},{2,6},{6,2},{3,7},{7,3},{8,12},{12,8},{9,1... | collective-permute-start | bytes 393224 | tf_op jit(solution)/shard_map/ppermute | solution.py:282
  114.6 2.2 %copy-start = (bf16[2048,1024]{1,0:T(8,128)(2,1)S(1)}, bf16[2048,1024]{1,0:T(8,128)(2,1)}, u32[]{:S(2)}) copy-start(bf16[2048,1024]{1,0:T(8,128)(2,1)} %all-gather.5.cloned.1.call-done.weights) | copy-start | bytes 12582916
  118.5 2.0 %collective-permute-start.22 = (bf16[4,128,512]{2,1,0:T(8,128)(2,1)S(1)}, bf16[4,128,512]{2,1,0:T(8,128)(2,1)S(1)}, u32[]{:S(2)}, u32[]{:S(2)}) collective-permute-start(bf16[4,128,512]{2,1,0:T(8,128)(2,1)S(1)} %project_kv.1.mine), channel_id=1, source_target_pairs={{0,4},{4,0},{1,5},{5,1},{2,6},{6,2},{3,7},{7,3},{8,12},{12,8},{9,1... | collective-permute-start | bytes 1572872 | tf_op jit(solution)/shard_map/ppermute | solution.py:282
  (2 other events, 2.5 us)
Sparse Core Ops, SparseCore 0:
  15.9 34.3 all-gather.2
  52.1 50.8 all-gather.4

commit v4 on v3

--- a/solution.py
+++ b/solution.py
@@ -304,23 +304,19 @@
     mine = jnp.where(core == 0, weight[:half], weight[half:])
     theirs = flip(jnp.where(core == 0, weight[half:], weight[:half]))
     half = 2 * kw_first.shape[1]
-    wide = jnp.concatenate(
-        [
-            mine[:, :half],
-            theirs[:, :half],
-            jnp.where(core == (server % 4) // 2, mine[:, half:], theirs[:, half:]),
-        ],
-        1,
-    )
-    query_weight, kv_weight = [
-        lax.all_gather(w, "dp", axis=0, tiled=True)
-        for w in (wide[:, 2 * half :], wide[:, : 2 * half])
-    ]
-
+    after, _ = lax.optimization_barrier((core, block))
+    query_weight = jnp.where(after == (server % 4) // 2, mine[:, half:], theirs[:, half:])
+    query_weight = lax.all_gather(query_weight, "dp", axis=0, tiled=True)
     for k in range(1, BACK + 1):
         if k == BACK:
             blocks[-1], qg0, qg1 = lax.optimization_barrier((blocks[-1], qg0, qg1))
         blocks.append(shift(blocks[-1], "server", 4))
+    after, _ = lax.optimization_barrier((core, blocks[1]))
+    kv_weight = jnp.concatenate(
+        [mine[:, :half], jnp.where(after >= 0, theirs[:, :half], mine[:, :half])], 1
+    )
+    kv_weight = lax.all_gather(kv_weight, "dp", axis=0, tiled=True)
+
     low = jnp.stack(blocks[:BACK])
     high = jnp.stack(blocks[1:])
     other = flip(jnp.where(core == 0, low, high))

time: 129 us -> 130 us (level)
    ppermute x6, waiting for transfers between devices: 10 us -> 12.7 us  [swap(): return lax.ppermute(x, both, pairs[j])]
    ppermute x6, waiting for transfers between devices: 8.94 us -> 6.49 us  [flip(): return lax.ppermute(x, 'section', [(0, 1), (1, 0)])]
    select_n x0 -> x1, other arithmetic: none -> 2.1 us  [body(): jnp.where(after >= 0, theirs[:, :half], mine[:, :half])]
  transfers between devices with their start and end apart: 25 -> 25, of which waited for: 18 -> 19; matrix products, arithmetic and copies ran while one was open for 1% -> 1% of each run, Pallas kernels for 11% -> 11%
where the time goes in v4:
time: 130 us
  waiting for transfers between devices  59.4 us (46%)
  starting transfers between devices  30.3 us (23%)
  Pallas kernels  16.5 us (13%)
  between operations  13.7 us (11%)
  other arithmetic  6.02 us (5%)
  local copies, waits for them, and re-layouts  4.23 us (3%)
    ppermute x8, waiting for transfers between devices, shift(): return lax.ppermute(x, axis, [(i, (i + k) % n) for i in range(n)])  27.3 us
    ppermute x6, starting transfers between devices, swap(): return lax.ppermute(x, both, pairs[j])  13.9 us
    ppermute x3, waiting for transfers between devices, body(): products.append(lax.ppermute(sent_products[k], 'server', pairs_x))  12.9 us
    ppermute x6, waiting for transfers between devices, swap(): return lax.ppermute(x, both, pairs[j])  12.7 us
    pallas_call x1, Pallas kernels, attention(): pl.pallas_call(attention_kernel, out_shape=(jax.ShapeDtypeStruct((CHUNK,...  11.8 us
    ppermute x3, starting transfers between devices, body(): products.append(lax.ppermute(sent_products[k], 'server', pairs_x))  7.67 us
    ppermute x6, waiting for transfers between devices, flip(): return lax.ppermute(x, 'section', [(0, 1), (1, 0)])  6.49 us
    ppermute x6, starting transfers between devices, flip(): return lax.ppermute(x, 'section', [(0, 1), (1, 0)])  4.5 us
  transfers between devices with their start and end apart: 25, of which 19 were waited for; matrix products, arithmetic and copies ran while one was open for 1% of the time, Pallas kernels for 11%

profile of v4, /device:TPU:1, one launch (start us, length us, event | category | flops | bytes accessed | tf_op | source)
XLA Modules:
  0.0 130.1 jit_solution(11384697483472932841)
XLA Ops:
  6.5 1.7 %slice_select_fusion = bf16[1024,512]{1,0:T(8,128)(2,1)S(1)} fusion(bf16[1024,1024]{1,0:T(8,128)(2,1)} %param.13, pred[]{:T(512)S(6)} %eq.10), kind=kLoop, calls=%fused_computation.2 | loop fusion | flops 524288 | bytes 3145729 | tf_op jit(solution)/shard_map/jit(_where)/select_n | solution.py:301
  9.3 3.3 %collective-permute-start.11 = (bf16[512,1024]{1,0:T(8,128)(2,1)S(1)}, bf16[512,1024]{1,0:T(8,128)(2,1)}, u32[]{:S(2)}, u32[]{:S(2)}) collective-permute-start(bf16[512,1024]{1,0:T(8,128)(2,1)S(1)} %get-tuple-element.50), channel_id=1, source_target_pairs={{0,4},{4,0},{1,5},{5,1},{2,6},{6,2},{3,7},{7,3},{8,12},{12,8},{9,1... | collective-permute-start | bytes 3145736 | tf_op jit(solution)/shard_map/ppermute | solution.py:282
  12.7 3.4 %collective-permute-start = (bf16[128,256]{1,0:T(8,128)(2,1)S(1)}, bf16[128,256]{1,0:T(8,128)(2,1)S(1)}, u32[]{:S(2)}, u32[]{:S(2)}) collective-permute-start(bf16[128,256]{1,0:T(8,128)(2,1)S(1)} %get-tuple-element.67), channel_id=1, source_target_pairs={{0,0},{4,16},{8,8},{12,24},{16,4},{20,20},{24,12},{28,28},{32,32},... | collective-permute-start | bytes 196616 | tf_op jit(solution)/shard_map/ppermute | solution.py:275
  16.8 2.9 %collective-permute-done = bf16[128,256]{1,0:T(8,128)(2,1)S(1)} collective-permute-done((bf16[128,256]{1,0:T(8,128)(2,1)S(1)}, bf16[128,256]{1,0:T(8,128)(2,1)S(1)}, u32[]{:S(2)}, u32[]{:S(2)}) %collective-permute-start) | collective-permute-done | bytes 65568 | tf_op jit(solution)/shard_map/ppermute | solution.py:275
  21.1 1.6 %collective-permute-start.2 = (bf16[256,256]{1,0:T(8,128)(2,1)S(1)}, bf16[256,256]{1,0:T(8,128)(2,1)S(1)}, u32[]{:S(2)}, u32[]{:S(2)}) collective-permute-start(bf16[256,256]{1,0:T(8,128)(2,1)S(1)} %constant_dynamic-update-slice_fusion.refs_0_), channel_id=1, source_target_pairs={{0,32},{8,40},{16,48},{24,56},{32,64},{40,72},{48,80},{56,88},{64,... | collective-permute-start | bytes 393224 | tf_op jit(solution)/shard_map/ppermute | solution.py:279
  22.7 6.3 %collective-permute-done.2.refs_1_ = bf16[256,256]{1,0:T(8,128)(2,1)S(1)} collective-permute-done((bf16[256,256]{1,0:T(8,128)(2,1)S(1)}, bf16[256,256]{1,0:T(8,128)(2,1)S(1)}, u32[]{:S(2)}, u32[]{:S(2)}) %collective-permute-start.2) | collective-permute-done | bytes 131104 | tf_op jit(solution)/shard_map/ppermute | solution.py:279
  29.0 2.1 %slice_select_fusion.1 = (bf16[512,512]{1,0:T(8,128)(2,1)S(1)}, bf16[512,512]{1,0:T(8,128)(2,1)}, bf16[512,512]{1,0:T(8,128)(2,1)S(1)}) fusion(bf16[512,1024]{1,0:T(8,128)(2,1)} %collective-permute-done.11, pred[]{:T(512)S(6)} %ge.3, bf16[512,1024]{1,0:T(8,128)(2,1)S(1)} %get-tuple-element.49, pred[]{:T(512)S(6)} %eq.12), kind=kLoop, calls=%fused_computation.5 | loop fusion | flops 524288 | bytes 3670018 | tf_op jit(solution)/shard_map/jit(_where)/select_n | solution.py:316
  32.5 3.1 %collective-permute-start.5 = (bf16[128,1024]{1,0:T(8,128)(2,1)S(1)}, bf16[128,1024]{1,0:T(8,128)(2,1)S(1)}, u32[]{:S(2)}, u32[]{:S(2)}) collective-permute-start(bf16[128,1024]{1,0:T(8,128)(2,1)S(1)} %get-tuple-element.59), channel_id=1, source_target_pairs={{0,0},{4,16},{8,8},{12,24},{16,4},{20,20},{24,12},{28,28},{32,32},... | collective-permute-start | bytes 786440 | tf_op jit(solution)/shard_map/ppermute | solution.py:275
  36.3 5.0 %collective-permute-done.3.refs_2_ = bf16[256,256]{1,0:T(8,128)(2,1)S(1)} collective-permute-done((bf16[256,256]{1,0:T(8,128)(2,1)S(1)}, bf16[256,256]{1,0:T(8,128)(2,1)S(1)}, u32[]{:S(2)}, u32[]{:S(2)}) %collective-permute-start.3) | collective-permute-done | bytes 131104 | tf_op jit(solution)/shard_map/ppermute | solution.py:279
  41.8 2.7 %collective-permute-done.6.qg1 = bf16[128,1024]{1,0:T(8,128)(2,1)S(1)} collective-permute-done((bf16[128,1024]{1,0:T(8,128)(2,1)S(1)}, bf16[128,1024]{1,0:T(8,128)(2,1)S(1)}, u32[]{:S(2)}, u32[]{:S(2)}) %collective-permute-start.6) | collective-permute-done | bytes 262176 | tf_op jit(solution)/shard_map/ppermute | solution.py:275
  44.5 1.8 %collective-permute-done.4.refs_3_ = bf16[256,256]{1,0:T(8,128)(2,1)S(1)} collective-permute-done((bf16[256,256]{1,0:T(8,128)(2,1)S(1)}, bf16[256,256]{1,0:T(8,128)(2,1)S(1)}, u32[]{:S(2)}, u32[]{:S(2)}) %collective-permute-start.4) | collective-permute-done | bytes 131104 | tf_op jit(solution)/shard_map/ppermute | solution.py:279
  46.4 5.4 %collective-permute-done.7.refs_4_ = bf16[256,256]{1,0:T(8,128)(2,1)S(1)} collective-permute-done((bf16[256,256]{1,0:T(8,128)(2,1)S(1)}, bf16[256,256]{1,0:T(8,128)(2,1)S(1)}, u32[]{:S(2)}, u32[]{:S(2)}) %collective-permute-start.7) | collective-permute-done | bytes 131104 | tf_op jit(solution)/shard_map/ppermute | solution.py:279
  52.1 1.8 %collective-permute-done.8.refs_5_ = bf16[4,256,256]{2,1,0:T(8,128)(2,1)S(1)} collective-permute-done((bf16[4,256,256]{2,1,0:T(8,128)(2,1)S(1)}, bf16[4,256,256]{2,1,0:T(8,128)(2,1)S(1)}, u32[]{:S(2)}, u32[]{:S(2)}) %collective-permute-start.8) | collective-permute-done | bytes 524320 | tf_op jit(solution)/shard_map/ppermute | solution.py:282
  53.9 11.8 %attention_grads.1 = (bf16[256,512]{1,0:T(8,128)(2,1)S(1)}, f32[5,256,256]{2,1,0:T(8,128)S(1)}, bf16[4,256,256]{2,1,0:T(8,128)(2,1)S(1)}) custom-call(s32[16]{0:T(128)S(1)} %concatenate.37.info, bf16[128,1024]{1,0:T(8,128)(2,1)S(1)} %collective-permute-done.5.qg0, bf16[128,1024]{1,0:T(8,128)(2,1)S(1)} %collective-permute-done.6.qg1, ...), custom_call_target="tpu_custom_call" | custom-call | flops 3019898880 | bytes 8388608 | tf_op jit(solution)/shard_map/attention_grads/pallas_call | solution.py:132
  66.3 1.8 %collective-permute-done.10.other = bf16[256,512]{1,0:T(8,128)(2,1)S(1)} collective-permute-done((bf16[256,512]{1,0:T(8,128)(2,1)S(1)}, bf16[256,512]{1,0:T(8,128)(2,1)S(1)}, u32[]{:S(2)}, u32[]{:S(2)}) %collective-permute-start.10) | collective-permute-done | bytes 262176 | tf_op jit(solution)/shard_map/ppermute | solution.py:282
  68.1 1.6 %copy-done.1 = bf16[2048,512]{1,0:T(8,128)(2,1)S(1)} copy-done((bf16[2048,512]{1,0:T(8,128)(2,1)S(1)}, bf16[2048,512]{1,0:T(8,128)(2,1)}, u32[]{:S(2)}) %copy-start.1) | copy-done | bytes 2097176
  69.6 2.0 %project_query.1 = (bf16[128,2048]{1,0:T(8,128)(2,1)S(1)}, bf16[128,2048]{1,0:T(8,128)(2,1)S(1)}, bf16[128,2048]{1,0:T(8,128)(2,1)S(1)}, bf16[128,2048]{1,0:T(8,...) custom-call(s32[16]{0:T(128)S(1)} %concatenate.37.info, ...), custom_call_target="tpu_custom_call" | custom-call | flops 1073741824 | bytes 4194304 | tf_op jit(solution)/shard_map/project_query/pallas_call | solution.py:187
  71.8 3.0 %collective-permute-start.14 = (bf16[128,2048]{1,0:T(8,128)(2,1)S(1)}, bf16[128,2048]{1,0:T(8,128)(2,1)S(1)}, u32[]{:S(2)}, u32[]{:S(2)}) collective-permute-start(bf16[128,2048]{1,0:T(8,128)(2,1)S(1)} %get-tuple-element.37), channel_id=1, source_target_pairs={{0,8},{8,16},{16,24},{24,0},{32,40},{40,48},{48,56},{56,32},{64,72... | collective-permute-start | bytes 1572872 | tf_op jit(solution)/shard_map/ppermute | solution.py:341
  74.7 2.7 %collective-permute-start.15 = (bf16[128,2048]{1,0:T(8,128)(2,1)S(1)}, bf16[128,2048]{1,0:T(8,128)(2,1)S(1)}, u32[]{:S(2)}, u32[]{:S(2)}) collective-permute-start(bf16[128,2048]{1,0:T(8,128)(2,1)S(1)} %get-tuple-element.38), channel_id=1, source_target_pairs={{0,24},{8,0},{16,8},{24,16},{32,56},{40,32},{48,40},{56,48},{64,88... | collective-permute-start | bytes 1572872 | tf_op jit(solution)/shard_map/ppermute | solution.py:341
  78.3 3.7 %collective-permute-done.13 = bf16[256,256]{1,0:T(8,128)(2,1)S(1)} collective-permute-done((bf16[256,256]{1,0:T(8,128)(2,1)S(1)}, bf16[256,256]{1,0:T(8,128)(2,1)S(1)}, u32[]{:S(2)}, u32[]{:S(2)}) %collective-permute-start.13) | collective-permute-done | bytes 131104 | tf_op jit(solution)/shard_map/ppermute | solution.py:279
  82.0 7.5 %collective-permute-done.14.refs_1_ = bf16[128,2048]{1,0:T(8,128)(2,1)S(1)} collective-permute-done((bf16[128,2048]{1,0:T(8,128)(2,1)S(1)}, bf16[128,2048]{1,0:T(8,128)(2,1)S(1)}, u32[]{:S(2)}, u32[]{:S(2)}) %collective-permute-start.14) | collective-permute-done | bytes 524320 | tf_op jit(solution)/shard_map/ppermute | solution.py:341
  89.5 2.0 %collective-permute-start.18 = (bf16[128,2048]{1,0:T(8,128)(2,1)S(1)}, bf16[128,2048]{1,0:T(8,128)(2,1)S(1)}, u32[]{:S(2)}, u32[]{:S(2)}) collective-permute-start(bf16[128,2048]{1,0:T(8,128)(2,1)S(1)} %get-tuple-element.40), channel_id=1, source_target_pairs={{0,16},{8,24},{16,0},{24,8},{32,48},{40,56},{48,32},{56,40},{64,80... | collective-permute-start | bytes 1572872 | tf_op jit(solution)/shard_map/ppermute | solution.py:341
  91.5 2.3 %collective-permute-done.16 = bf16[256,256]{1,0:T(8,128)(2,1)S(1)} collective-permute-done((bf16[256,256]{1,0:T(8,128)(2,1)S(1)}, bf16[256,256]{1,0:T(8,128)(2,1)S(1)}, u32[]{:S(2)}, u32[]{:S(2)}) %collective-permute-start.16) | collective-permute-done | bytes 131104 | tf_op jit(solution)/shard_map/ppermute | solution.py:279
  93.8 1.6 %collective-permute-start.17 = (bf16[256,256]{1,0:T(8,128)(2,1)S(1)}, bf16[256,256]{1,0:T(8,128)(2,1)S(1)}, u32[]{:S(2)}, u32[]{:S(2)}) collective-permute-start(bf16[256,256]{1,0:T(8,128)(2,1)S(1)} %fusion.2), channel_id=1, source_target_pairs={{0,224},{8,232},{16,240},{24,248},{32,0},{40,8},{48,16},{56,24},{6... | collective-permute-start | bytes 393224 | tf_op jit(solution)/shard_map/ppermute | solution.py:279
  95.5 2.7 %collective-permute-done.17 = bf16[256,256]{1,0:T(8,128)(2,1)S(1)} collective-permute-done((bf16[256,256]{1,0:T(8,128)(2,1)S(1)}, bf16[256,256]{1,0:T(8,128)(2,1)S(1)}, u32[]{:S(2)}, u32[]{:S(2)}) %collective-permute-start.17) | collective-permute-done | bytes 131104 | tf_op jit(solution)/shard_map/ppermute | solution.py:279
  98.2 5.5 %collective-permute-done.18.refs_2_ = bf16[128,2048]{1,0:T(8,128)(2,1)S(1)} collective-permute-done((bf16[128,2048]{1,0:T(8,128)(2,1)S(1)}, bf16[128,2048]{1,0:T(8,128)(2,1)S(1)}, u32[]{:S(2)}, u32[]{:S(2)}) %collective-permute-start.18) | collective-permute-done | bytes 524320 | tf_op jit(solution)/shard_map/ppermute | solution.py:341
  103.7 4.1 %collective-permute-start.20 = (bf16[128,256]{1,0:T(8,128)(2,1)S(1)}, bf16[128,256]{1,0:T(8,128)(2,1)S(1)}, u32[]{:S(2)}, u32[]{:S(2)}) collective-permute-start(bf16[128,256]{1,0:T(8,128)(2,1)S(1)} %get-tuple-element.65), channel_id=1, source_target_pairs={{0,8},{4,24},{8,0},{12,16},{16,12},{20,28},{24,4},{28,20},{32,40},... | collective-permute-start | bytes 196616 | tf_op jit(solution)/shard_map/ppermute | solution.py:275
  107.7 1.9 %collective-permute-start.19 = (bf16[128,256]{1,0:T(8,128)(2,1)S(1)}, bf16[128,256]{1,0:T(8,128)(2,1)S(1)}, u32[]{:S(2)}, u32[]{:S(2)}) collective-permute-start(bf16[128,256]{1,0:T(8,128)(2,1)S(1)} %get-tuple-element.64), channel_id=1, source_target_pairs={{0,0},{4,16},{8,8},{12,24},{16,4},{20,20},{24,12},{28,28},{32,32},... | collective-permute-start | bytes 196616 | tf_op jit(solution)/shard_map/ppermute | solution.py:275
  110.1 4.8 %collective-permute-done.19 = bf16[128,256]{1,0:T(8,128)(2,1)S(1)} collective-permute-done((bf16[128,256]{1,0:T(8,128)(2,1)S(1)}, bf16[128,256]{1,0:T(8,128)(2,1)S(1)}, u32[]{:S(2)}, u32[]{:S(2)}) %collective-permute-start.19) | collective-permute-done | bytes 65568 | tf_op jit(solution)/shard_map/ppermute | solution.py:275
  116.4 2.2 %copy-done = bf16[2048,1024]{1,0:T(8,128)(2,1)S(1)} copy-done((bf16[2048,1024]{1,0:T(8,128)(2,1)S(1)}, bf16[2048,1024]{1,0:T(8,128)(2,1)}, u32[]{:S(2)}) %copy-start) | copy-done | bytes 4194328
  118.6 1.6 %project_kv.1.mine = bf16[4,128,512]{2,1,0:T(8,128)(2,1)S(1)} custom-call(bf16[128,1024]{1,0:T(8,128)(2,1)S(1)} %pad_maximum_fusion.6.grad, bf16[2048,1024]{1,0:T(8,128)(2,1)S(1)} %copy-done, bf16[128,2048]{1,0:T(8,128)(2,1)S(1)} %get-tuple-element.43.refs_0_, bf16[128,2048]{1,0:T(8,128)(2,1)S(1)} %collective-permute-done.14.refs_1_, ...), custom_call_target="tpu_custom_call" | custom-call | flops 536870912 | bytes 8388608 | tf_op jit(solution)/shard_map/project_kv/pallas_call | solution.py:220
  120.6 1.6 %collective-permute-done.22.theirs = bf16[4,128,512]{2,1,0:T(8,128)(2,1)S(1)} collective-permute-done((bf16[4,128,512]{2,1,0:T(8,128)(2,1)S(1)}, bf16[4,128,512]{2,1,0:T(8,128)(2,1)S(1)}, u32[]{:S(2)}, u32[]{:S(2)}) %collective-permute-start.22) | collective-permute-done | bytes 524320 | tf_op jit(solution)/shard_map/ppermute | solution.py:282
  (66 shorter events, 10.9 us)
Async XLA Ops:
  6.5 1.8 %copy-start.2 = (bf16[1024,256]{1,0:T(8,128)(2,1)S(1)}, bf16[1024,256]{1,0:T(8,128)(2,1)}, u32[]{:S(2)}) copy-start(bf16[1024,256]{1,0:T(8,128)(2,1)} %param.14) | copy-start | bytes 1572868
  6.5 1.8 %copy-start.3 = (bf16[1024,256]{1,0:T(8,128)(2,1)S(1)}, bf16[1024,256]{1,0:T(8,128)(2,1)}, u32[]{:S(2)}) copy-start(bf16[1024,256]{1,0:T(8,128)(2,1)} %param.15) | copy-start | bytes 1572868
  6.5 61.5 %all-gather.3.cloned.1.call-start = ((), (), s32[]{:S(2)}) async-start(), calls=%async_computation | async-start | bytes 2621440 | tf_op jit(solution)/shard_map/all_gather | solution.py:309
  9.1 3.5 %copy-start.6 = (bf16[1,128,256]{2,1,0:T(8,128)(2,1)S(1)}, bf16[1,128,256]{2,1,0:T(8,128)(2,1)}, u32[]{:S(2)}) copy-start(bf16[1,128,256]{2,1,0:T(8,128)(2,1)} %param.9) | copy-start | bytes 196612
  9.1 3.5 %copy-start.7 = (bf16[1,128,256]{2,1,0:T(8,128)(2,1)S(1)}, bf16[1,128,256]{2,1,0:T(8,128)(2,1)}, u32[]{:S(2)}) copy-start(bf16[1,128,256]{2,1,0:T(8,128)(2,1)} %param.10) | copy-start | bytes 196612
  9.3 19.8 %collective-permute-start.11 = (bf16[512,1024]{1,0:T(8,128)(2,1)S(1)}, bf16[512,1024]{1,0:T(8,128)(2,1)}, u32[]{:S(2)}, u32[]{:S(2)}) collective-permute-start(bf16[512,1024]{1,0:T(8,128)(2,1)S(1)} %get-tuple-element.50), channel_id=1, source_target_pairs={{0,4},{4,0},{1,5},{5,1},{2,6},{6,2},{3,7},{7,3},{8,12},{12,8},{9,1... | collective-permute-start | bytes 3145736 | tf_op jit(solution)/shard_map/ppermute | solution.py:282
  12.7 7.1 %collective-permute-start = (bf16[128,256]{1,0:T(8,128)(2,1)S(1)}, bf16[128,256]{1,0:T(8,128)(2,1)S(1)}, u32[]{:S(2)}, u32[]{:S(2)}) collective-permute-start(bf16[128,256]{1,0:T(8,128)(2,1)S(1)} %get-tuple-element.67), channel_id=1, source_target_pairs={{0,0},{4,16},{8,8},{12,24},{16,4},{20,20},{24,12},{28,28},{32,32},... | collective-permute-start | bytes 196616 | tf_op jit(solution)/shard_map/ppermute | solution.py:275
  16.1 5.0 %collective-permute-start.1 = (bf16[128,256]{1,0:T(8,128)(2,1)S(1)}, bf16[128,256]{1,0:T(8,128)(2,1)S(1)}, u32[]{:S(2)}, u32[]{:S(2)}) collective-permute-start(bf16[128,256]{1,0:T(8,128)(2,1)S(1)} %get-tuple-element.66), channel_id=1, source_target_pairs={{0,8},{4,24},{8,0},{12,16},{16,12},{20,28},{24,4},{28,20},{32,40},... | collective-permute-start | bytes 196616 | tf_op jit(solution)/shard_map/ppermute | solution.py:275
  21.1 7.9 %collective-permute-start.2 = (bf16[256,256]{1,0:T(8,128)(2,1)S(1)}, bf16[256,256]{1,0:T(8,128)(2,1)S(1)}, u32[]{:S(2)}, u32[]{:S(2)}) collective-permute-start(bf16[256,256]{1,0:T(8,128)(2,1)S(1)} %constant_dynamic-update-slice_fusion.refs_0_), channel_id=1, source_target_pairs={{0,32},{8,40},{16,48},{24,56},{32,64},{40,72},{48,80},{56,88},{64,... | collective-permute-start | bytes 393224 | tf_op jit(solution)/shard_map/ppermute | solution.py:279
  31.2 85.2 %all-gather.5.cloned.1.call-start = ((), (), s32[]{:S(2)}) async-start(), calls=%async_computation.1 | async-start | bytes 5242880 | tf_op jit(solution)/shard_map/all_gather | solution.py:318
  32.3 19.7 %copy-start.8 = (s32[1,8]{1,0:T(1,128)S(1)}, s32[1,8]{1,0:T(1,128)}, u32[]{:S(2)}) copy-start(s32[1,8]{1,0:T(1,128)} %param.12) | copy-start | bytes 100
  32.5 9.3 %collective-permute-start.5 = (bf16[128,1024]{1,0:T(8,128)(2,1)S(1)}, bf16[128,1024]{1,0:T(8,128)(2,1)S(1)}, u32[]{:S(2)}, u32[]{:S(2)}) collective-permute-start(bf16[128,1024]{1,0:T(8,128)(2,1)S(1)} %get-tuple-element.59), channel_id=1, source_target_pairs={{0,0},{4,16},{8,8},{12,24},{16,4},{20,20},{24,12},{28,28},{32,32},... | collective-permute-start | bytes 786440 | tf_op jit(solution)/shard_map/ppermute | solution.py:275
  35.6 8.9 %collective-permute-start.6 = (bf16[128,1024]{1,0:T(8,128)(2,1)S(1)}, bf16[128,1024]{1,0:T(8,128)(2,1)S(1)}, u32[]{:S(2)}, u32[]{:S(2)}) collective-permute-start(bf16[128,1024]{1,0:T(8,128)(2,1)S(1)} %get-tuple-element.58), channel_id=1, source_target_pairs={{0,8},{4,24},{8,0},{12,16},{16,12},{20,28},{24,4},{28,20},{32,40},... | collective-permute-start | bytes 786440 | tf_op jit(solution)/shard_map/ppermute | solution.py:275
  36.3 5.0 %collective-permute-start.3 = (bf16[256,256]{1,0:T(8,128)(2,1)S(1)}, bf16[256,256]{1,0:T(8,128)(2,1)S(1)}, u32[]{:S(2)}, u32[]{:S(2)}) collective-permute-start(bf16[256,256]{1,0:T(8,128)(2,1)S(1)} %collective-permute-done.2.refs_1_), channel_id=1, source_target_pairs={{0,32},{8,40},{16,48},{24,56},{32,64},{40,72},{48,80},{56,88},{64,... | collective-permute-start | bytes 393224 | tf_op jit(solution)/shard_map/ppermute | solution.py:279
  41.3 5.0 %collective-permute-start.4 = (bf16[256,256]{1,0:T(8,128)(2,1)S(1)}, bf16[256,256]{1,0:T(8,128)(2,1)S(1)}, u32[]{:S(2)}, u32[]{:S(2)}) collective-permute-start(bf16[256,256]{1,0:T(8,128)(2,1)S(1)} %collective-permute-done.3.refs_2_), channel_id=1, source_target_pairs={{0,32},{8,40},{16,48},{24,56},{32,64},{40,72},{48,80},{56,88},{64,... | collective-permute-start | bytes 393224 | tf_op jit(solution)/shard_map/ppermute | solution.py:279
  46.4 5.4 %collective-permute-start.7 = (bf16[256,256]{1,0:T(8,128)(2,1)S(1)}, bf16[256,256]{1,0:T(8,128)(2,1)S(1)}, u32[]{:S(2)}, u32[]{:S(2)}) collective-permute-start(bf16[256,256]{1,0:T(8,128)(2,1)S(1)} %collective-permute-done.4.refs_3_), channel_id=1, source_target_pairs={{0,32},{8,40},{16,48},{24,56},{32,64},{40,72},{48,80},{56,88},{64,... | collective-permute-start | bytes 393224 | tf_op jit(solution)/shard_map/ppermute | solution.py:279
  51.9 2.0 %collective-permute-start.8 = (bf16[4,256,256]{2,1,0:T(8,128)(2,1)S(1)}, bf16[4,256,256]{2,1,0:T(8,128)(2,1)S(1)}, u32[]{:S(2)}, u32[]{:S(2)}) collective-permute-start(bf16[4,256,256]{2,1,0:T(8,128)(2,1)S(1)} %maximum_select_fusion), channel_id=1, source_target_pairs={{0,4},{4,0},{1,5},{5,1},{2,6},{6,2},{3,7},{7,3},{8,12},{12,8},{9,1... | collective-permute-start | bytes 1572872 | tf_op jit(solution)/shard_map/ppermute | solution.py:282
  65.7 2.4 %collective-permute-start.9 = (bf16[4,256,256]{2,1,0:T(8,128)(2,1)S(1)}, bf16[4,256,256]{2,1,0:T(8,128)(2,1)S(1)}, u32[]{:S(2)}, u32[]{:S(2)}) collective-permute-start(bf16[4,256,256]{2,1,0:T(8,128)(2,1)S(1)} %get-tuple-element.32), channel_id=1, source_target_pairs={{0,4},{4,0},{1,5},{5,1},{2,6},{6,2},{3,7},{7,3},{8,12},{12,8},{9,1... | collective-permute-start | bytes 1572872 | tf_op jit(solution)/shard_map/ppermute | solution.py:282
  65.9 2.2 %collective-permute-start.10 = (bf16[256,512]{1,0:T(8,128)(2,1)S(1)}, bf16[256,512]{1,0:T(8,128)(2,1)S(1)}, u32[]{:S(2)}, u32[]{:S(2)}) collective-permute-start(bf16[256,512]{1,0:T(8,128)(2,1)S(1)} %get-tuple-element.33.dq), channel_id=1, source_target_pairs={{0,4},{4,0},{1,5},{5,1},{2,6},{6,2},{3,7},{7,3},{8,12},{12,8},{9,1... | collective-permute-start | bytes 786440 | tf_op jit(solution)/shard_map/ppermute | solution.py:282
  68.1 1.6 %copy-start.1 = (bf16[2048,512]{1,0:T(8,128)(2,1)S(1)}, bf16[2048,512]{1,0:T(8,128)(2,1)}, u32[]{:S(2)}) copy-start(bf16[2048,512]{1,0:T(8,128)(2,1)} %all-gather.3.cloned.1.call-done.refs_0_) | copy-start | bytes 6291460
  71.7 5.8 %collective-permute-start.12 = (bf16[256,256]{1,0:T(8,128)(2,1)S(1)}, bf16[256,256]{1,0:T(8,128)(2,1)S(1)}, u32[]{:S(2)}, u32[]{:S(2)}) collective-permute-start(bf16[256,256]{1,0:T(8,128)(2,1)S(1)} %get-tuple-element.36), channel_id=1, source_target_pairs={{0,224},{8,232},{16,240},{24,248},{32,0},{40,8},{48,16},{56,24},{6... | collective-permute-start | bytes 393224 | tf_op jit(solution)/shard_map/ppermute | solution.py:279
  71.8 17.7 %collective-permute-start.14 = (bf16[128,2048]{1,0:T(8,128)(2,1)S(1)}, bf16[128,2048]{1,0:T(8,128)(2,1)S(1)}, u32[]{:S(2)}, u32[]{:S(2)}) collective-permute-start(bf16[128,2048]{1,0:T(8,128)(2,1)S(1)} %get-tuple-element.37), channel_id=1, source_target_pairs={{0,8},{8,16},{16,24},{24,0},{32,40},{40,48},{48,56},{56,32},{64,72... | collective-permute-start | bytes 1572872 | tf_op jit(solution)/shard_map/ppermute | solution.py:341
  74.7 14.7 %collective-permute-start.15 = (bf16[128,2048]{1,0:T(8,128)(2,1)S(1)}, bf16[128,2048]{1,0:T(8,128)(2,1)S(1)}, u32[]{:S(2)}, u32[]{:S(2)}) collective-permute-start(bf16[128,2048]{1,0:T(8,128)(2,1)S(1)} %get-tuple-element.38), channel_id=1, source_target_pairs={{0,24},{8,0},{16,8},{24,16},{32,56},{40,32},{48,40},{56,48},{64,88... | collective-permute-start | bytes 1572872 | tf_op jit(solution)/shard_map/ppermute | solution.py:341
  77.5 4.5 %collective-permute-start.13 = (bf16[256,256]{1,0:T(8,128)(2,1)S(1)}, bf16[256,256]{1,0:T(8,128)(2,1)S(1)}, u32[]{:S(2)}, u32[]{:S(2)}) collective-permute-start(bf16[256,256]{1,0:T(8,128)(2,1)S(1)} %fusion), channel_id=1, source_target_pairs={{0,224},{8,232},{16,240},{24,248},{32,0},{40,8},{48,16},{56,24},{6... | collective-permute-start | bytes 393224 | tf_op jit(solution)/shard_map/ppermute | solution.py:279
  89.5 4.3 %collective-permute-start.16 = (bf16[256,256]{1,0:T(8,128)(2,1)S(1)}, bf16[256,256]{1,0:T(8,128)(2,1)S(1)}, u32[]{:S(2)}, u32[]{:S(2)}) collective-permute-start(bf16[256,256]{1,0:T(8,128)(2,1)S(1)} %fusion.1), channel_id=1, source_target_pairs={{0,224},{8,232},{16,240},{24,248},{32,0},{40,8},{48,16},{56,24},{6... | collective-permute-start | bytes 393224 | tf_op jit(solution)/shard_map/ppermute | solution.py:279
  89.5 14.2 %collective-permute-start.18 = (bf16[128,2048]{1,0:T(8,128)(2,1)S(1)}, bf16[128,2048]{1,0:T(8,128)(2,1)S(1)}, u32[]{:S(2)}, u32[]{:S(2)}) collective-permute-start(bf16[128,2048]{1,0:T(8,128)(2,1)S(1)} %get-tuple-element.40), channel_id=1, source_target_pairs={{0,16},{8,24},{16,0},{24,8},{32,48},{40,56},{48,32},{56,40},{64,80... | collective-permute-start | bytes 1572872 | tf_op jit(solution)/shard_map/ppermute | solution.py:341
  93.8 4.3 %collective-permute-start.17 = (bf16[256,256]{1,0:T(8,128)(2,1)S(1)}, bf16[256,256]{1,0:T(8,128)(2,1)S(1)}, u32[]{:S(2)}, u32[]{:S(2)}) collective-permute-start(bf16[256,256]{1,0:T(8,128)(2,1)S(1)} %fusion.2), channel_id=1, source_target_pairs={{0,224},{8,232},{16,240},{24,248},{32,0},{40,8},{48,16},{56,24},{6... | collective-permute-start | bytes 393224 | tf_op jit(solution)/shard_map/ppermute | solution.py:279
  103.7 6.4 %collective-permute-start.20 = (bf16[128,256]{1,0:T(8,128)(2,1)S(1)}, bf16[128,256]{1,0:T(8,128)(2,1)S(1)}, u32[]{:S(2)}, u32[]{:S(2)}) collective-permute-start(bf16[128,256]{1,0:T(8,128)(2,1)S(1)} %get-tuple-element.65), channel_id=1, source_target_pairs={{0,8},{4,24},{8,0},{12,16},{16,12},{20,28},{24,4},{28,20},{32,40},... | collective-permute-start | bytes 196616 | tf_op jit(solution)/shard_map/ppermute | solution.py:275
  107.7 7.1 %collective-permute-start.19 = (bf16[128,256]{1,0:T(8,128)(2,1)S(1)}, bf16[128,256]{1,0:T(8,128)(2,1)S(1)}, u32[]{:S(2)}, u32[]{:S(2)}) collective-permute-start(bf16[128,256]{1,0:T(8,128)(2,1)S(1)} %get-tuple-element.64), channel_id=1, source_target_pairs={{0,0},{4,16},{8,8},{12,24},{16,4},{20,20},{24,12},{28,28},{32,32},... | collective-permute-start | bytes 196616 | tf_op jit(solution)/shard_map/ppermute | solution.py:275
  114.9 1.4 %collective-permute-start.21 = (bf16[128,512]{1,0:T(8,128)(2,1)S(1)}, bf16[128,512]{1,0:T(8,128)(2,1)S(1)}, u32[]{:S(2)}, u32[]{:S(2)}) collective-permute-start(bf16[128,512]{1,0:T(8,128)(2,1)S(1)} %pad_maximum_fusion.7), channel_id=1, source_target_pairs={{0,4},{4,0},{1,5},{5,1},{2,6},{6,2},{3,7},{7,3},{8,12},{12,8},{9,1... | collective-permute-start | bytes 393224 | tf_op jit(solution)/shard_map/ppermute | solution.py:282
  116.4 2.2 %copy-start = (bf16[2048,1024]{1,0:T(8,128)(2,1)S(1)}, bf16[2048,1024]{1,0:T(8,128)(2,1)}, u32[]{:S(2)}) copy-start(bf16[2048,1024]{1,0:T(8,128)(2,1)} %all-gather.5.cloned.1.call-done.weights) | copy-start | bytes 12582916
  120.2 2.0 %collective-permute-start.22 = (bf16[4,128,512]{2,1,0:T(8,128)(2,1)S(1)}, bf16[4,128,512]{2,1,0:T(8,128)(2,1)S(1)}, u32[]{:S(2)}, u32[]{:S(2)}) collective-permute-start(bf16[4,128,512]{2,1,0:T(8,128)(2,1)S(1)} %project_kv.1.mine), channel_id=1, source_target_pairs={{0,4},{4,0},{1,5},{5,1},{2,6},{6,2},{3,7},{7,3},{8,12},{12,8},{9,1... | collective-permute-start | bytes 1572872 | tf_op jit(solution)/shard_map/ppermute | solution.py:282
  (2 other events, 2.5 us)
Sparse Core Ops, SparseCore 0:
  31.3 31.9 all-gather.2
  65.1 50.8 all-gather.4

commit v5 on v4

--- a/solution.py
+++ b/solution.py
@@ -307,16 +307,15 @@
     after, _ = lax.optimization_barrier((core, block))
     query_weight = jnp.where(after == (server % 4) // 2, mine[:, half:], theirs[:, half:])
     query_weight = lax.all_gather(query_weight, "dp", axis=0, tiled=True)
+    kv_weight = jnp.concatenate(
+        [mine[:, :half], jnp.where(after >= 0, theirs[:, :half], mine[:, :half])], 1
+    )
+    kv_weight = lax.all_gather(kv_weight, "dp", axis=0, tiled=True)
+
     for k in range(1, BACK + 1):
         if k == BACK:
             blocks[-1], qg0, qg1 = lax.optimization_barrier((blocks[-1], qg0, qg1))
         blocks.append(shift(blocks[-1], "server", 4))
-    after, _ = lax.optimization_barrier((core, blocks[1]))
-    kv_weight = jnp.concatenate(
-        [mine[:, :half], jnp.where(after >= 0, theirs[:, :half], mine[:, :half])], 1
-    )
-    kv_weight = lax.all_gather(kv_weight, "dp", axis=0, tiled=True)
-
     low = jnp.stack(blocks[:BACK])
     high = jnp.stack(blocks[1:])
     other = flip(jnp.where(core == 0, low, high))

time: 130 us -> 126 us (0.969)
  waiting for transfers between devices: 59.4 us -> 56.6 us
    ppermute x6, waiting for transfers between devices: 12.7 us -> 10.2 us  [swap(): return lax.ppermute(x, both, pairs[j])]
  transfers between devices with their start and end apart: 25 -> 25, of which waited for: 19 -> 18; matrix products, arithmetic and copies ran while one was open for 1% -> 1% of each run, Pallas kernels for 11% -> 11%
where the time goes in v5:
time: 126 us
  waiting for transfers between devices  56.6 us (45%)
  starting transfers between devices  30.2 us (24%)
  Pallas kernels  16.5 us (13%)
  between operations  13.7 us (11%)
  other arithmetic  4.82 us (4%)
  local copies, waits for them, and re-layouts  4.22 us (3%)
    ppermute x8, waiting for transfers between devices, shift(): return lax.ppermute(x, axis, [(i, (i + k) % n) for i in range(n)])  26.8 us
    ppermute x6, starting transfers between devices, swap(): return lax.ppermute(x, both, pairs[j])  13.9 us
    ppermute x3, waiting for transfers between devices, body(): products.append(lax.ppermute(sent_products[k], 'server', pairs_x))  12.8 us
    pallas_call x1, Pallas kernels, attention(): pl.pallas_call(attention_kernel, out_shape=(jax.ShapeDtypeStruct((CHUNK,...  11.8 us
    ppermute x6, waiting for transfers between devices, swap(): return lax.ppermute(x, both, pairs[j])  10.2 us
    ppermute x3, starting transfers between devices, body(): products.append(lax.ppermute(sent_products[k], 'server', pairs_x))  8.16 us
    ppermute x6, waiting for transfers between devices, flip(): return lax.ppermute(x, 'section', [(0, 1), (1, 0)])  6.65 us
    ppermute x6, starting transfers between devices, flip(): return lax.ppermute(x, 'section', [(0, 1), (1, 0)])  4.34 us
  transfers between devices with their start and end apart: 25, of which 18 were waited for; matrix products, arithmetic and copies ran while one was open for 1% of the time, Pallas kernels for 11%

profile of v5, /device:TPU:1, one launch (start us, length us, event | category | flops | bytes accessed | tf_op | source)
XLA Modules:
  0.0 126.0 jit_solution(6911602303338342481)
XLA Ops:
  6.5 1.7 %slice_select_fusion = bf16[1024,512]{1,0:T(8,128)(2,1)S(1)} fusion(bf16[1024,1024]{1,0:T(8,128)(2,1)} %param.13, pred[]{:T(512)S(6)} %eq.10), kind=kLoop, calls=%fused_computation.2 | loop fusion | flops 524288 | bytes 3145729 | tf_op jit(solution)/shard_map/jit(_where)/select_n | solution.py:301
  9.3 3.3 %collective-permute-start.11 = (bf16[512,1024]{1,0:T(8,128)(2,1)S(1)}, bf16[512,1024]{1,0:T(8,128)(2,1)S(1)}, u32[]{:S(2)}, u32[]{:S(2)}) collective-permute-start(bf16[512,1024]{1,0:T(8,128)(2,1)S(1)} %get-tuple-element.48), channel_id=1, source_target_pairs={{0,4},{4,0},{1,5},{5,1},{2,6},{6,2},{3,7},{7,3},{8,12},{12,8},{9,1... | collective-permute-start | bytes 3145736 | tf_op jit(solution)/shard_map/ppermute | solution.py:282
  12.7 3.4 %collective-permute-start = (bf16[128,256]{1,0:T(8,128)(2,1)S(1)}, bf16[128,256]{1,0:T(8,128)(2,1)S(1)}, u32[]{:S(2)}, u32[]{:S(2)}) collective-permute-start(bf16[128,256]{1,0:T(8,128)(2,1)S(1)} %get-tuple-element.65), channel_id=1, source_target_pairs={{0,0},{4,16},{8,8},{12,24},{16,4},{20,20},{24,12},{28,28},{32,32},... | collective-permute-start | bytes 196616 | tf_op jit(solution)/shard_map/ppermute | solution.py:275
  16.8 2.9 %collective-permute-done = bf16[128,256]{1,0:T(8,128)(2,1)S(1)} collective-permute-done((bf16[128,256]{1,0:T(8,128)(2,1)S(1)}, bf16[128,256]{1,0:T(8,128)(2,1)S(1)}, u32[]{:S(2)}, u32[]{:S(2)}) %collective-permute-start) | collective-permute-done | bytes 65568 | tf_op jit(solution)/shard_map/ppermute | solution.py:275
  23.2 1.7 %collective-permute-start.2 = (bf16[256,256]{1,0:T(8,128)(2,1)S(1)}, bf16[256,256]{1,0:T(8,128)(2,1)S(1)}, u32[]{:S(2)}, u32[]{:S(2)}) collective-permute-start(bf16[256,256]{1,0:T(8,128)(2,1)S(1)} %constant_dynamic-update-slice_fusion.refs_0_), channel_id=1, source_target_pairs={{0,32},{8,40},{16,48},{24,56},{32,64},{40,72},{48,80},{56,88},{64,... | collective-permute-start | bytes 393224 | tf_op jit(solution)/shard_map/ppermute | solution.py:279
  25.1 2.4 %collective-permute-start.5 = (bf16[128,1024]{1,0:T(8,128)(2,1)S(1)}, bf16[128,1024]{1,0:T(8,128)(2,1)S(1)}, u32[]{:S(2)}, u32[]{:S(2)}) collective-permute-start(bf16[128,1024]{1,0:T(8,128)(2,1)S(1)} %get-tuple-element.57), channel_id=1, source_target_pairs={{0,0},{4,16},{8,8},{12,24},{16,4},{20,20},{24,12},{28,28},{32,32},... | collective-permute-start | bytes 786440 | tf_op jit(solution)/shard_map/ppermute | solution.py:275
  27.5 1.4 %collective-permute-start.6 = (bf16[128,1024]{1,0:T(8,128)(2,1)S(1)}, bf16[128,1024]{1,0:T(8,128)(2,1)S(1)}, u32[]{:S(2)}, u32[]{:S(2)}) collective-permute-start(bf16[128,1024]{1,0:T(8,128)(2,1)S(1)} %get-tuple-element.56), channel_id=1, source_target_pairs={{0,8},{4,24},{8,0},{12,16},{16,12},{20,28},{24,4},{28,20},{32,40},... | collective-permute-start | bytes 786440 | tf_op jit(solution)/shard_map/ppermute | solution.py:275
  28.9 2.4 %collective-permute-done.2.refs_1_ = bf16[256,256]{1,0:T(8,128)(2,1)S(1)} collective-permute-done((bf16[256,256]{1,0:T(8,128)(2,1)S(1)}, bf16[256,256]{1,0:T(8,128)(2,1)S(1)}, u32[]{:S(2)}, u32[]{:S(2)}) %collective-permute-start.2) | collective-permute-done | bytes 131104 | tf_op jit(solution)/shard_map/ppermute | solution.py:279
  31.2 5.0 %collective-permute-done.3.refs_2_ = bf16[256,256]{1,0:T(8,128)(2,1)S(1)} collective-permute-done((bf16[256,256]{1,0:T(8,128)(2,1)S(1)}, bf16[256,256]{1,0:T(8,128)(2,1)S(1)}, u32[]{:S(2)}, u32[]{:S(2)}) %collective-permute-start.3) | collective-permute-done | bytes 131104 | tf_op jit(solution)/shard_map/ppermute | solution.py:279
  37.1 4.6 %collective-permute-done.4.refs_3_ = bf16[256,256]{1,0:T(8,128)(2,1)S(1)} collective-permute-done((bf16[256,256]{1,0:T(8,128)(2,1)S(1)}, bf16[256,256]{1,0:T(8,128)(2,1)S(1)}, u32[]{:S(2)}, u32[]{:S(2)}) %collective-permute-start.4) | collective-permute-done | bytes 131104 | tf_op jit(solution)/shard_map/ppermute | solution.py:279
  41.7 5.5 %collective-permute-done.7.refs_4_ = bf16[256,256]{1,0:T(8,128)(2,1)S(1)} collective-permute-done((bf16[256,256]{1,0:T(8,128)(2,1)S(1)}, bf16[256,256]{1,0:T(8,128)(2,1)S(1)}, u32[]{:S(2)}, u32[]{:S(2)}) %collective-permute-start.7) | collective-permute-done | bytes 131104 | tf_op jit(solution)/shard_map/ppermute | solution.py:279
  47.6 1.8 %collective-permute-done.8.refs_5_ = bf16[4,256,256]{2,1,0:T(8,128)(2,1)S(1)} collective-permute-done((bf16[4,256,256]{2,1,0:T(8,128)(2,1)S(1)}, bf16[4,256,256]{2,1,0:T(8,128)(2,1)S(1)}, u32[]{:S(2)}, u32[]{:S(2)}) %collective-permute-start.8) | collective-permute-done | bytes 524320 | tf_op jit(solution)/shard_map/ppermute | solution.py:282
  49.4 11.8 %attention_grads.1 = (bf16[256,512]{1,0:T(8,128)(2,1)S(1)}, f32[5,256,256]{2,1,0:T(8,128)S(1)}, bf16[4,256,256]{2,1,0:T(8,128)(2,1)S(1)}) custom-call(s32[16]{0:T(128)S(1)} %concatenate.37.info, bf16[128,1024]{1,0:T(8,128)(2,1)S(1)} %collective-permute-done.5.qg0, bf16[128,1024]{1,0:T(8,128)(2,1)S(1)} %collective-permute-done.6.qg1, ...), custom_call_target="tpu_custom_call" | custom-call | flops 3019898880 | bytes 8388608 | tf_op jit(solution)/shard_map/attention_grads/pallas_call | solution.py:132
  61.7 1.8 %collective-permute-done.10.other = bf16[256,512]{1,0:T(8,128)(2,1)S(1)} collective-permute-done((bf16[256,512]{1,0:T(8,128)(2,1)S(1)}, bf16[256,512]{1,0:T(8,128)(2,1)S(1)}, u32[]{:S(2)}, u32[]{:S(2)}) %collective-permute-start.10) | collective-permute-done | bytes 262176 | tf_op jit(solution)/shard_map/ppermute | solution.py:282
  63.5 1.6 %copy-done.1 = bf16[2048,512]{1,0:T(8,128)(2,1)S(1)} copy-done((bf16[2048,512]{1,0:T(8,128)(2,1)S(1)}, bf16[2048,512]{1,0:T(8,128)(2,1)}, u32[]{:S(2)}) %copy-start.1) | copy-done | bytes 2097176
  65.1 2.0 %project_query.1 = (bf16[128,2048]{1,0:T(8,128)(2,1)S(1)}, bf16[128,2048]{1,0:T(8,128)(2,1)S(1)}, bf16[128,2048]{1,0:T(8,128)(2,1)S(1)}, bf16[128,2048]{1,0:T(8,...) custom-call(s32[16]{0:T(128)S(1)} %concatenate.37.info, ...), custom_call_target="tpu_custom_call" | custom-call | flops 1073741824 | bytes 4194304 | tf_op jit(solution)/shard_map/project_query/pallas_call | solution.py:187
  67.2 2.0 %collective-permute-start.14 = (bf16[128,2048]{1,0:T(8,128)(2,1)S(1)}, bf16[128,2048]{1,0:T(8,128)(2,1)S(1)}, u32[]{:S(2)}, u32[]{:S(2)}) collective-permute-start(bf16[128,2048]{1,0:T(8,128)(2,1)S(1)} %get-tuple-element.36), channel_id=1, source_target_pairs={{0,8},{8,16},{16,24},{24,0},{32,40},{40,48},{48,56},{56,32},{64,72... | collective-permute-start | bytes 1572872 | tf_op jit(solution)/shard_map/ppermute | solution.py:340
  69.2 4.2 %collective-permute-start.15 = (bf16[128,2048]{1,0:T(8,128)(2,1)S(1)}, bf16[128,2048]{1,0:T(8,128)(2,1)S(1)}, u32[]{:S(2)}, u32[]{:S(2)}) collective-permute-start(bf16[128,2048]{1,0:T(8,128)(2,1)S(1)} %get-tuple-element.37), channel_id=1, source_target_pairs={{0,24},{8,0},{16,8},{24,16},{32,56},{40,32},{48,40},{56,48},{64,88... | collective-permute-start | bytes 1572872 | tf_op jit(solution)/shard_map/ppermute | solution.py:340
  73.8 4.3 %collective-permute-done.13 = bf16[256,256]{1,0:T(8,128)(2,1)S(1)} collective-permute-done((bf16[256,256]{1,0:T(8,128)(2,1)S(1)}, bf16[256,256]{1,0:T(8,128)(2,1)S(1)}, u32[]{:S(2)}, u32[]{:S(2)}) %collective-permute-start.13) | collective-permute-done | bytes 131104 | tf_op jit(solution)/shard_map/ppermute | solution.py:279
  78.1 7.4 %collective-permute-done.14.refs_1_ = bf16[128,2048]{1,0:T(8,128)(2,1)S(1)} collective-permute-done((bf16[128,2048]{1,0:T(8,128)(2,1)S(1)}, bf16[128,2048]{1,0:T(8,128)(2,1)S(1)}, u32[]{:S(2)}, u32[]{:S(2)}) %collective-permute-start.14) | collective-permute-done | bytes 524320 | tf_op jit(solution)/shard_map/ppermute | solution.py:340
  85.4 2.0 %collective-permute-start.18 = (bf16[128,2048]{1,0:T(8,128)(2,1)S(1)}, bf16[128,2048]{1,0:T(8,128)(2,1)S(1)}, u32[]{:S(2)}, u32[]{:S(2)}) collective-permute-start(bf16[128,2048]{1,0:T(8,128)(2,1)S(1)} %get-tuple-element.39), channel_id=1, source_target_pairs={{0,16},{8,24},{16,0},{24,8},{32,48},{40,56},{48,32},{56,40},{64,80... | collective-permute-start | bytes 1572872 | tf_op jit(solution)/shard_map/ppermute | solution.py:340
  87.4 2.3 %collective-permute-done.16 = bf16[256,256]{1,0:T(8,128)(2,1)S(1)} collective-permute-done((bf16[256,256]{1,0:T(8,128)(2,1)S(1)}, bf16[256,256]{1,0:T(8,128)(2,1)S(1)}, u32[]{:S(2)}, u32[]{:S(2)}) %collective-permute-start.16) | collective-permute-done | bytes 131104 | tf_op jit(solution)/shard_map/ppermute | solution.py:279
  89.8 1.6 %collective-permute-start.17 = (bf16[256,256]{1,0:T(8,128)(2,1)S(1)}, bf16[256,256]{1,0:T(8,128)(2,1)S(1)}, u32[]{:S(2)}, u32[]{:S(2)}) collective-permute-start(bf16[256,256]{1,0:T(8,128)(2,1)S(1)} %fusion.2), channel_id=1, source_target_pairs={{0,224},{8,232},{16,240},{24,248},{32,0},{40,8},{48,16},{56,24},{6... | collective-permute-start | bytes 393224 | tf_op jit(solution)/shard_map/ppermute | solution.py:279
  91.4 2.7 %collective-permute-done.17 = bf16[256,256]{1,0:T(8,128)(2,1)S(1)} collective-permute-done((bf16[256,256]{1,0:T(8,128)(2,1)S(1)}, bf16[256,256]{1,0:T(8,128)(2,1)S(1)}, u32[]{:S(2)}, u32[]{:S(2)}) %collective-permute-start.17) | collective-permute-done | bytes 131104 | tf_op jit(solution)/shard_map/ppermute | solution.py:279
  94.1 5.5 %collective-permute-done.18.refs_2_ = bf16[128,2048]{1,0:T(8,128)(2,1)S(1)} collective-permute-done((bf16[128,2048]{1,0:T(8,128)(2,1)S(1)}, bf16[128,2048]{1,0:T(8,128)(2,1)S(1)}, u32[]{:S(2)}, u32[]{:S(2)}) %collective-permute-start.18) | collective-permute-done | bytes 524320 | tf_op jit(solution)/shard_map/ppermute | solution.py:340
  99.6 4.1 %collective-permute-start.20 = (bf16[128,256]{1,0:T(8,128)(2,1)S(1)}, bf16[128,256]{1,0:T(8,128)(2,1)S(1)}, u32[]{:S(2)}, u32[]{:S(2)}) collective-permute-start(bf16[128,256]{1,0:T(8,128)(2,1)S(1)} %get-tuple-element.63), channel_id=1, source_target_pairs={{0,8},{4,24},{8,0},{12,16},{16,12},{20,28},{24,4},{28,20},{32,40},... | collective-permute-start | bytes 196616 | tf_op jit(solution)/shard_map/ppermute | solution.py:275
  103.7 1.9 %collective-permute-start.19 = (bf16[128,256]{1,0:T(8,128)(2,1)S(1)}, bf16[128,256]{1,0:T(8,128)(2,1)S(1)}, u32[]{:S(2)}, u32[]{:S(2)}) collective-permute-start(bf16[128,256]{1,0:T(8,128)(2,1)S(1)} %get-tuple-element.62), channel_id=1, source_target_pairs={{0,0},{4,16},{8,8},{12,24},{16,4},{20,20},{24,12},{28,28},{32,32},... | collective-permute-start | bytes 196616 | tf_op jit(solution)/shard_map/ppermute | solution.py:275
  106.0 4.7 %collective-permute-done.19 = bf16[128,256]{1,0:T(8,128)(2,1)S(1)} collective-permute-done((bf16[128,256]{1,0:T(8,128)(2,1)S(1)}, bf16[128,256]{1,0:T(8,128)(2,1)S(1)}, u32[]{:S(2)}, u32[]{:S(2)}) %collective-permute-start.19) | collective-permute-done | bytes 65568 | tf_op jit(solution)/shard_map/ppermute | solution.py:275
  110.9 1.3 %collective-permute-done.21 = bf16[128,512]{1,0:T(8,128)(2,1)S(1)} collective-permute-done((bf16[128,512]{1,0:T(8,128)(2,1)S(1)}, bf16[128,512]{1,0:T(8,128)(2,1)S(1)}, u32[]{:S(2)}, u32[]{:S(2)}) %collective-permute-start.21) | collective-permute-done | bytes 131104 | tf_op jit(solution)/shard_map/ppermute | solution.py:282
  112.3 2.2 %copy-done = bf16[2048,1024]{1,0:T(8,128)(2,1)S(1)} copy-done((bf16[2048,1024]{1,0:T(8,128)(2,1)S(1)}, bf16[2048,1024]{1,0:T(8,128)(2,1)}, u32[]{:S(2)}) %copy-start) | copy-done | bytes 4194328
  114.5 1.6 %project_kv.1.mine = bf16[4,128,512]{2,1,0:T(8,128)(2,1)S(1)} custom-call(bf16[128,1024]{1,0:T(8,128)(2,1)S(1)} %pad_maximum_fusion.6.grad, bf16[2048,1024]{1,0:T(8,128)(2,1)S(1)} %copy-done, bf16[128,2048]{1,0:T(8,128)(2,1)S(1)} %get-tuple-element.41.refs_0_, bf16[128,2048]{1,0:T(8,128)(2,1)S(1)} %collective-permute-done.14.refs_1_, ...), custom_call_target="tpu_custom_call" | custom-call | flops 536870912 | bytes 8388608 | tf_op jit(solution)/shard_map/project_kv/pallas_call | solution.py:220
  116.4 1.8 %collective-permute-done.22.theirs = bf16[4,128,512]{2,1,0:T(8,128)(2,1)S(1)} collective-permute-done((bf16[4,128,512]{2,1,0:T(8,128)(2,1)S(1)}, bf16[4,128,512]{2,1,0:T(8,128)(2,1)S(1)}, u32[]{:S(2)}, u32[]{:S(2)}) %collective-permute-start.22) | collective-permute-done | bytes 524320 | tf_op jit(solution)/shard_map/ppermute | solution.py:282
  (66 shorter events, 9.4 us)
Async XLA Ops:
  6.5 1.8 %copy-start.3 = (bf16[1024,256]{1,0:T(8,128)(2,1)S(1)}, bf16[1024,256]{1,0:T(8,128)(2,1)}, u32[]{:S(2)}) copy-start(bf16[1024,256]{1,0:T(8,128)(2,1)} %param.15) | copy-start | bytes 1572868
  6.5 57.0 %all-gather.3.cloned.1.call-start = ((), (), s32[]{:S(2)}) async-start(), calls=%async_computation | async-start | bytes 2621440 | tf_op jit(solution)/shard_map/all_gather | solution.py:309
  9.1 3.5 %copy-start.6 = (bf16[1,128,256]{2,1,0:T(8,128)(2,1)S(1)}, bf16[1,128,256]{2,1,0:T(8,128)(2,1)}, u32[]{:S(2)}) copy-start(bf16[1,128,256]{2,1,0:T(8,128)(2,1)} %param.9) | copy-start | bytes 196612
  9.1 3.5 %copy-start.7 = (bf16[1,128,256]{2,1,0:T(8,128)(2,1)S(1)}, bf16[1,128,256]{2,1,0:T(8,128)(2,1)}, u32[]{:S(2)}) copy-start(bf16[1,128,256]{2,1,0:T(8,128)(2,1)} %param.10) | copy-start | bytes 196612
  9.3 11.8 %collective-permute-start.11 = (bf16[512,1024]{1,0:T(8,128)(2,1)S(1)}, bf16[512,1024]{1,0:T(8,128)(2,1)S(1)}, u32[]{:S(2)}, u32[]{:S(2)}) collective-permute-start(bf16[512,1024]{1,0:T(8,128)(2,1)S(1)} %get-tuple-element.48), channel_id=1, source_target_pairs={{0,4},{4,0},{1,5},{5,1},{2,6},{6,2},{3,7},{7,3},{8,12},{12,8},{9,1... | collective-permute-start | bytes 3145736 | tf_op jit(solution)/shard_map/ppermute | solution.py:282
  12.7 7.1 %collective-permute-start = (bf16[128,256]{1,0:T(8,128)(2,1)S(1)}, bf16[128,256]{1,0:T(8,128)(2,1)S(1)}, u32[]{:S(2)}, u32[]{:S(2)}) collective-permute-start(bf16[128,256]{1,0:T(8,128)(2,1)S(1)} %get-tuple-element.65), channel_id=1, source_target_pairs={{0,0},{4,16},{8,8},{12,24},{16,4},{20,20},{24,12},{28,28},{32,32},... | collective-permute-start | bytes 196616 | tf_op jit(solution)/shard_map/ppermute | solution.py:275
  16.1 5.0 %collective-permute-start.1 = (bf16[128,256]{1,0:T(8,128)(2,1)S(1)}, bf16[128,256]{1,0:T(8,128)(2,1)S(1)}, u32[]{:S(2)}, u32[]{:S(2)}) collective-permute-start(bf16[128,256]{1,0:T(8,128)(2,1)S(1)} %get-tuple-element.64), channel_id=1, source_target_pairs={{0,8},{4,24},{8,0},{12,16},{16,12},{20,28},{24,4},{28,20},{32,40},... | collective-permute-start | bytes 196616 | tf_op jit(solution)/shard_map/ppermute | solution.py:275
  22.0 2.9 %copy-start.4 = (bf16[1,128,1024]{2,1,0:T(8,128)(2,1)S(1)}, bf16[1,128,1024]{2,1,0:T(8,128)(2,1)}, u32[]{:S(2)}) copy-start(bf16[1,128,1024]{2,1,0:T(8,128)(2,1)} %param.11) | copy-start | bytes 786436
  22.0 3.0 %copy-start.5 = (bf16[1,128,1024]{2,1,0:T(8,128)(2,1)S(1)}, bf16[1,128,1024]{2,1,0:T(8,128)(2,1)}, u32[]{:S(2)}) copy-start(bf16[1,128,1024]{2,1,0:T(8,128)(2,1)} %param.8) | copy-start | bytes 786436
  22.0 90.2 %all-gather.5.cloned.1.call-start = ((), (), s32[]{:S(2)}) async-start(), calls=%async_computation.1 | async-start | bytes 5242880 | tf_op jit(solution)/shard_map/all_gather | solution.py:313
  23.2 24.3 %copy-start.8 = (s32[1,8]{1,0:T(1,128)S(1)}, s32[1,8]{1,0:T(1,128)}, u32[]{:S(2)}) copy-start(s32[1,8]{1,0:T(1,128)} %param.12) | copy-start | bytes 100
  23.2 8.0 %collective-permute-start.2 = (bf16[256,256]{1,0:T(8,128)(2,1)S(1)}, bf16[256,256]{1,0:T(8,128)(2,1)S(1)}, u32[]{:S(2)}, u32[]{:S(2)}) collective-permute-start(bf16[256,256]{1,0:T(8,128)(2,1)S(1)} %constant_dynamic-update-slice_fusion.refs_0_), channel_id=1, source_target_pairs={{0,32},{8,40},{16,48},{24,56},{32,64},{40,72},{48,80},{56,88},{64,... | collective-permute-start | bytes 393224 | tf_op jit(solution)/shard_map/ppermute | solution.py:279
  25.1 11.2 %collective-permute-start.5 = (bf16[128,1024]{1,0:T(8,128)(2,1)S(1)}, bf16[128,1024]{1,0:T(8,128)(2,1)S(1)}, u32[]{:S(2)}, u32[]{:S(2)}) collective-permute-start(bf16[128,1024]{1,0:T(8,128)(2,1)S(1)} %get-tuple-element.57), channel_id=1, source_target_pairs={{0,0},{4,16},{8,8},{12,24},{16,4},{20,20},{24,12},{28,28},{32,32},... | collective-permute-start | bytes 786440 | tf_op jit(solution)/shard_map/ppermute | solution.py:275
  27.5 9.6 %collective-permute-start.6 = (bf16[128,1024]{1,0:T(8,128)(2,1)S(1)}, bf16[128,1024]{1,0:T(8,128)(2,1)S(1)}, u32[]{:S(2)}, u32[]{:S(2)}) collective-permute-start(bf16[128,1024]{1,0:T(8,128)(2,1)S(1)} %get-tuple-element.56), channel_id=1, source_target_pairs={{0,8},{4,24},{8,0},{12,16},{16,12},{20,28},{24,4},{28,20},{32,40},... | collective-permute-start | bytes 786440 | tf_op jit(solution)/shard_map/ppermute | solution.py:275
  31.2 5.0 %collective-permute-start.3 = (bf16[256,256]{1,0:T(8,128)(2,1)S(1)}, bf16[256,256]{1,0:T(8,128)(2,1)S(1)}, u32[]{:S(2)}, u32[]{:S(2)}) collective-permute-start(bf16[256,256]{1,0:T(8,128)(2,1)S(1)} %collective-permute-done.2.refs_1_), channel_id=1, source_target_pairs={{0,32},{8,40},{16,48},{24,56},{32,64},{40,72},{48,80},{56,88},{64,... | collective-permute-start | bytes 393224 | tf_op jit(solution)/shard_map/ppermute | solution.py:279
  36.3 5.4 %collective-permute-start.4 = (bf16[256,256]{1,0:T(8,128)(2,1)S(1)}, bf16[256,256]{1,0:T(8,128)(2,1)S(1)}, u32[]{:S(2)}, u32[]{:S(2)}) collective-permute-start(bf16[256,256]{1,0:T(8,128)(2,1)S(1)} %collective-permute-done.3.refs_2_), channel_id=1, source_target_pairs={{0,32},{8,40},{16,48},{24,56},{32,64},{40,72},{48,80},{56,88},{64,... | collective-permute-start | bytes 393224 | tf_op jit(solution)/shard_map/ppermute | solution.py:279
  41.7 5.6 %collective-permute-start.7 = (bf16[256,256]{1,0:T(8,128)(2,1)S(1)}, bf16[256,256]{1,0:T(8,128)(2,1)S(1)}, u32[]{:S(2)}, u32[]{:S(2)}) collective-permute-start(bf16[256,256]{1,0:T(8,128)(2,1)S(1)} %collective-permute-done.4.refs_3_), channel_id=1, source_target_pairs={{0,32},{8,40},{16,48},{24,56},{32,64},{40,72},{48,80},{56,88},{64,... | collective-permute-start | bytes 393224 | tf_op jit(solution)/shard_map/ppermute | solution.py:279
  47.4 2.0 %collective-permute-start.8 = (bf16[4,256,256]{2,1,0:T(8,128)(2,1)S(1)}, bf16[4,256,256]{2,1,0:T(8,128)(2,1)S(1)}, u32[]{:S(2)}, u32[]{:S(2)}) collective-permute-start(bf16[4,256,256]{2,1,0:T(8,128)(2,1)S(1)} %maximum_select_fusion), channel_id=1, source_target_pairs={{0,4},{4,0},{1,5},{5,1},{2,6},{6,2},{3,7},{7,3},{8,12},{12,8},{9,1... | collective-permute-start | bytes 1572872 | tf_op jit(solution)/shard_map/ppermute | solution.py:282
  61.1 2.4 %collective-permute-start.9 = (bf16[4,256,256]{2,1,0:T(8,128)(2,1)S(1)}, bf16[4,256,256]{2,1,0:T(8,128)(2,1)S(1)}, u32[]{:S(2)}, u32[]{:S(2)}) collective-permute-start(bf16[4,256,256]{2,1,0:T(8,128)(2,1)S(1)} %get-tuple-element.31), channel_id=1, source_target_pairs={{0,4},{4,0},{1,5},{5,1},{2,6},{6,2},{3,7},{7,3},{8,12},{12,8},{9,1... | collective-permute-start | bytes 1572872 | tf_op jit(solution)/shard_map/ppermute | solution.py:282
  61.3 2.2 %collective-permute-start.10 = (bf16[256,512]{1,0:T(8,128)(2,1)S(1)}, bf16[256,512]{1,0:T(8,128)(2,1)S(1)}, u32[]{:S(2)}, u32[]{:S(2)}) collective-permute-start(bf16[256,512]{1,0:T(8,128)(2,1)S(1)} %get-tuple-element.32.dq), channel_id=1, source_target_pairs={{0,4},{4,0},{1,5},{5,1},{2,6},{6,2},{3,7},{7,3},{8,12},{12,8},{9,1... | collective-permute-start | bytes 786440 | tf_op jit(solution)/shard_map/ppermute | solution.py:282
  67.2 6.3 %collective-permute-start.12 = (bf16[256,256]{1,0:T(8,128)(2,1)S(1)}, bf16[256,256]{1,0:T(8,128)(2,1)S(1)}, u32[]{:S(2)}, u32[]{:S(2)}) collective-permute-start(bf16[256,256]{1,0:T(8,128)(2,1)S(1)} %get-tuple-element.35), channel_id=1, source_target_pairs={{0,224},{8,232},{16,240},{24,248},{32,0},{40,8},{48,16},{56,24},{6... | collective-permute-start | bytes 393224 | tf_op jit(solution)/shard_map/ppermute | solution.py:279
  67.2 18.2 %collective-permute-start.14 = (bf16[128,2048]{1,0:T(8,128)(2,1)S(1)}, bf16[128,2048]{1,0:T(8,128)(2,1)S(1)}, u32[]{:S(2)}, u32[]{:S(2)}) collective-permute-start(bf16[128,2048]{1,0:T(8,128)(2,1)S(1)} %get-tuple-element.36), channel_id=1, source_target_pairs={{0,8},{8,16},{16,24},{24,0},{32,40},{40,48},{48,56},{56,32},{64,72... | collective-permute-start | bytes 1572872 | tf_op jit(solution)/shard_map/ppermute | solution.py:340
  69.2 16.2 %collective-permute-start.15 = (bf16[128,2048]{1,0:T(8,128)(2,1)S(1)}, bf16[128,2048]{1,0:T(8,128)(2,1)S(1)}, u32[]{:S(2)}, u32[]{:S(2)}) collective-permute-start(bf16[128,2048]{1,0:T(8,128)(2,1)S(1)} %get-tuple-element.37), channel_id=1, source_target_pairs={{0,24},{8,0},{16,8},{24,16},{32,56},{40,32},{48,40},{56,48},{64,88... | collective-permute-start | bytes 1572872 | tf_op jit(solution)/shard_map/ppermute | solution.py:340
  73.4 4.6 %collective-permute-start.13 = (bf16[256,256]{1,0:T(8,128)(2,1)S(1)}, bf16[256,256]{1,0:T(8,128)(2,1)S(1)}, u32[]{:S(2)}, u32[]{:S(2)}) collective-permute-start(bf16[256,256]{1,0:T(8,128)(2,1)S(1)} %fusion), channel_id=1, source_target_pairs={{0,224},{8,232},{16,240},{24,248},{32,0},{40,8},{48,16},{56,24},{6... | collective-permute-start | bytes 393224 | tf_op jit(solution)/shard_map/ppermute | solution.py:279
  85.4 4.3 %collective-permute-start.16 = (bf16[256,256]{1,0:T(8,128)(2,1)S(1)}, bf16[256,256]{1,0:T(8,128)(2,1)S(1)}, u32[]{:S(2)}, u32[]{:S(2)}) collective-permute-start(bf16[256,256]{1,0:T(8,128)(2,1)S(1)} %fusion.1), channel_id=1, source_target_pairs={{0,224},{8,232},{16,240},{24,248},{32,0},{40,8},{48,16},{56,24},{6... | collective-permute-start | bytes 393224 | tf_op jit(solution)/shard_map/ppermute | solution.py:279
  85.4 14.2 %collective-permute-start.18 = (bf16[128,2048]{1,0:T(8,128)(2,1)S(1)}, bf16[128,2048]{1,0:T(8,128)(2,1)S(1)}, u32[]{:S(2)}, u32[]{:S(2)}) collective-permute-start(bf16[128,2048]{1,0:T(8,128)(2,1)S(1)} %get-tuple-element.39), channel_id=1, source_target_pairs={{0,16},{8,24},{16,0},{24,8},{32,48},{40,56},{48,32},{56,40},{64,80... | collective-permute-start | bytes 1572872 | tf_op jit(solution)/shard_map/ppermute | solution.py:340
  89.8 4.3 %collective-permute-start.17 = (bf16[256,256]{1,0:T(8,128)(2,1)S(1)}, bf16[256,256]{1,0:T(8,128)(2,1)S(1)}, u32[]{:S(2)}, u32[]{:S(2)}) collective-permute-start(bf16[256,256]{1,0:T(8,128)(2,1)S(1)} %fusion.2), channel_id=1, source_target_pairs={{0,224},{8,232},{16,240},{24,248},{32,0},{40,8},{48,16},{56,24},{6... | collective-permute-start | bytes 393224 | tf_op jit(solution)/shard_map/ppermute | solution.py:279
  99.6 6.4 %collective-permute-start.20 = (bf16[128,256]{1,0:T(8,128)(2,1)S(1)}, bf16[128,256]{1,0:T(8,128)(2,1)S(1)}, u32[]{:S(2)}, u32[]{:S(2)}) collective-permute-start(bf16[128,256]{1,0:T(8,128)(2,1)S(1)} %get-tuple-element.63), channel_id=1, source_target_pairs={{0,8},{4,24},{8,0},{12,16},{16,12},{20,28},{24,4},{28,20},{32,40},... | collective-permute-start | bytes 196616 | tf_op jit(solution)/shard_map/ppermute | solution.py:275
  103.7 7.1 %collective-permute-start.19 = (bf16[128,256]{1,0:T(8,128)(2,1)S(1)}, bf16[128,256]{1,0:T(8,128)(2,1)S(1)}, u32[]{:S(2)}, u32[]{:S(2)}) collective-permute-start(bf16[128,256]{1,0:T(8,128)(2,1)S(1)} %get-tuple-element.62), channel_id=1, source_target_pairs={{0,0},{4,16},{8,8},{12,24},{16,4},{20,20},{24,12},{28,28},{32,32},... | collective-permute-start | bytes 196616 | tf_op jit(solution)/shard_map/ppermute | solution.py:275
  110.8 1.4 %collective-permute-start.21 = (bf16[128,512]{1,0:T(8,128)(2,1)S(1)}, bf16[128,512]{1,0:T(8,128)(2,1)S(1)}, u32[]{:S(2)}, u32[]{:S(2)}) collective-permute-start(bf16[128,512]{1,0:T(8,128)(2,1)S(1)} %pad_maximum_fusion.7), channel_id=1, source_target_pairs={{0,4},{4,0},{1,5},{5,1},{2,6},{6,2},{3,7},{7,3},{8,12},{12,8},{9,1... | collective-permute-start | bytes 393224 | tf_op jit(solution)/shard_map/ppermute | solution.py:282
  112.3 2.2 %copy-start = (bf16[2048,1024]{1,0:T(8,128)(2,1)S(1)}, bf16[2048,1024]{1,0:T(8,128)(2,1)}, u32[]{:S(2)}) copy-start(bf16[2048,1024]{1,0:T(8,128)(2,1)} %all-gather.5.cloned.1.call-done.weights) | copy-start | bytes 12582916
  116.1 2.0 %collective-permute-start.22 = (bf16[4,128,512]{2,1,0:T(8,128)(2,1)S(1)}, bf16[4,128,512]{2,1,0:T(8,128)(2,1)S(1)}, u32[]{:S(2)}, u32[]{:S(2)}) collective-permute-start(bf16[4,128,512]{2,1,0:T(8,128)(2,1)S(1)} %project_kv.1.mine), channel_id=1, source_target_pairs={{0,4},{4,0},{1,5},{5,1},{2,6},{6,2},{3,7},{7,3},{8,12},{12,8},{9,1... | collective-permute-start | bytes 1572872 | tf_op jit(solution)/shard_map/ppermute | solution.py:282
  (2 other events, 3.3 us)
Sparse Core Ops, SparseCore 0:
  22.1 33.7 all-gather.2
  57.7 50.8 all-gather.4

commit v6 on v5

--- a/solution.py
+++ b/solution.py
@@ -205,26 +205,26 @@
 
 def project_kernel(grad, weights, *refs):
     *terms, out = refs
-    n, _, width = out.shape
-    for k in range(n):
-        at = slice(k * width, (k + 1) * width)
-        total = nt(grad[...], weights[at])
-        for term in terms:
-            total = total + term[:, at].astype(F32)
-        out[k] = total.astype(BF)
+    total = nt(grad[...], weights[...])
+    for term in terms:
+        total = total + term[...].astype(F32)
+    out[0] = total.astype(BF)
 
 
 def project(grad, weights, terms, n):
-    vmem = pl.BlockSpec(memory_space=pltpu.VMEM)
     width, dims = weights.shape
+    width = width // n
     return pl.pallas_call(
         project_kernel,
-        out_shape=jax.ShapeDtypeStruct((n, ROWS, width // n), BF),
-        in_specs=[vmem] * (2 + len(terms)),
-        out_specs=vmem,
-        compiler_params=pltpu.CompilerParams(vmem_limit_bytes=24 * 1024 * 1024),
+        grid=(n,),
+        out_shape=jax.ShapeDtypeStruct((n, ROWS, width), BF),
+        in_specs=[pl.BlockSpec((ROWS, dims), lambda k: (0, 0))]
+        + [pl.BlockSpec((width, dims), lambda k: (k, 0))]
+        + [pl.BlockSpec((ROWS, width), lambda k: (0, k))] * len(terms),
+        out_specs=pl.BlockSpec((1, ROWS, width), lambda k: (k, 0, 0)),
+        compiler_params=pltpu.CompilerParams(vmem_limit_bytes=58 * 1024 * 1024),
         cost_estimate=pl.CostEstimate(
-            flops=2 * ROWS * width * dims, bytes_accessed=8 << 20, transcendentals=0
+            flops=2 * n * ROWS * width * dims, bytes_accessed=8 << 20, transcendentals=0
         ),
         name="project_kv",
     )(grad, weights, *terms)

time: 126 us -> 130 us (1.032)
  Pallas kernels: 16.5 us -> 20.2 us
    pallas_call x1, Pallas kernels: 1.64 us -> 5.42 us  [project(): pl.pallas_call(project_kernel, grid=(n,), out_shape=jax.ShapeDtypeStruct(...]
    unnamed x19 -> x27, local copies, waits for them, and re-layouts: 3.88 us -> 2.75 us
  transfers between devices with their start and end apart: 25 -> 25, of which waited for: 18 -> 18; matrix products, arithmetic and copies ran while one was open for 1% -> 2% of each run, Pallas kernels for 11% -> 11%
where the time goes in v6:
time: 130 us; the launch traced here: 129 us
  waiting for transfers between devices  56.9 us (44%)
  starting transfers between devices  29.9 us (23%)
  Pallas kernels  20.2 us (16%)
  between operations  13.7 us (11%)
  other arithmetic  5.56 us (4%)
  local copies, waits for them, and re-layouts  3.1 us (2%)
    ppermute x8, waiting for transfers between devices, shift(): return lax.ppermute(x, axis, [(i, (i + k) % n) for i in range(n)])  26.8 us
    ppermute x6, starting transfers between devices, swap(): return lax.ppermute(x, both, pairs[j])  13.7 us
    ppermute x3, waiting for transfers between devices, body(): products.append(lax.ppermute(sent_products[k], 'server', pairs_x))  12.9 us
    pallas_call x1, Pallas kernels, attention(): pl.pallas_call(attention_kernel, out_shape=(jax.ShapeDtypeStruct((CHUNK,...  11.8 us
    ppermute x6, waiting for transfers between devices, swap(): return lax.ppermute(x, both, pairs[j])  10.3 us
    ppermute x3, starting transfers between devices, body(): products.append(lax.ppermute(sent_products[k], 'server', pairs_x))  8.07 us
    ppermute x6, waiting for transfers between devices, flip(): return lax.ppermute(x, 'section', [(0, 1), (1, 0)])  6.86 us
    pallas_call x1, Pallas kernels, project(): pl.pallas_call(project_kernel, grid=(n,), out_shape=jax.ShapeDtypeStruct(...  5.42 us
  transfers between devices with their start and end apart: 25, of which 18 were waited for; matrix products, arithmetic and copies ran while one was open for 2% of the time, Pallas kernels for 11%

profile of v6, /device:TPU:1, one launch (start us, length us, event | category | flops | bytes accessed | tf_op | source)
XLA Modules:
  0.0 129.4 jit_solution(14185217940440362522)
XLA Ops:
  6.5 1.7 %slice_select_fusion = bf16[1024,512]{1,0:T(8,128)(2,1)S(1)} fusion(bf16[1024,1024]{1,0:T(8,128)(2,1)} %param.13, pred[]{:T(512)S(6)} %eq.10), kind=kLoop, calls=%fused_computation.2 | loop fusion | flops 524288 | bytes 3145729 | tf_op jit(solution)/shard_map/jit(_where)/select_n | solution.py:301
  9.3 3.3 %collective-permute-start.11 = (bf16[512,1024]{1,0:T(8,128)(2,1)S(1)}, bf16[512,1024]{1,0:T(8,128)(2,1)S(1)}, u32[]{:S(2)}, u32[]{:S(2)}) collective-permute-start(bf16[512,1024]{1,0:T(8,128)(2,1)S(1)} %get-tuple-element.48), channel_id=1, source_target_pairs={{0,4},{4,0},{1,5},{5,1},{2,6},{6,2},{3,7},{7,3},{8,12},{12,8},{9,1... | collective-permute-start | bytes 3145736 | tf_op jit(solution)/shard_map/ppermute | solution.py:282
  12.7 3.4 %collective-permute-start = (bf16[128,256]{1,0:T(8,128)(2,1)S(1)}, bf16[128,256]{1,0:T(8,128)(2,1)S(1)}, u32[]{:S(2)}, u32[]{:S(2)}) collective-permute-start(bf16[128,256]{1,0:T(8,128)(2,1)S(1)} %get-tuple-element.65), channel_id=1, source_target_pairs={{0,0},{4,16},{8,8},{12,24},{16,4},{20,20},{24,12},{28,28},{32,32},... | collective-permute-start | bytes 196616 | tf_op jit(solution)/shard_map/ppermute | solution.py:275
  16.8 2.9 %collective-permute-done = bf16[128,256]{1,0:T(8,128)(2,1)S(1)} collective-permute-done((bf16[128,256]{1,0:T(8,128)(2,1)S(1)}, bf16[128,256]{1,0:T(8,128)(2,1)S(1)}, u32[]{:S(2)}, u32[]{:S(2)}) %collective-permute-start) | collective-permute-done | bytes 65568 | tf_op jit(solution)/shard_map/ppermute | solution.py:275
  19.8 1.3 %collective-permute-done.1 = bf16[128,256]{1,0:T(8,128)(2,1)S(1)} collective-permute-done((bf16[128,256]{1,0:T(8,128)(2,1)S(1)}, bf16[128,256]{1,0:T(8,128)(2,1)S(1)}, u32[]{:S(2)}, u32[]{:S(2)}) %collective-permute-start.1) | collective-permute-done | bytes 65568 | tf_op jit(solution)/shard_map/ppermute | solution.py:275
  23.2 1.7 %collective-permute-start.2 = (bf16[256,256]{1,0:T(8,128)(2,1)S(1)}, bf16[256,256]{1,0:T(8,128)(2,1)S(1)}, u32[]{:S(2)}, u32[]{:S(2)}) collective-permute-start(bf16[256,256]{1,0:T(8,128)(2,1)S(1)} %constant_dynamic-update-slice_fusion.refs_0_), channel_id=1, source_target_pairs={{0,32},{8,40},{16,48},{24,56},{32,64},{40,72},{48,80},{56,88},{64,... | collective-permute-start | bytes 393224 | tf_op jit(solution)/shard_map/ppermute | solution.py:279
  25.1 2.4 %collective-permute-start.5 = (bf16[128,1024]{1,0:T(8,128)(2,1)S(1)}, bf16[128,1024]{1,0:T(8,128)(2,1)S(1)}, u32[]{:S(2)}, u32[]{:S(2)}) collective-permute-start(bf16[128,1024]{1,0:T(8,128)(2,1)S(1)} %get-tuple-element.57), channel_id=1, source_target_pairs={{0,0},{4,16},{8,8},{12,24},{16,4},{20,20},{24,12},{28,28},{32,32},... | collective-permute-start | bytes 786440 | tf_op jit(solution)/shard_map/ppermute | solution.py:275
  27.5 1.4 %collective-permute-start.6 = (bf16[128,1024]{1,0:T(8,128)(2,1)S(1)}, bf16[128,1024]{1,0:T(8,128)(2,1)S(1)}, u32[]{:S(2)}, u32[]{:S(2)}) collective-permute-start(bf16[128,1024]{1,0:T(8,128)(2,1)S(1)} %get-tuple-element.56), channel_id=1, source_target_pairs={{0,8},{4,24},{8,0},{12,16},{16,12},{20,28},{24,4},{28,20},{32,40},... | collective-permute-start | bytes 786440 | tf_op jit(solution)/shard_map/ppermute | solution.py:275
  28.9 2.3 %collective-permute-done.2.refs_1_ = bf16[256,256]{1,0:T(8,128)(2,1)S(1)} collective-permute-done((bf16[256,256]{1,0:T(8,128)(2,1)S(1)}, bf16[256,256]{1,0:T(8,128)(2,1)S(1)}, u32[]{:S(2)}, u32[]{:S(2)}) %collective-permute-start.2) | collective-permute-done | bytes 131104 | tf_op jit(solution)/shard_map/ppermute | solution.py:279
  31.3 5.0 %collective-permute-done.3.refs_2_ = bf16[256,256]{1,0:T(8,128)(2,1)S(1)} collective-permute-done((bf16[256,256]{1,0:T(8,128)(2,1)S(1)}, bf16[256,256]{1,0:T(8,128)(2,1)S(1)}, u32[]{:S(2)}, u32[]{:S(2)}) %collective-permute-start.3) | collective-permute-done | bytes 131104 | tf_op jit(solution)/shard_map/ppermute | solution.py:279
  37.1 4.6 %collective-permute-done.4.refs_3_ = bf16[256,256]{1,0:T(8,128)(2,1)S(1)} collective-permute-done((bf16[256,256]{1,0:T(8,128)(2,1)S(1)}, bf16[256,256]{1,0:T(8,128)(2,1)S(1)}, u32[]{:S(2)}, u32[]{:S(2)}) %collective-permute-start.4) | collective-permute-done | bytes 131104 | tf_op jit(solution)/shard_map/ppermute | solution.py:279
  41.7 5.5 %collective-permute-done.7.refs_4_ = bf16[256,256]{1,0:T(8,128)(2,1)S(1)} collective-permute-done((bf16[256,256]{1,0:T(8,128)(2,1)S(1)}, bf16[256,256]{1,0:T(8,128)(2,1)S(1)}, u32[]{:S(2)}, u32[]{:S(2)}) %collective-permute-start.7) | collective-permute-done | bytes 131104 | tf_op jit(solution)/shard_map/ppermute | solution.py:279
  47.6 1.8 %collective-permute-done.8.refs_5_ = bf16[4,256,256]{2,1,0:T(8,128)(2,1)S(1)} collective-permute-done((bf16[4,256,256]{2,1,0:T(8,128)(2,1)S(1)}, bf16[4,256,256]{2,1,0:T(8,128)(2,1)S(1)}, u32[]{:S(2)}, u32[]{:S(2)}) %collective-permute-start.8) | collective-permute-done | bytes 524320 | tf_op jit(solution)/shard_map/ppermute | solution.py:282
  49.4 11.8 %attention_grads.1 = (bf16[256,512]{1,0:T(8,128)(2,1)S(1)}, f32[5,256,256]{2,1,0:T(8,128)S(1)}, bf16[4,256,256]{2,1,0:T(8,128)(2,1)S(1)}) custom-call(s32[16]{0:T(128)S(1)} %concatenate.37.info, bf16[128,1024]{1,0:T(8,128)(2,1)S(1)} %collective-permute-done.5.qg0, bf16[128,1024]{1,0:T(8,128)(2,1)S(1)} %collective-permute-done.6.qg1, ...), custom_call_target="tpu_custom_call" | custom-call | flops 3019898880 | bytes 8388608 | tf_op jit(solution)/shard_map/attention_grads/pallas_call | solution.py:132
  61.8 1.8 %collective-permute-done.10.other = bf16[256,512]{1,0:T(8,128)(2,1)S(1)} collective-permute-done((bf16[256,512]{1,0:T(8,128)(2,1)S(1)}, bf16[256,512]{1,0:T(8,128)(2,1)S(1)}, u32[]{:S(2)}, u32[]{:S(2)}) %collective-permute-start.10) | collective-permute-done | bytes 262176 | tf_op jit(solution)/shard_map/ppermute | solution.py:282
  63.5 1.6 %copy-done.1 = bf16[2048,512]{1,0:T(8,128)(2,1)S(1)} copy-done((bf16[2048,512]{1,0:T(8,128)(2,1)S(1)}, bf16[2048,512]{1,0:T(8,128)(2,1)}, u32[]{:S(2)}) %copy-start.1) | copy-done | bytes 2097176
  65.1 2.0 %project_query.1 = (bf16[128,2048]{1,0:T(8,128)(2,1)S(1)}, bf16[128,2048]{1,0:T(8,128)(2,1)S(1)}, bf16[128,2048]{1,0:T(8,128)(2,1)S(1)}, bf16[128,2048]{1,0:T(8,...) custom-call(s32[16]{0:T(128)S(1)} %concatenate.37.info, ...), custom_call_target="tpu_custom_call" | custom-call | flops 1073741824 | bytes 4194304 | tf_op jit(solution)/shard_map/project_query/pallas_call | solution.py:187
  67.2 2.0 %collective-permute-start.14 = (bf16[128,2048]{1,0:T(8,128)(2,1)S(1)}, bf16[128,2048]{1,0:T(8,128)(2,1)S(1)}, u32[]{:S(2)}, u32[]{:S(2)}) collective-permute-start(bf16[128,2048]{1,0:T(8,128)(2,1)S(1)} %get-tuple-element.36), channel_id=1, source_target_pairs={{0,8},{8,16},{16,24},{24,0},{32,40},{40,48},{48,56},{56,32},{64,72... | collective-permute-start | bytes 1572872 | tf_op jit(solution)/shard_map/ppermute | solution.py:340
  69.2 4.2 %collective-permute-start.15 = (bf16[128,2048]{1,0:T(8,128)(2,1)S(1)}, bf16[128,2048]{1,0:T(8,128)(2,1)S(1)}, u32[]{:S(2)}, u32[]{:S(2)}) collective-permute-start(bf16[128,2048]{1,0:T(8,128)(2,1)S(1)} %get-tuple-element.37), channel_id=1, source_target_pairs={{0,24},{8,0},{16,8},{24,16},{32,56},{40,32},{48,40},{56,48},{64,88... | collective-permute-start | bytes 1572872 | tf_op jit(solution)/shard_map/ppermute | solution.py:340
  73.7 4.2 %collective-permute-done.13 = bf16[256,256]{1,0:T(8,128)(2,1)S(1)} collective-permute-done((bf16[256,256]{1,0:T(8,128)(2,1)S(1)}, bf16[256,256]{1,0:T(8,128)(2,1)S(1)}, u32[]{:S(2)}, u32[]{:S(2)}) %collective-permute-start.13) | collective-permute-done | bytes 131104 | tf_op jit(solution)/shard_map/ppermute | solution.py:279
  78.0 7.4 %collective-permute-done.14.refs_1_ = bf16[128,2048]{1,0:T(8,128)(2,1)S(1)} collective-permute-done((bf16[128,2048]{1,0:T(8,128)(2,1)S(1)}, bf16[128,2048]{1,0:T(8,128)(2,1)S(1)}, u32[]{:S(2)}, u32[]{:S(2)}) %collective-permute-start.14) | collective-permute-done | bytes 524320 | tf_op jit(solution)/shard_map/ppermute | solution.py:340
  85.5 1.9 %collective-permute-start.18 = (bf16[128,2048]{1,0:T(8,128)(2,1)S(1)}, bf16[128,2048]{1,0:T(8,128)(2,1)S(1)}, u32[]{:S(2)}, u32[]{:S(2)}) collective-permute-start(bf16[128,2048]{1,0:T(8,128)(2,1)S(1)} %get-tuple-element.39), channel_id=1, source_target_pairs={{0,16},{8,24},{16,0},{24,8},{32,48},{40,56},{48,32},{56,40},{64,80... | collective-permute-start | bytes 1572872 | tf_op jit(solution)/shard_map/ppermute | solution.py:340
  87.4 2.4 %collective-permute-done.16 = bf16[256,256]{1,0:T(8,128)(2,1)S(1)} collective-permute-done((bf16[256,256]{1,0:T(8,128)(2,1)S(1)}, bf16[256,256]{1,0:T(8,128)(2,1)S(1)}, u32[]{:S(2)}, u32[]{:S(2)}) %collective-permute-start.16) | collective-permute-done | bytes 131104 | tf_op jit(solution)/shard_map/ppermute | solution.py:279
  89.9 1.6 %collective-permute-start.17 = (bf16[256,256]{1,0:T(8,128)(2,1)S(1)}, bf16[256,256]{1,0:T(8,128)(2,1)S(1)}, u32[]{:S(2)}, u32[]{:S(2)}) collective-permute-start(bf16[256,256]{1,0:T(8,128)(2,1)S(1)} %fusion.2), channel_id=1, source_target_pairs={{0,224},{8,232},{16,240},{24,248},{32,0},{40,8},{48,16},{56,24},{6... | collective-permute-start | bytes 393224 | tf_op jit(solution)/shard_map/ppermute | solution.py:279
  91.5 2.7 %collective-permute-done.17 = bf16[256,256]{1,0:T(8,128)(2,1)S(1)} collective-permute-done((bf16[256,256]{1,0:T(8,128)(2,1)S(1)}, bf16[256,256]{1,0:T(8,128)(2,1)S(1)}, u32[]{:S(2)}, u32[]{:S(2)}) %collective-permute-start.17) | collective-permute-done | bytes 131104 | tf_op jit(solution)/shard_map/ppermute | solution.py:279
  94.2 5.6 %collective-permute-done.18.refs_2_ = bf16[128,2048]{1,0:T(8,128)(2,1)S(1)} collective-permute-done((bf16[128,2048]{1,0:T(8,128)(2,1)S(1)}, bf16[128,2048]{1,0:T(8,128)(2,1)S(1)}, u32[]{:S(2)}, u32[]{:S(2)}) %collective-permute-start.18) | collective-permute-done | bytes 524320 | tf_op jit(solution)/shard_map/ppermute | solution.py:340
  99.8 3.9 %collective-permute-start.20 = (bf16[128,256]{1,0:T(8,128)(2,1)S(1)}, bf16[128,256]{1,0:T(8,128)(2,1)S(1)}, u32[]{:S(2)}, u32[]{:S(2)}) collective-permute-start(bf16[128,256]{1,0:T(8,128)(2,1)S(1)} %get-tuple-element.63), channel_id=1, source_target_pairs={{0,8},{4,24},{8,0},{12,16},{16,12},{20,28},{24,4},{28,20},{32,40},... | collective-permute-start | bytes 196616 | tf_op jit(solution)/shard_map/ppermute | solution.py:275
  103.7 1.9 %collective-permute-start.19 = (bf16[128,256]{1,0:T(8,128)(2,1)S(1)}, bf16[128,256]{1,0:T(8,128)(2,1)S(1)}, u32[]{:S(2)}, u32[]{:S(2)}) collective-permute-start(bf16[128,256]{1,0:T(8,128)(2,1)S(1)} %get-tuple-element.62), channel_id=1, source_target_pairs={{0,0},{4,16},{8,8},{12,24},{16,4},{20,20},{24,12},{28,28},{32,32},... | collective-permute-start | bytes 196616 | tf_op jit(solution)/shard_map/ppermute | solution.py:275
  106.0 4.7 %collective-permute-done.19 = bf16[128,256]{1,0:T(8,128)(2,1)S(1)} collective-permute-done((bf16[128,256]{1,0:T(8,128)(2,1)S(1)}, bf16[128,256]{1,0:T(8,128)(2,1)S(1)}, u32[]{:S(2)}, u32[]{:S(2)}) %collective-permute-start.19) | collective-permute-done | bytes 65568 | tf_op jit(solution)/shard_map/ppermute | solution.py:275
  110.9 1.3 %collective-permute-done.21 = bf16[128,512]{1,0:T(8,128)(2,1)S(1)} collective-permute-done((bf16[128,512]{1,0:T(8,128)(2,1)S(1)}, bf16[128,512]{1,0:T(8,128)(2,1)S(1)}, u32[]{:S(2)}, u32[]{:S(2)}) %collective-permute-start.21) | collective-permute-done | bytes 131104 | tf_op jit(solution)/shard_map/ppermute | solution.py:282
  113.0 5.4 %project_kv.1.mine = bf16[4,128,512]{2,1,0:T(8,128)(2,1)} custom-call(bf16[128,1024]{1,0:T(8,128)(2,1)} %pad_maximum_fusion.6.grad, bf16[2048,1024]{1,0:T(8,128)(2,1)} %all-gather.5.cloned.1.call-done.weights, bf16[128,2048]{1,0:T(8,128)(2,1)} %copy-done.2, bf16[128,2048]{1,0:T(8,128)(2,1)} %copy-done.3, bf16[128,2048]{1,0:T(8,128)(2,1)} %copy-done.5, ...), custom_call_target="tpu_custom_call" | custom-call | flops 536870912 | bytes 8388608 | tf_op jit(solution)/shard_map/project_kv/pallas_call | solution.py:217
  118.5 2.0 %collective-permute-done.22.theirs = bf16[4,128,512]{2,1,0:T(8,128)(2,1)S(1)} collective-permute-done((bf16[4,128,512]{2,1,0:T(8,128)(2,1)}, bf16[4,128,512]{2,1,0:T(8,128)(2,1)S(1)}, u32[]{:S(2)}, u32[]{:S(2)}) %collective-permute-start.22) | collective-permute-done | bytes 524320 | tf_op jit(solution)/shard_map/ppermute | solution.py:282
  (74 shorter events, 9.9 us)
Async XLA Ops:
  6.5 57.0 %all-gather.3.cloned.1.call-start = ((), (), s32[]{:S(2)}) async-start(), calls=%async_computation | async-start | bytes 2621440 | tf_op jit(solution)/shard_map/all_gather | solution.py:309
  9.1 3.5 %copy-start.10 = (bf16[1,128,256]{2,1,0:T(8,128)(2,1)S(1)}, bf16[1,128,256]{2,1,0:T(8,128)(2,1)}, u32[]{:S(2)}) copy-start(bf16[1,128,256]{2,1,0:T(8,128)(2,1)} %param.9) | copy-start | bytes 196612
  9.1 3.5 %copy-start.11 = (bf16[1,128,256]{2,1,0:T(8,128)(2,1)S(1)}, bf16[1,128,256]{2,1,0:T(8,128)(2,1)}, u32[]{:S(2)}) copy-start(bf16[1,128,256]{2,1,0:T(8,128)(2,1)} %param.10) | copy-start | bytes 196612
  9.3 11.8 %collective-permute-start.11 = (bf16[512,1024]{1,0:T(8,128)(2,1)S(1)}, bf16[512,1024]{1,0:T(8,128)(2,1)S(1)}, u32[]{:S(2)}, u32[]{:S(2)}) collective-permute-start(bf16[512,1024]{1,0:T(8,128)(2,1)S(1)} %get-tuple-element.48), channel_id=1, source_target_pairs={{0,4},{4,0},{1,5},{5,1},{2,6},{6,2},{3,7},{7,3},{8,12},{12,8},{9,1... | collective-permute-start | bytes 3145736 | tf_op jit(solution)/shard_map/ppermute | solution.py:282
  12.7 7.1 %collective-permute-start = (bf16[128,256]{1,0:T(8,128)(2,1)S(1)}, bf16[128,256]{1,0:T(8,128)(2,1)S(1)}, u32[]{:S(2)}, u32[]{:S(2)}) collective-permute-start(bf16[128,256]{1,0:T(8,128)(2,1)S(1)} %get-tuple-element.65), channel_id=1, source_target_pairs={{0,0},{4,16},{8,8},{12,24},{16,4},{20,20},{24,12},{28,28},{32,32},... | collective-permute-start | bytes 196616 | tf_op jit(solution)/shard_map/ppermute | solution.py:275
  16.1 5.0 %collective-permute-start.1 = (bf16[128,256]{1,0:T(8,128)(2,1)S(1)}, bf16[128,256]{1,0:T(8,128)(2,1)S(1)}, u32[]{:S(2)}, u32[]{:S(2)}) collective-permute-start(bf16[128,256]{1,0:T(8,128)(2,1)S(1)} %get-tuple-element.64), channel_id=1, source_target_pairs={{0,8},{4,24},{8,0},{12,16},{16,12},{20,28},{24,4},{28,20},{32,40},... | collective-permute-start | bytes 196616 | tf_op jit(solution)/shard_map/ppermute | solution.py:275
  22.0 90.9 %all-gather.5.cloned.1.call-start = ((), (), s32[]{:S(2)}) async-start(), calls=%async_computation.1 | async-start | bytes 5242880 | tf_op jit(solution)/shard_map/all_gather | solution.py:313
  23.2 24.3 %copy-start.12 = (s32[1,8]{1,0:T(1,128)S(1)}, s32[1,8]{1,0:T(1,128)}, u32[]{:S(2)}) copy-start(s32[1,8]{1,0:T(1,128)} %param.12) | copy-start | bytes 100
  23.2 8.0 %collective-permute-start.2 = (bf16[256,256]{1,0:T(8,128)(2,1)S(1)}, bf16[256,256]{1,0:T(8,128)(2,1)S(1)}, u32[]{:S(2)}, u32[]{:S(2)}) collective-permute-start(bf16[256,256]{1,0:T(8,128)(2,1)S(1)} %constant_dynamic-update-slice_fusion.refs_0_), channel_id=1, source_target_pairs={{0,32},{8,40},{16,48},{24,56},{32,64},{40,72},{48,80},{56,88},{64,... | collective-permute-start | bytes 393224 | tf_op jit(solution)/shard_map/ppermute | solution.py:279
  25.1 11.2 %collective-permute-start.5 = (bf16[128,1024]{1,0:T(8,128)(2,1)S(1)}, bf16[128,1024]{1,0:T(8,128)(2,1)S(1)}, u32[]{:S(2)}, u32[]{:S(2)}) collective-permute-start(bf16[128,1024]{1,0:T(8,128)(2,1)S(1)} %get-tuple-element.57), channel_id=1, source_target_pairs={{0,0},{4,16},{8,8},{12,24},{16,4},{20,20},{24,12},{28,28},{32,32},... | collective-permute-start | bytes 786440 | tf_op jit(solution)/shard_map/ppermute | solution.py:275
  27.5 9.6 %collective-permute-start.6 = (bf16[128,1024]{1,0:T(8,128)(2,1)S(1)}, bf16[128,1024]{1,0:T(8,128)(2,1)S(1)}, u32[]{:S(2)}, u32[]{:S(2)}) collective-permute-start(bf16[128,1024]{1,0:T(8,128)(2,1)S(1)} %get-tuple-element.56), channel_id=1, source_target_pairs={{0,8},{4,24},{8,0},{12,16},{16,12},{20,28},{24,4},{28,20},{32,40},... | collective-permute-start | bytes 786440 | tf_op jit(solution)/shard_map/ppermute | solution.py:275
  31.3 5.0 %collective-permute-start.3 = (bf16[256,256]{1,0:T(8,128)(2,1)S(1)}, bf16[256,256]{1,0:T(8,128)(2,1)S(1)}, u32[]{:S(2)}, u32[]{:S(2)}) collective-permute-start(bf16[256,256]{1,0:T(8,128)(2,1)S(1)} %collective-permute-done.2.refs_1_), channel_id=1, source_target_pairs={{0,32},{8,40},{16,48},{24,56},{32,64},{40,72},{48,80},{56,88},{64,... | collective-permute-start | bytes 393224 | tf_op jit(solution)/shard_map/ppermute | solution.py:279
  36.3 5.4 %collective-permute-start.4 = (bf16[256,256]{1,0:T(8,128)(2,1)S(1)}, bf16[256,256]{1,0:T(8,128)(2,1)S(1)}, u32[]{:S(2)}, u32[]{:S(2)}) collective-permute-start(bf16[256,256]{1,0:T(8,128)(2,1)S(1)} %collective-permute-done.3.refs_2_), channel_id=1, source_target_pairs={{0,32},{8,40},{16,48},{24,56},{32,64},{40,72},{48,80},{56,88},{64,... | collective-permute-start | bytes 393224 | tf_op jit(solution)/shard_map/ppermute | solution.py:279
  41.7 5.6 %collective-permute-start.7 = (bf16[256,256]{1,0:T(8,128)(2,1)S(1)}, bf16[256,256]{1,0:T(8,128)(2,1)S(1)}, u32[]{:S(2)}, u32[]{:S(2)}) collective-permute-start(bf16[256,256]{1,0:T(8,128)(2,1)S(1)} %collective-permute-done.4.refs_3_), channel_id=1, source_target_pairs={{0,32},{8,40},{16,48},{24,56},{32,64},{40,72},{48,80},{56,88},{64,... | collective-permute-start | bytes 393224 | tf_op jit(solution)/shard_map/ppermute | solution.py:279
  47.4 2.0 %collective-permute-start.8 = (bf16[4,256,256]{2,1,0:T(8,128)(2,1)S(1)}, bf16[4,256,256]{2,1,0:T(8,128)(2,1)S(1)}, u32[]{:S(2)}, u32[]{:S(2)}) collective-permute-start(bf16[4,256,256]{2,1,0:T(8,128)(2,1)S(1)} %maximum_select_fusion), channel_id=1, source_target_pairs={{0,4},{4,0},{1,5},{5,1},{2,6},{6,2},{3,7},{7,3},{8,12},{12,8},{9,1... | collective-permute-start | bytes 1572872 | tf_op jit(solution)/shard_map/ppermute | solution.py:282
  61.2 2.4 %collective-permute-start.9 = (bf16[4,256,256]{2,1,0:T(8,128)(2,1)S(1)}, bf16[4,256,256]{2,1,0:T(8,128)(2,1)S(1)}, u32[]{:S(2)}, u32[]{:S(2)}) collective-permute-start(bf16[4,256,256]{2,1,0:T(8,128)(2,1)S(1)} %get-tuple-element.31), channel_id=1, source_target_pairs={{0,4},{4,0},{1,5},{5,1},{2,6},{6,2},{3,7},{7,3},{8,12},{12,8},{9,1... | collective-permute-start | bytes 1572872 | tf_op jit(solution)/shard_map/ppermute | solution.py:282
  61.4 2.2 %collective-permute-start.10 = (bf16[256,512]{1,0:T(8,128)(2,1)S(1)}, bf16[256,512]{1,0:T(8,128)(2,1)S(1)}, u32[]{:S(2)}, u32[]{:S(2)}) collective-permute-start(bf16[256,512]{1,0:T(8,128)(2,1)S(1)} %get-tuple-element.32.dq), channel_id=1, source_target_pairs={{0,4},{4,0},{1,5},{5,1},{2,6},{6,2},{3,7},{7,3},{8,12},{12,8},{9,1... | collective-permute-start | bytes 786440 | tf_op jit(solution)/shard_map/ppermute | solution.py:282
  67.1 27.1 %copy-start.2 = (bf16[128,2048]{1,0:T(8,128)(2,1)}, bf16[128,2048]{1,0:T(8,128)(2,1)S(1)}, u32[]{:S(2)}) copy-start(bf16[128,2048]{1,0:T(8,128)(2,1)S(1)} %get-tuple-element.41.refs_0_) | copy-start | bytes 1572868
  67.1 6.3 %collective-permute-start.12 = (bf16[256,256]{1,0:T(8,128)(2,1)S(1)}, bf16[256,256]{1,0:T(8,128)(2,1)S(1)}, u32[]{:S(2)}, u32[]{:S(2)}) collective-permute-start(bf16[256,256]{1,0:T(8,128)(2,1)S(1)} %get-tuple-element.35), channel_id=1, source_target_pairs={{0,224},{8,232},{16,240},{24,248},{32,0},{40,8},{48,16},{56,24},{6... | collective-permute-start | bytes 393224 | tf_op jit(solution)/shard_map/ppermute | solution.py:279
  67.2 18.2 %collective-permute-start.14 = (bf16[128,2048]{1,0:T(8,128)(2,1)S(1)}, bf16[128,2048]{1,0:T(8,128)(2,1)S(1)}, u32[]{:S(2)}, u32[]{:S(2)}) collective-permute-start(bf16[128,2048]{1,0:T(8,128)(2,1)S(1)} %get-tuple-element.36), channel_id=1, source_target_pairs={{0,8},{8,16},{16,24},{24,0},{32,40},{40,48},{48,56},{56,32},{64,72... | collective-permute-start | bytes 1572872 | tf_op jit(solution)/shard_map/ppermute | solution.py:340
  69.2 16.2 %collective-permute-start.15 = (bf16[128,2048]{1,0:T(8,128)(2,1)S(1)}, bf16[128,2048]{1,0:T(8,128)(2,1)S(1)}, u32[]{:S(2)}, u32[]{:S(2)}) collective-permute-start(bf16[128,2048]{1,0:T(8,128)(2,1)S(1)} %get-tuple-element.37), channel_id=1, source_target_pairs={{0,24},{8,0},{16,8},{24,16},{32,56},{40,32},{48,40},{56,48},{64,88... | collective-permute-start | bytes 1572872 | tf_op jit(solution)/shard_map/ppermute | solution.py:340
  73.4 4.6 %collective-permute-start.13 = (bf16[256,256]{1,0:T(8,128)(2,1)S(1)}, bf16[256,256]{1,0:T(8,128)(2,1)S(1)}, u32[]{:S(2)}, u32[]{:S(2)}) collective-permute-start(bf16[256,256]{1,0:T(8,128)(2,1)S(1)} %fusion), channel_id=1, source_target_pairs={{0,224},{8,232},{16,240},{24,248},{32,0},{40,8},{48,16},{56,24},{6... | collective-permute-start | bytes 393224 | tf_op jit(solution)/shard_map/ppermute | solution.py:279
  85.4 27.5 %copy-start.3 = (bf16[128,2048]{1,0:T(8,128)(2,1)}, bf16[128,2048]{1,0:T(8,128)(2,1)S(1)}, u32[]{:S(2)}) copy-start(bf16[128,2048]{1,0:T(8,128)(2,1)S(1)} %collective-permute-done.14.refs_1_) | copy-start | bytes 1572868
  85.4 27.5 %copy-start.4 = (bf16[128,2048]{1,0:T(8,128)(2,1)}, bf16[128,2048]{1,0:T(8,128)(2,1)S(1)}, u32[]{:S(2)}) copy-start(bf16[128,2048]{1,0:T(8,128)(2,1)S(1)} %collective-permute-done.15.refs_3_) | copy-start | bytes 1572868
  85.4 4.4 %collective-permute-start.16 = (bf16[256,256]{1,0:T(8,128)(2,1)S(1)}, bf16[256,256]{1,0:T(8,128)(2,1)S(1)}, u32[]{:S(2)}, u32[]{:S(2)}) collective-permute-start(bf16[256,256]{1,0:T(8,128)(2,1)S(1)} %fusion.1), channel_id=1, source_target_pairs={{0,224},{8,232},{16,240},{24,248},{32,0},{40,8},{48,16},{56,24},{6... | collective-permute-start | bytes 393224 | tf_op jit(solution)/shard_map/ppermute | solution.py:279
  85.5 14.3 %collective-permute-start.18 = (bf16[128,2048]{1,0:T(8,128)(2,1)S(1)}, bf16[128,2048]{1,0:T(8,128)(2,1)S(1)}, u32[]{:S(2)}, u32[]{:S(2)}) collective-permute-start(bf16[128,2048]{1,0:T(8,128)(2,1)S(1)} %get-tuple-element.39), channel_id=1, source_target_pairs={{0,16},{8,24},{16,0},{24,8},{32,48},{40,56},{48,32},{56,40},{64,80... | collective-permute-start | bytes 1572872 | tf_op jit(solution)/shard_map/ppermute | solution.py:340
  89.9 4.3 %collective-permute-start.17 = (bf16[256,256]{1,0:T(8,128)(2,1)S(1)}, bf16[256,256]{1,0:T(8,128)(2,1)S(1)}, u32[]{:S(2)}, u32[]{:S(2)}) collective-permute-start(bf16[256,256]{1,0:T(8,128)(2,1)S(1)} %fusion.2), channel_id=1, source_target_pairs={{0,224},{8,232},{16,240},{24,248},{32,0},{40,8},{48,16},{56,24},{6... | collective-permute-start | bytes 393224 | tf_op jit(solution)/shard_map/ppermute | solution.py:279
  99.8 13.2 %copy-start.5 = (bf16[128,2048]{1,0:T(8,128)(2,1)}, bf16[128,2048]{1,0:T(8,128)(2,1)S(1)}, u32[]{:S(2)}) copy-start(bf16[128,2048]{1,0:T(8,128)(2,1)S(1)} %collective-permute-done.18.refs_2_) | copy-start | bytes 1572868
  99.8 6.3 %collective-permute-start.20 = (bf16[128,256]{1,0:T(8,128)(2,1)S(1)}, bf16[128,256]{1,0:T(8,128)(2,1)S(1)}, u32[]{:S(2)}, u32[]{:S(2)}) collective-permute-start(bf16[128,256]{1,0:T(8,128)(2,1)S(1)} %get-tuple-element.63), channel_id=1, source_target_pairs={{0,8},{4,24},{8,0},{12,16},{16,12},{20,28},{24,4},{28,20},{32,40},... | collective-permute-start | bytes 196616 | tf_op jit(solution)/shard_map/ppermute | solution.py:275
  103.7 7.1 %collective-permute-start.19 = (bf16[128,256]{1,0:T(8,128)(2,1)S(1)}, bf16[128,256]{1,0:T(8,128)(2,1)S(1)}, u32[]{:S(2)}, u32[]{:S(2)}) collective-permute-start(bf16[128,256]{1,0:T(8,128)(2,1)S(1)} %get-tuple-element.62), channel_id=1, source_target_pairs={{0,0},{4,16},{8,8},{12,24},{16,4},{20,20},{24,12},{28,28},{32,32},... | collective-permute-start | bytes 196616 | tf_op jit(solution)/shard_map/ppermute | solution.py:275
  110.8 1.4 %collective-permute-start.21 = (bf16[128,512]{1,0:T(8,128)(2,1)S(1)}, bf16[128,512]{1,0:T(8,128)(2,1)S(1)}, u32[]{:S(2)}, u32[]{:S(2)}) collective-permute-start(bf16[128,512]{1,0:T(8,128)(2,1)S(1)} %pad_maximum_fusion.7), channel_id=1, source_target_pairs={{0,4},{4,0},{1,5},{5,1},{2,6},{6,2},{3,7},{7,3},{8,12},{12,8},{9,1... | collective-permute-start | bytes 393224 | tf_op jit(solution)/shard_map/ppermute | solution.py:282
  118.4 2.1 %collective-permute-start.22 = (bf16[4,128,512]{2,1,0:T(8,128)(2,1)}, bf16[4,128,512]{2,1,0:T(8,128)(2,1)S(1)}, u32[]{:S(2)}, u32[]{:S(2)}) collective-permute-start(bf16[4,128,512]{2,1,0:T(8,128)(2,1)} %project_kv.1.mine), channel_id=1, source_target_pairs={{0,4},{4,0},{1,5},{5,1},{2,6},{6,2},{3,7},{7,3},{8,12},{12,8},{9,1... | collective-permute-start | bytes 1572872 | tf_op jit(solution)/shard_map/ppermute | solution.py:282
  (6 other events, 12.1 us)
Sparse Core Ops, SparseCore 0:
  22.2 33.7 all-gather.2
  57.7 50.8 all-gather.4
